TPU v7x, 512 devices: a whole 4x4x16 slice. The times are simulated.
512 devices in a mesh: seq: 64 (over z, y), head: 8 (over x, core).
Axes of the slice: x: 4, y: 4, z: 16, core: 2. Of those that a mesh axis runs over, the one named last changes fastest.
Arguments:
- hidden_in: bfloat16 [4, 16384], P(None, 'seq'), may hold values from -12 to 12
- norm_gain: float32 [16384], P('seq'), may hold values from 0.25 to 1.75
- qkv_codes: int32 [16384, 4608], P('seq', 'head'), may hold values from 0 to 255
- qkv_scale: float32 [18432], P('head'), may hold values from 0.00390625 to 0.015625
- out_codes: int32 [16384, 4096], P('seq', 'head'), may hold values from 0 to 255
- out_scale: float32 [16384], P('seq'), may hold values from 0.0078125 to 0.03125
- cache_keys: bfloat16 [4, 65536, 8, 128], P(None, 'seq', 'head'), may hold values from -200 to 200
- cache_values: bfloat16 [4, 65536, 8, 128], P(None, 'seq', 'head'), may hold values from -6 to 6
- lengths: int32 [4], replicated, may hold values from 32768 to 65536, as said below
Outputs:
- hidden_out: bfloat16 [4, 16384], P(None, 'seq')
Inputs may be any that keep to these rules, and one draw needn't show every extreme that they name: `lengths`: some sequence uses all 65536 cached positions in every draw.
All inputs are finite; a program needn't handle non-finite values.
Results may differ from a plain program's by a relative error of at most 0.02.
The roundings to bfloat16 on the way count: a program that leaves them out, or rounds other values in their place, can miss the bound.
Values sent between devices are 32-bit elements; how exact they have to be, the bound alone decides.
No kernel may reach another device: no remote copies, remote signals or barrier semaphores. Data moves between devices by JAX's collectives and lax.ppermute only.
A program may use at most 64 MiB of HBM per device.

v0:
```python
import functools
import math

import jax
import jax.numpy as jnp
import numpy as np
from jax import lax
from jax.sharding import Mesh
from jax.sharding import PartitionSpec as P

D = 16384
HEADS = 128
KV_HEADS = 8
HEAD_DIM = 128
TILE = 128
DECODE_STEPS = 2
SEQ = ("seq_0", "seq_1")


code_norm = 147.8
epsilon = 1e-05
rope_base = 500000.0


def collected_together(value, axis):
    leaves = jax.tree.leaves(value)
    order = sorted(range(len(leaves)), key=lambda k: -leaves[k].size)
    width = (1, *leaves[order[0]].shape)[-1]
    lines = [
        jnp.pad(leaves[k].reshape(-1), (0, -leaves[k].size % width)).reshape(-1, width)
        for k in order
    ]
    both, at, found = (lax.all_gather(jnp.concatenate(lines), axis), 0, {})
    for k, line in zip(order, lines):
        share = both[:, at : at + len(line)].reshape(len(both), -1)
        found[k] = share[:, : leaves[k].size].reshape(-1, *leaves[k].shape)
        at += len(line)
    numbers = iter(range(len(leaves)))
    return jax.tree.map(lambda _: found[next(numbers)], value)


def merged_by_axis(value, axes, combine):
    for axis in axes:
        pieces = collected_together(value, axis)
        value = jax.tree.map(lambda part: part[0], pieces)
        for k in range(1, lax.axis_size(axis)):
            value = combine(value, jax.tree.map(lambda part: part[k], pieces))
    return value


def one_axis_at_a_time(value, axes):
    return functools.reduce(lax.psum, axes, value)


def from_everyone(value, axis):
    copies = jnp.broadcast_to(value, (lax.axis_size(axis), *value.shape))
    return lax.all_to_all(copies, axis, split_axis=0, concat_axis=0, tiled=True)


def over_copies(value, axis):
    everything = from_everyone(value, axis)
    return jnp.sum(everything, axis=0)


def decode_codes(code_words):
    num_rows = code_words.shape[0]
    tile_bytes = TILE // 4
    byte_tiles = code_words.reshape(num_rows, -1, tile_bytes)
    byte_first = jnp.repeat(byte_tiles, 4, axis=2)
    byte_second = jnp.repeat(jnp.roll(byte_tiles, -1, axis=2), 4, axis=2)
    byte_third = jnp.repeat(jnp.roll(byte_tiles, -2, axis=2), 4, axis=2)
    window = byte_first * 65536 + byte_second * 256 + byte_third
    divisor = jnp.asarray(np.array([256, 64, 16, 4])[np.arange(TILE) % 4], dtype=jnp.int32)
    trellis_state = window // divisor % 65536
    low_product = trellis_state * 25297 + 13946
    low_half = low_product % 65536
    high_half = (trellis_state * 519 + 1169 + low_product // 65536) % 65536
    byte_total = low_half % 256 + low_half // 256 + high_half % 256 + high_half // 256
    return ((byte_total - 510).astype(jnp.float32) / code_norm).reshape(num_rows, -1)


def rope_tables(positions):
    half_dim = HEAD_DIM // 2
    freqs = jnp.exp(
        -(jnp.arange(half_dim, dtype=jnp.float32) * (2.0 / HEAD_DIM)) * math.log(rope_base)
    )
    angles = positions.astype(jnp.float32)[:, None] * freqs[None, :]
    return (jnp.cos(angles), jnp.sin(angles))


def rotate(values, cosine_table, sine_table):
    half_dim = values.shape[-1] // 2
    first_half = values[..., :half_dim]
    second = values[..., half_dim:]
    return jnp.concatenate(
        [
            first_half * cosine_table - second * sine_table,
            second * cosine_table + first_half * sine_table,
        ],
        axis=-1,
    )


def finish(top_max, denominator, numerator, queries, new_keys, new_values):
    score_scale = HEAD_DIM ** (-0.5)
    query_float = queries.astype(jnp.float32)
    new_scores = [
        jnp.sum(query_float * new_key.astype(jnp.float32)[:, :, None, :], axis=-1) * score_scale
        for new_key in new_keys
    ]
    peak_score = top_max
    for new_score in new_scores:
        peak_score = jnp.maximum(peak_score, new_score)
    factor = jnp.exp(top_max - peak_score)
    denominator = denominator * factor
    numerator = numerator * factor[..., None]
    for new_score, new_value in zip(new_scores, new_values):
        weight_new = jnp.exp(new_score - peak_score)
        denominator = denominator + weight_new
        numerator = numerator + weight_new[..., None] * new_value.astype(jnp.float32)[:, :, None, :]
    attended = numerator / denominator[..., None]
    return attended.astype(jnp.bfloat16).reshape(attended.shape[0], -1)


def merge_partials(left_part, right_part):
    left_max, left_sum, left_acc = left_part
    right_max, right_sum, right_acc = right_part
    joined_max = jnp.maximum(left_max, right_max)
    left_factor = jnp.exp(left_max - joined_max)
    right_factor = jnp.exp(right_max - joined_max)
    joined_sum = left_sum * left_factor + right_sum * right_factor
    joined_acc = left_acc * left_factor[..., None] + right_acc * right_factor[..., None]
    return (joined_max, joined_sum, joined_acc)


def combine_blocks(local_max, local_sum, local_acc):
    top_max, denominator, numerator = merged_by_axis(
        (local_max, local_sum, local_acc), SEQ, merge_partials
    )
    return (top_max, denominator, numerator)


def shards(
    hidden_in,
    norm_gain,
    qkv_codes,
    qkv_scale,
    out_codes,
    out_scale,
    cache_keys,
    cache_values,
    lengths,
):
    score_scale = HEAD_DIM ** (-0.5)
    groups = HEADS // KV_HEADS
    w_qkv = (decode_codes(qkv_codes) * qkv_scale[None, :]).astype(jnp.bfloat16)
    w_out = (decode_codes(out_codes) * out_scale[:, None]).astype(jnp.bfloat16)
    batch_size = cache_keys.shape[0]
    block_len = cache_keys.shape[1]
    group_count = cache_keys.shape[2]
    shard_start = lax.axis_index(SEQ) * block_len
    live_mask = (shard_start + jnp.arange(block_len, dtype=jnp.int32))[None, :] < lengths[:, None]
    live_mask = live_mask[:, None, None, :]
    hidden = hidden_in
    new_keys = []
    new_values = []
    for decode_step in range(DECODE_STEPS):
        positions = lengths + decode_step
        squares = jnp.sum(jnp.square(hidden.astype(jnp.float32)), axis=1)
        normed = (hidden.astype(jnp.float32) * norm_gain[None, :]).astype(jnp.bfloat16)
        partial_value = jnp.dot(normed, w_qkv, preferred_element_type=jnp.float32)
        partial_value, squares = (
            one_axis_at_a_time(partial_value, SEQ),
            one_axis_at_a_time(squares, SEQ),
        )
        projected = partial_value * lax.rsqrt(squares / D + epsilon)[:, None]
        grouped = projected.reshape(batch_size, group_count, groups + 2, HEAD_DIM)
        cosine_table, sine_table = rope_tables(positions)
        queries = rotate(
            grouped[:, :, :groups], cosine_table[:, None, None, :], sine_table[:, None, None, :]
        ).astype(jnp.bfloat16)
        new_keys.append(
            rotate(grouped[:, :, groups], cosine_table[:, None, :], sine_table[:, None, :]).astype(
                jnp.bfloat16
            )
        )
        new_values.append(grouped[:, :, groups + 1].astype(jnp.bfloat16))
        scores = (
            jnp.einsum("bgrd,bcgd->bgrc", queries, cache_keys, preferred_element_type=jnp.float32)
            * score_scale
        )
        local_max = jnp.max(jnp.where(live_mask, scores, -1e30), axis=3)
        weights = jnp.where(live_mask, jnp.exp(scores - local_max[..., None]), 0.0)
        local_sum = jnp.sum(weights, axis=3)
        local_acc = jnp.einsum(
            "bgrc,bcgd->bgrd",
            weights.astype(jnp.bfloat16),
            cache_values,
            preferred_element_type=jnp.float32,
        )
        top_max, denominator, numerator = combine_blocks(local_max, local_sum, local_acc)
        attended = finish(top_max, denominator, numerator, queries, new_keys, new_values)
        update = lax.dot_general(
            attended, w_out, (((1,), (1,)), ((), ())), preferred_element_type=jnp.float32
        )
        update = over_copies(update, "head")
        hidden = (hidden.astype(jnp.float32) + update).astype(jnp.bfloat16)
    return hidden


def solution(mesh):
    split = Mesh(mesh.devices.reshape(16, 4, mesh.shape["head"]), ("seq_0", "seq_1", "head"))
    placed = (
        P(None, SEQ),
        P(SEQ),
        P(SEQ, "head"),
        P("head"),
        P(SEQ, "head"),
        P(SEQ),
        P(None, SEQ, "head", None),
        P(None, SEQ, "head", None),
        P(),
    )
    return jax.shard_map(
        shards, mesh=split, in_specs=placed, out_specs=P(None, SEQ), check_vma=False
    )
```

profile of v0, /device:TPU:1, one launch (start us, length us, event | category | flops | bytes accessed | tf_op | source)
XLA Modules:
  0.0 367.4 jit_solution(6575985192465526155)
XLA Ops:
  0.0 1.2 slice.860
  1.3 1.1 slice.862
  2.5 0.2 fusion.45
  2.7 0.4 broadcast_in_dim.41
  3.1 1.9 add.975
  5.1 0.1 fusion.167
  5.2 34.5 %fusion.7 = bf16[256,2304]{0,1:T(8,128)(2,1)S(1)} fusion(s32[256,2304]{0,1:T(8,128)} %add.975, f32[2304]{0:T(1024)S(1)} %broadcast_multiply_fusion.2, s32[2304]{0:T(1024)S(1)} %broadcast_bitcast_fusion), kind=kLoop, calls=%fused_computation.51 | loop fusion | flops 58392576 | bytes 3557376 | tf_op jit(solution)/shard_map/convert_element_type | solution.py:156
  39.7 0.4 fusion.192
  40.1 49.5 %all-reduce.9 = (f32[4,2304]{1,0:T(4,128)S(1)}, f32[4]{0:T(128)S(1)}) all-reduce(f32[4,2304]{1,0:T(4,128)S(1)} %fusion.192, f32[4]{0:T(128)S(1)} %fusion.167), channel_id=1, replica_groups=mesh['seq_0'=16,'seq_1'=4,'head'=8] {'seq_0'}, use_global_device_ids=true, to_apply=%region_0.1 | all-reduce | flops 9220 | bytes 73760 | tf_op jit(solution)/shard_map/psum | solution.py:52
  89.6 13.8 %all-reduce.11 = (f32[4,2304]{1,0:T(4,128)S(1)}, f32[4]{0:T(128)S(1)}) all-reduce(f32[4,2304]{1,0:T(4,128)S(1)} %get-tuple-element.25, f32[4]{0:T(128)S(1)} %get-tuple-element.26), channel_id=1, replica_groups=mesh['seq_0'=16,'seq_1'=4,'head'=8] {'seq_1'}, use_global_device_ids=true, to_apply=%region_1.2 | all-reduce | flops 9220 | bytes 73760 | tf_op jit(solution)/shard_map/psum | solution.py:52
  103.7 0.7 multiply_cosine_fusion.1
  104.6 0.6 copy-done.5
  105.1 0.5 select_reduce_fusion.1
  105.6 0.6 reshape.5494
  106.2 0.8 fusion.48
  107.0 0.9 fusion.40
  108.0 0.8 reshape.5496
  108.8 0.6 pad_bitcast_fusion.6
  109.4 0.8 maximum_bitcast_fusion
  110.1 22.4 %all-gather.4 = f32[16,66,128]{2,1,0:T(8,128)S(1)} all-gather(f32[1,66,128]{2,1,0:T(8,128)S(1)} %maximum_bitcast_fusion), channel_id=2, replica_groups=mesh['seq_0'=16,'seq_1'=4,'head'=8] {'seq_0'}, dimensions={0}, use_global_device_ids=true | all-gather | bytes 574464 | tf_op jit(solution)/shard_map/all_gather | solution.py:33
  132.7 0.3 fusion.108
  133.0 9.6 %all-gather.5 = f32[4,66,128]{2,1,0:T(8,128)S(1)} all-gather(f32[1,66,128]{2,1,0:T(8,128)S(1)} %maximum_bitcast_fusion.1), channel_id=3, replica_groups=mesh['seq_0'=16,'seq_1'=4,'head'=8] {'seq_1'}, dimensions={0}, use_global_device_ids=true | all-gather | bytes 168960 | tf_op jit(solution)/shard_map/all_gather | solution.py:33
  142.7 0.7 fusion.195
  143.4 0.2 copy.20
  143.7 0.9 slice.926
  144.8 0.2 multiply_reduce_fusion
  145.7 0.7 broadcast_multiply_fusion.3
  146.4 1.3 sign_compare_fusion.7
  147.7 57.7 %fusion.37 = bf16[256,16,32,4]{0,3,2,1:T(4,128)(2,1)} fusion(f32[256]{0:T(256)S(1)} %broadcast_multiply_fusion.3, s32[32,4]{1,0:T(8,128)S(1)} %copy-done.10, s32[256,16,32]{0,2,1:T(8,128)S(1)} %get-tuple-element.131, pred[256,16,32]{0,2,1:T(8,128)(4,1)S(1)} %get-tuple-element.130), kind=kLoop, calls=%fused_computation.92 | loop fusion | flops 50855936 | bytes 1705472 | tf_op jit(solution)/shard_map/convert_element_type | solution.py:157
  205.4 1.4 convert_element_type.227
  206.8 0.1 fusion.164
  206.9 0.2 fusion.155
  207.2 35.9 %all_to_all.10 = f32[8,4,256]{2,1,0:T(4,128)S(1)} all-to-all(f32[8,4,256]{2,1,0:T(4,128)S(1)} %broadcast_in_dim.46), channel_id=1, replica_groups=mesh['seq_0'=16,'seq_1'=4,'head'=8] {'head'}, dimensions={0} | all-to-all | bytes 65536 | tf_op jit(solution)/shard_map/all_to_all | solution.py:57
  243.1 0.1 fusion.170
  243.2 0.4 fusion.190
  243.6 40.9 %all-reduce.8 = (f32[4,2304]{1,0:T(4,128)S(1)}, f32[4]{0:T(128)S(1)}) all-reduce(f32[4,2304]{1,0:T(4,128)S(1)} %fusion.190, f32[4]{0:T(128)S(1)} %get-tuple-element.80), channel_id=1, replica_groups=mesh['seq_0'=16,'seq_1'=4,'head'=8] {'seq_0'}, use_global_device_ids=true, to_apply=%region_9.10 | all-reduce | flops 9220 | bytes 73760 | tf_op jit(solution)/shard_map/psum | solution.py:52
  284.5 11.2 %all-reduce.10 = (f32[4,2304]{1,0:T(4,128)S(1)}, f32[4]{0:T(128)S(1)}) all-reduce(f32[4,2304]{1,0:T(4,128)S(1)} %get-tuple-element.23, f32[4]{0:T(128)S(1)} %get-tuple-element.24), channel_id=1, replica_groups=mesh['seq_0'=16,'seq_1'=4,'head'=8] {'seq_1'}, use_global_device_ids=true, to_apply=%region_10.11 | all-reduce | flops 9220 | bytes 73760 | tf_op jit(solution)/shard_map/psum | solution.py:52
  295.9 0.5 select_reduce_fusion
  296.4 1.5 fusion.38
  298.0 0.2 fusion.50
  298.4 22.1 %all-gather.6 = f32[16,66,128]{2,1,0:T(8,128)S(1)} all-gather(f32[1,66,128]{2,1,0:T(8,128)S(1)} %maximum_bitcast_fusion.2), channel_id=4, replica_groups=mesh['seq_0'=16,'seq_1'=4,'head'=8] {'seq_0'}, dimensions={0}, use_global_device_ids=true | all-gather | bytes 574464 | tf_op jit(solution)/shard_map/all_gather | solution.py:33
  320.7 0.3 fusion.63
  321.0 9.1 %all-gather.7 = f32[4,66,128]{2,1,0:T(8,128)S(1)} all-gather(f32[1,66,128]{2,1,0:T(8,128)S(1)} %maximum_bitcast_fusion.3), channel_id=5, replica_groups=mesh['seq_0'=16,'seq_1'=4,'head'=8] {'seq_1'}, dimensions={0}, use_global_device_ids=true | all-gather | bytes 168960 | tf_op jit(solution)/shard_map/all_gather | solution.py:33
  330.4 0.2 fusion.60
  331.4 0.2 fusion.165
  331.5 0.2 fusion.152
  331.8 35.0 %all_to_all.11 = f32[8,4,256]{2,1,0:T(4,128)S(1)} all-to-all(f32[8,4,256]{2,1,0:T(4,128)S(1)} %broadcast_in_dim.47), channel_id=1, replica_groups=mesh['seq_0'=16,'seq_1'=4,'head'=8] {'head'}, dimensions={0} | all-to-all | bytes 65536 | tf_op jit(solution)/shard_map/all_to_all | solution.py:57
  366.8 0.6 fusion.171
  (123 shorter events, 3.1 us)
Async XLA Ops:
  0.0 105.1 %copy-start = (bf16[4,1024,1,128]{3,1,2,0:T(8,128)(2,1)S(1)}, bf16[4,1024,1,128]{3,1,2,0:T(8,128)(2,1)}, u32[]{:S(2)}) copy-start(bf16[4,1024,1,128]{3,1,2,0:T(8,128)(2,1)} %param.17) | copy-start | bytes 3145732
  0.0 2.4 copy-start.1
  2.5 101.3 %copy-start.14 = (f32[64]{0:T(128)}, f32[64]{0:T(128)S(1)}, u32[]{:S(2)}) copy-start(f32[64]{0:T(128)S(1)} %multiply_exponential_fusion) | copy-start | bytes 772
  3.1 1.9 copy-start.24
  3.1 1.9 copy-start.11
  3.1 1.9 copy-start.9
  5.0 34.7 %copy-start.17 = (f32[256]{0:T(256)S(1)}, f32[256]{0:T(256)}, u32[]{:S(2)}) copy-start(f32[256]{0:T(256)} %param.12) | copy-start | bytes 3076
  5.2 98.4 %copy-start.23 = (s32[4]{0:T(128)S(1)}, s32[4]{0:T(128)}, u32[]{:S(2)}) copy-start(s32[4]{0:T(128)} %param.19) | copy-start | bytes 52
  39.7 67.3 %copy-start.2 = (bf16[4,1024,1,128]{3,1,2,0:T(8,128)(2,1)S(1)}, bf16[4,1024,1,128]{3,1,2,0:T(8,128)(2,1)}, u32[]{:S(2)}) copy-start(bf16[4,1024,1,128]{3,1,2,0:T(8,128)(2,1)} %param.18) | copy-start | bytes 3145732
  103.6 1.0 copy-start.4
  103.6 1.0 copy-start.19
  103.6 1.0 copy-start.21
  104.5 0.6 copy-start.5
  104.5 1.1 copy-start.7
  108.0 35.5 %copy-start.3 = (s32[256,512]{1,0:T(8,128)S(1)}, s32[256,512]{1,0:T(8,128)}, u32[]{:S(2)}) copy-start(s32[256,512]{1,0:T(8,128)} %param.15) | copy-start | bytes 1572868
  132.7 11.9 %copy-start.15 = (f32[64]{0:T(128)S(1)}, f32[64]{0:T(128)}, u32[]{:S(2)}) copy-start(f32[64]{0:T(128)} %copy-done.14) | copy-start | bytes 772
  132.7 12.1 %copy-start.6 = (bf16[4,1,16,64]{3,2,0,1:T(8,128)(2,1)S(1)}, bf16[4,1,16,64]{3,2,0,1:T(8,128)(2,1)}, u32[]{:S(2)}) copy-start(bf16[4,1,16,64]{3,2,0,1:T(8,128)(2,1)} %copy-done.5) | copy-start | bytes 24580
  132.7 12.1 %copy-start.8 = (bf16[4,1,16,64]{3,2,0,1:T(8,128)(2,1)S(1)}, bf16[4,1,16,64]{3,2,0,1:T(8,128)(2,1)}, u32[]{:S(2)}) copy-start(bf16[4,1,16,64]{3,2,0,1:T(8,128)(2,1)} %copy-done.7) | copy-start | bytes 24580
  133.0 11.6 %copy-start.22 = (f32[4]{0:T(128)S(1)}, f32[4]{0:T(128)}, u32[]{:S(2)}) copy-start(f32[4]{0:T(128)} %copy-done.21) | copy-start | bytes 52
  143.6 4.0 %copy-start.10 = (s32[32,4]{1,0:T(8,128)S(1)}, s32[32,4]{1,0:T(8,128)}, u32[]{:S(2)}) copy-start(s32[32,4]{1,0:T(8,128)} %constant.217) | copy-start | bytes 1540
  205.4 37.8 %copy-start.18 = (f32[256]{0:T(256)S(1)}, f32[256]{0:T(256)}, u32[]{:S(2)}) copy-start(f32[256]{0:T(256)} %param.12) | copy-start | bytes 3076
  205.4 90.4 %copy-start.12 = (f32[4,64]{1,0:T(4,128)S(1)}, f32[4,64]{1,0:T(4,128)}, u32[]{:S(2)}) copy-start(f32[4,64]{1,0:T(4,128)} %get-tuple-element.156) | copy-start | bytes 3076
  205.4 90.4 %copy-start.13 = (f32[4,64]{1,0:T(4,128)S(1)}, f32[4,64]{1,0:T(4,128)}, u32[]{:S(2)}) copy-start(f32[4,64]{1,0:T(4,128)} %get-tuple-element.157) | copy-start | bytes 3076
  296.4 33.8 %copy-start.16 = (f32[64]{0:T(128)S(1)}, f32[64]{0:T(128)}, u32[]{:S(2)}) copy-start(f32[64]{0:T(128)} %copy-done.14) | copy-start | bytes 772
  296.4 33.8 %copy-start.20 = (f32[4]{0:T(128)S(1)}, f32[4]{0:T(128)}, u32[]{:S(2)}) copy-start(f32[4]{0:T(128)} %copy-done.19) | copy-start | bytes 52
where the time goes:
time: 368 us; the launch traced here: 367 us
  blocking collectives  250 us (68%)
  other arithmetic  101 us (27%)
  local copies, waits for them, and re-layouts  11.6 us (3%)
  matrix products  4.83 us (1%)
    psum x4, blocking collectives, one_axis_at_a_time(): return functools.reduce(lax.psum, axes, value)  115 us
    all_to_all x2, blocking collectives, from_everyone(): return lax.all_to_all(copies, axis, split_axis=0, concat_axis=0, tiled=True)  70.9 us
    all_gather x4, blocking collectives, collected_together(): both, at, found = (lax.all_gather(jnp.concatenate(lines), axis), 0, {})  63.3 us
    convert_element_type x1, other arithmetic, shards(): w_out = (decode_codes(out_codes) * out_scale[:, None]).astype(jnp.bfloat16)  57.7 us
    convert_element_type x1, other arithmetic, shards(): w_qkv = (decode_codes(qkv_codes) * qkv_scale[None, :]).astype(jnp.bfloat16)  34.5 us

commit v1 on v0

v1 whole, which is shorter than its diff:
```python
import functools
import math

import jax
import jax.numpy as jnp
from jax import lax
from jax.experimental import pallas as pl
from jax.experimental.pallas import tpu as pltpu
from jax.sharding import Mesh
from jax.sharding import PartitionSpec as P

HEAD_DIM = 128
GROUPS = 16
DECODE_STEPS = 2
NEAR = ("z_low", "y")
FAR = "z_high"
SEQ = (FAR, *NEAR)

CODE_NORM = 147.8
EPSILON = 1e-05
ROPE_BASE = 500000.0
SCORE_SCALE = HEAD_DIM ** (-0.5)

GROUP_ROW = (0, 512, 1152, 1664)
GROUP_PLACE = (0, 2, 1, 3)
TAIL_ROW = (1024, 2176)

f32 = jnp.float32
bf16 = jnp.bfloat16
NT = (((1,), (1,)), ((), ()))


def iota(shape, axis):
    return lax.broadcasted_iota(jnp.int32, shape, axis)


def call(kernel, outs, name):
    return pl.pallas_call(
        kernel,
        out_shape=outs,
        name=name,
        compiler_params=pltpu.CompilerParams(vmem_limit_bytes=48 * 1024 * 1024),
    )


def shape_of(shape, dtype=f32):
    return jax.ShapeDtypeStruct(shape, dtype)


def byte_sum(state):
    x = state * 34038481 + 76625530
    pairs = (x & 0x00FF00FF) + ((x >> 8) & 0x00FF00FF)
    total = (pairs + (pairs >> 16)) & 0x7FF
    return (total - 510).astype(f32)


def interleave():
    row = iota((512, 512), 0)
    column = iota((512, 512), 1)
    return (column == 4 * (row & 127) + (row >> 7)).astype(f32).astype(bf16)


def by_sequence():
    row = iota((64, 64), 0)
    column = iota((64, 64), 1)
    return (column == 4 * (row & 15) + (row >> 4)).astype(f32).astype(bf16)


def exact_product(x, ones):
    rows = x.shape[0]
    high = x.astype(bf16).astype(f32)
    rest = x - high
    middle = rest.astype(bf16).astype(f32)
    low = rest - middle
    parts = jnp.concatenate([high, middle, low, jnp.zeros_like(low)], axis=0).astype(bf16)
    product = jnp.dot(parts, ones, preferred_element_type=f32)
    return product[:rows] + product[rows : 2 * rows] + product[2 * rows : 3 * rows]


def project(hidden, gain, weights, out_ref):
    squares = jnp.sum(hidden * hidden, axis=1, keepdims=True)
    normed = (hidden * gain).astype(bf16)
    y = lax.dot_general(normed, weights, NT, preferred_element_type=f32)
    half = y.shape[1] // 2
    first = iota((8, half), 0) < 4
    packed = jnp.where(first, y[:, :half], y[:, half:])
    spread = jnp.broadcast_to(squares, (8, 128))
    for j in range(out_ref.shape[0]):
        out_ref[j, :, :half] = packed
        out_ref[j, :, half:] = spread


def decode_qkv_kernel(hidden_ref, gain_ref, codes_ref, scale_ref, w_ref, hid_ref, out_ref):
    lane = iota((32, 128), 1)
    word = iota((32, 128), 0)
    for tile in range(18):
        codes = codes_ref[tile * 32 : tile * 32 + 32, :]
        window = (codes << 16) | (pltpu.roll(codes, 31, 0) << 8) | pltpu.roll(codes, 30, 0)
        scales = jnp.broadcast_to(scale_ref[tile : tile + 1, :], (32, 128)) * (1.0 / CODE_NORM)
        for r in range(4):
            column = jnp.sum(
                jnp.where(lane == 4 * word + r, scales, 0.0), axis=1, keepdims=True
            )
            values = byte_sum((window >> (8 - 2 * r)) & 0xFFFF) * column
            if tile < 16:
                at = GROUP_ROW[tile // 4] + r * 128 + (tile % 4) * 32
            else:
                at = TAIL_ROW[r // 2] + (r % 2) * 64 + (tile - 16) * 32
            w_ref[at : at + 32, :] = values.astype(bf16)
    hidden = hidden_ref[...].astype(f32)
    hidden = jnp.concatenate([hidden, hidden], axis=0)
    hid_ref[...] = hidden
    project(hidden, gain_ref[...], w_ref[...], out_ref)


def decode_out_kernel(codes_ref, scale_ref, w_ref):
    lane = iota((32, 128), 1)
    within = lane & 31
    for block in range(8):
        rows = slice(block * 32, block * 32 + 32)
        across = iota((32, 256), 1) == iota((32, 256), 0) + block * 32
        scale = jnp.broadcast_to(scale_ref[...], (32, 256)) * (1.0 / CODE_NORM)
        column = jnp.sum(jnp.where(across, scale, 0.0), axis=1, keepdims=True)
        for group in range(4):
            codes = codes_ref[rows, group * 128 : group * 128 + 128]
            second = jnp.where(within < 31, pltpu.roll(codes, 127, 1), pltpu.roll(codes, 31, 1))
            third = jnp.where(within < 30, pltpu.roll(codes, 126, 1), pltpu.roll(codes, 30, 1))
            window = (codes << 16) | (second << 8) | third
            for r in range(4):
                values = byte_sum((window >> (8 - 2 * r)) & 0xFFFF) * column
                at = group * 512 + r * 128
                w_ref[rows, at : at + 128] = values.astype(bf16)


def total_of(ref):
    total = ref[0]
    for j in range(1, ref.shape[0]):
        total = total + ref[j]
    return total


def pass_sum_kernel(in_ref, out_ref):
    total = total_of(in_ref)
    for j in range(out_ref.shape[0]):
        out_ref[j] = total


def store_partial(out_ref, m_row, l_row, acc):
    stats = jnp.concatenate([m_row, l_row], axis=1)
    stats = jnp.broadcast_to(stats, (8, 128))
    for j in range(out_ref.shape[0]):
        out_ref[j, :64, :] = acc
        out_ref[j, 64:, :] = stats


def merged(in_ref):
    count = in_ref.shape[0]
    stats = [in_ref[j, 64:65, :] for j in range(count)]
    top = functools.reduce(jnp.maximum, [s[:, :64] for s in stats])
    factors = [jnp.exp(s[:, :64] - top) for s in stats]
    sums = functools.reduce(lambda a, b: a + b, [s[:, 64:] * w for s, w in zip(stats, factors)])
    across = iota((64, 64), 0) == iota((64, 64), 1)

    def as_column(row):
        return jnp.sum(jnp.where(across, jnp.broadcast_to(row, (64, 64)), 0.0), axis=1, keepdims=True)

    acc = in_ref[0, :64, :] * as_column(factors[0])
    for j in range(1, count):
        acc = acc + in_ref[j, :64, :] * as_column(factors[j])
    return top, sums, acc, as_column


def pass_merge_kernel(in_ref, out_ref):
    top, sums, acc, _ = merged(in_ref)
    store_partial(out_ref, top, sums, acc)


def attend_kernel(features, limit_ref, in_ref, cos_ref, sin_ref, keys_ref, values_ref,
                  out_ref, q_ref, k_ref, v_ref):
    y = total_of(in_ref)
    rms = lax.rsqrt(y[:, 1152:] / features + EPSILON)
    y = y[:, :1152] * jnp.concatenate([rms] * 9, axis=1)
    heads = jnp.concatenate([y[:, :512], y[:, 512:1024]], axis=0)
    heads = exact_product(heads, interleave())
    row = iota((128, 512), 0)
    column = iota((128, 512), 1)
    where_to = ((row >> 5) & 1) * 128 + 4 * (row & 31) + (row >> 6) + 2 * (column >> 8)
    spread = ((column & 255) == where_to).astype(f32).astype(bf16)
    tail = exact_product(y[:, 1024:], spread)
    tail = tail[:, :256] + pltpu.roll(tail[:, 256:], 4, 0)
    cos = cos_ref[...]
    sin = sin_ref[...]
    key = tail[:, :128]
    key = key * cos + pltpu.roll(key, 64, 1) * sin
    k_ref[...] = key.astype(bf16).astype(f32)
    v_ref[...] = tail[:, 128:].astype(bf16).astype(f32)
    cos = jnp.concatenate([cos, cos], axis=0)
    sin = jnp.concatenate([sin, sin], axis=0)
    turned = []
    for tile in range(4):
        part = heads[:, tile * 128 : tile * 128 + 128]
        turned.append(part * cos + pltpu.roll(part, 64, 1) * sin)
    queries = jnp.concatenate(turned, axis=0).astype(bf16)
    queries = jnp.dot(by_sequence(), queries, preferred_element_type=f32)
    q_ref[...] = queries
    queries = queries.astype(bf16)
    length = keys_ref.shape[1]
    place = iota((16, length), 1)
    maxima, sums, accs = [], [], []
    for b in range(4):
        scores = lax.dot_general(
            queries[b * 16 : b * 16 + 16], keys_ref[b], NT, preferred_element_type=f32
        ) * SCORE_SCALE
        live = place < limit_ref[b]
        top = jnp.max(jnp.where(live, scores, -1e30), axis=1, keepdims=True)
        weights = jnp.where(live, jnp.exp(scores - top), 0.0)
        maxima.append(top)
        sums.append(jnp.sum(weights, axis=1, keepdims=True))
        accs.append(jnp.dot(weights.astype(bf16), values_ref[b], preferred_element_type=f32))
    across = iota((64, 64), 0) == iota((64, 64), 1)

    def as_row(columns):
        column = jnp.broadcast_to(jnp.concatenate(columns, axis=0), (64, 64))
        return jnp.sum(jnp.where(across, column, 0.0), axis=0, keepdims=True)

    store_partial(out_ref, as_row(maxima), as_row(sums), jnp.concatenate(accs, axis=0))


def finish_kernel(steps, in_ref, q_ref, w_ref, *refs):
    out_ref = refs[-1]
    top, sums, acc, as_column = merged(in_ref)
    top, denominator = as_column(top), as_column(sums)
    queries = q_ref[...]

    def by_head(ref):
        return jnp.concatenate(
            [jnp.broadcast_to(ref[b : b + 1, :], (16, 128)) for b in range(4)], axis=0
        )

    scores = [
        jnp.sum(queries * by_head(refs[2 * u]), axis=1, keepdims=True) * SCORE_SCALE
        for u in range(steps)
    ]
    peak = functools.reduce(jnp.maximum, scores, top)
    factor = jnp.exp(top - peak)
    denominator = denominator * factor
    numerator = acc * factor
    for u in range(steps):
        weight = jnp.exp(scores[u] - peak)
        denominator = denominator + weight
        numerator = numerator + weight * by_head(refs[2 * u + 1])
    attended = (numerator / denominator).astype(bf16)
    attended = lax.dot_general(
        by_sequence(), attended, (((0,), (0,)), ((), ())), preferred_element_type=f32
    )
    attended = jnp.concatenate([attended[t * 16 : t * 16 + 16] for t in range(4)], axis=1)
    attended = lax.dot_general(
        attended.astype(bf16), interleave(), NT, preferred_element_type=f32
    )
    place = iota((16, 512), 0) >> 2
    columns = jnp.concatenate(
        [jnp.where(place == GROUP_PLACE[g], attended, 0.0) for g in range(4)], axis=1
    ).astype(bf16)
    update = lax.dot_general(columns, w_ref[...], NT, preferred_element_type=f32)
    update = update[:8] + update[8:]
    update = update + pltpu.roll(update, 4, 0)
    packed = jnp.where(iota((8, 128), 0) < 4, update[:, :128], update[:, 128:])
    for j in range(out_ref.shape[0]):
        out_ref[j] = packed


def updated(in_ref, hid_ref):
    update = total_of(in_ref)
    turned = pltpu.roll(update, 4, 0)
    first = iota((8, 128), 0) < 4
    update = jnp.concatenate(
        [jnp.where(first, update, turned), jnp.where(first, turned, update)], axis=1
    )
    return (hid_ref[...] + update).astype(bf16)


def next_kernel(in_ref, hid_ref, gain_ref, w_ref, new_ref, out_ref):
    hidden = updated(in_ref, hid_ref).astype(f32)
    new_ref[...] = hidden
    project(hidden, gain_ref[...], w_ref[...], out_ref)


def last_kernel(in_ref, hid_ref, out_ref):
    out_ref[...] = updated(in_ref, hid_ref)[:4]


def exchange(value, axes):
    return lax.all_to_all(value, axes, split_axis=0, concat_axis=0, tiled=True)


def shards(features, hidden_in, norm_gain, qkv_codes, qkv_scale, out_codes, out_scale,
           cache_keys, cache_values, lengths):
    near = lax.axis_size(NEAR)
    far = lax.axis_size(FAR)
    heads = lax.axis_size("head")
    gain = norm_gain.reshape(1, -1)
    batch, block_len = cache_keys.shape[:2]
    keys = cache_keys.reshape(batch, block_len, HEAD_DIM)
    values = cache_values.reshape(batch, block_len, HEAD_DIM)
    limit = lengths - lax.axis_index(SEQ) * block_len

    half_dim = HEAD_DIM // 2
    freqs = jnp.exp(
        -(jnp.arange(half_dim, dtype=f32) * (2.0 / HEAD_DIM)) * math.log(ROPE_BASE)
    )
    steps = jnp.arange(DECODE_STEPS, dtype=jnp.int32)
    positions = lengths[None, :] + steps[:, None]
    angles = positions.astype(f32)[:, :, None] * freqs
    cosines, sines = jnp.cos(angles), jnp.sin(angles)
    cosines = jnp.tile(jnp.concatenate([cosines, cosines], axis=-1), (1, 2, 1))
    sines = jnp.tile(jnp.concatenate([-sines, sines], axis=-1), (1, 2, 1))

    w_qkv, hidden, partial = call(
        decode_qkv_kernel,
        (shape_of((2304, 256), bf16), shape_of((8, 256)), shape_of((near, 8, 1280))),
        "decode_qkv",
    )(hidden_in, gain, qkv_codes.T, qkv_scale.reshape(18, 128))
    w_out = call(decode_out_kernel, shape_of((256, 2048), bf16), "decode_out")(
        out_codes, out_scale.reshape(1, -1)
    )
    fresh = []
    for step in range(DECODE_STEPS):
        partial = exchange(partial, NEAR)
        partial = call(pass_sum_kernel, shape_of((far, 8, 1280)), "pass_sum")(partial)
        partial = exchange(partial, FAR)
        part, queries, new_key, new_value = pl.pallas_call(
            functools.partial(attend_kernel, features),
            out_shape=(
                shape_of((near, 72, 128)),
                shape_of((64, 128)),
                shape_of((8, 128)),
                shape_of((8, 128)),
            ),
            in_specs=[pl.BlockSpec(memory_space=pltpu.SMEM)]
            + [pl.BlockSpec(memory_space=pltpu.VMEM)] * 5,
            name="attend",
            compiler_params=pltpu.CompilerParams(vmem_limit_bytes=48 * 1024 * 1024),
        )(limit, partial, cosines[step], sines[step], keys, values)
        fresh += [new_key, new_value]
        part = exchange(part, NEAR)
        part = call(pass_merge_kernel, shape_of((far, 72, 128)), "pass_merge")(part)
        part = exchange(part, FAR)
        update = call(
            functools.partial(finish_kernel, step + 1), shape_of((heads, 8, 128)), "finish"
        )(part, queries, w_out, *fresh)
        update = exchange(update, "head")
        if step + 1 < DECODE_STEPS:
            hidden, partial = call(
                next_kernel, (shape_of((8, 256)), shape_of((near, 8, 1280))), "next_step"
            )(update, hidden, gain, w_qkv)
    return call(last_kernel, shape_of((4, 256), bf16), "last")(update, hidden)


def solution(mesh):
    seq, head = mesh.shape["seq"], mesh.shape["head"]
    far = seq // 8
    split = Mesh(mesh.devices.reshape(far, 2, 4, head), (*SEQ, "head"))
    placed = (
        P(None, SEQ),
        P(SEQ),
        P(SEQ, "head"),
        P("head"),
        P(SEQ, "head"),
        P(SEQ),
        P(None, SEQ, "head", None),
        P(None, SEQ, "head", None),
        P(),
    )

    def run(hidden_in, *others):
        features = hidden_in.shape[1]
        return jax.shard_map(
            functools.partial(shards, float(features)),
            mesh=split,
            in_specs=placed,
            out_specs=P(None, SEQ),
            check_vma=False,
        )(hidden_in, *others)

    return run
```

time: 368 us -> 190 us (0.52)
  blocking collectives: 250 us -> 115 us
  other arithmetic: 101 us -> 0.22 us
  waiting for transfers between devices: 0 us -> 35.7 us
  starting transfers between devices: 0 us -> 20.8 us
  Pallas kernels: 0 us -> 12.4 us
  local copies, waits for them, and re-layouts: 11.6 us -> 5.23 us
  matrix products: 4.83 us -> 0 us
    psum x4 -> x0, blocking collectives: 115 us -> none  [one_axis_at_a_time(): return functools.reduce(lax.psum, axes, value)]
    convert_element_type x6 -> x1, other arithmetic: 92.9 us -> 0.01 us  [shards(): angles = positions.astype(f32)[:, :, None] * freqs]
    all_gather x4 -> x0, blocking collectives: 63.3 us -> none  [collected_together(): both, at, found = (lax.all_gather(jnp.concatenate(lines), axis), 0, {})]
    all_to_all x2 -> x8, blocking collectives: 70.9 us -> 115 us  [exchange(): return lax.all_to_all(value, axes, split_axis=0, concat_axis=0, tiled=True)]
    all_to_all x0 -> x2, waiting for transfers between devices: none -> 35.7 us  [exchange(): return lax.all_to_all(value, axes, split_axis=0, concat_axis=0, tiled=True)]
    all_to_all x0 -> x2, starting transfers between devices: none -> 20.8 us  [exchange(): return lax.all_to_all(value, axes, split_axis=0, concat_axis=0, tiled=True)]
    pallas_call x0 -> x12, Pallas kernels: none -> 12.4 us  [the longest x2 4.64 us: shards(): pl.pallas_call(functools.partial(attend_kernel, features), out_shape=(sha...]
    dot_general x8 -> x0, matrix products: 4.83 us -> none  [the longest x2 2.48 us: shards(): jnp.einsum('bgrc,bcgd->bgrd', weights.astype(jnp.bfloat16), cache_values,...]
  transfers between devices with their start and end apart: 0 -> 2, of which waited for: 0 -> 2; matrix products, arithmetic and copies ran while one was open for 0% -> 0% of each run, Pallas kernels for 0% -> 1%
where the time goes in v1:
time: 190 us; the launch traced here: 189 us
  blocking collectives  115 us (61%)
  waiting for transfers between devices  35.7 us (19%)
  starting transfers between devices  20.8 us (11%)
  Pallas kernels  12.4 us (7%)
  local copies, waits for them, and re-layouts  5.23 us (3%)
    all_to_all x8, blocking collectives, exchange(): return lax.all_to_all(value, axes, split_axis=0, concat_axis=0, tiled=True)  115 us
    all_to_all x2, waiting for transfers between devices, exchange(): return lax.all_to_all(value, axes, split_axis=0, concat_axis=0, tiled=True)  35.7 us
    all_to_all x2, starting transfers between devices, exchange(): return lax.all_to_all(value, axes, split_axis=0, concat_axis=0, tiled=True)  20.8 us
    unnamed x24, local copies, waits for them, and re-layouts  5.22 us
    pallas_call x2, Pallas kernels, shards(): pl.pallas_call(functools.partial(attend_kernel, features), out_shape=(sha...  4.64 us
  transfers between devices with their start and end apart: 2, of which 2 were waited for; matrix products, arithmetic and copies ran while one was open for 0% of the time, Pallas kernels for 1%

profile of v1, /device:TPU:1, one launch (start us, length us, event | category | flops | bytes accessed | tf_op | source)
XLA Modules:
  0.0 189.4 jit_solution(12633307500990825193)
XLA Ops:
  0.0 0.0 copy-start.4
  0.0 1.1 copy-done.4
  1.1 0.0 copy-start.6
  1.1 0.7 copy-done.6
  1.8 0.0 copy-start.7
  1.8 0.7 copy-done.7
  2.5 0.0 copy-start.9
  2.5 0.7 copy-done.9
  3.1 0.0 copy-start.11
  3.1 0.0 copy-start.1
  3.1 1.5 decode_qkv.1
  4.7 0.0 copy-start.2
  4.7 1.0 copy-done.2
  5.7 0.0 copy-start
  5.7 12.9 %all_to_all.50.in_ref = f32[8,8,1280]{2,1,0:T(8,128)S(1)} all-to-all(f32[8,8,1280]{2,1,0:T(8,128)S(1)} %get-tuple-element.18), channel_id=1, replica_groups=mesh['z_high'=8,'z_low'=2,'y'=4,'head'=8] {'z_low','y'}, dimensions={0} | all-to-all | bytes 655360 | tf_op jit(solution)/shard_map/all_to_all | solution.py:293
  18.6 0.7 pass_sum.2
  19.3 14.0 %all-to-all-start.1 = ((f32[8,8,1280]{2,1,0:T(8,128)}), f32[8,8,1280]{2,1,0:T(8,128)S(1)}, u32[]{:S(2)}, u32[]{:S(2)}) async-start(f32[8,8,1280]{2,1,0:T(8,128)} %pass_sum.2), calls=%async_computation.1 | async-start | bytes 655360 | tf_op jit(solution)/shard_map/all_to_all | solution.py:293
  33.4 0.0 copy-done.11
  33.4 0.1 multiply_sine_fusion
  33.5 0.1 fusion.4
  33.6 19.6 %all-to-all-done.1.in_ref = f32[8,8,1280]{2,1,0:T(8,128)S(1)} async-done(((f32[8,8,1280]{2,1,0:T(8,128)}), f32[8,8,1280]{2,1,0:T(8,128)S(1)}, u32[]{:S(2)}, u32[]{:S(2)}) %all-to-all-start.1) | async-done | bytes 327712 | tf_op jit(solution)/shard_map/all_to_all | solution.py:293
  53.2 0.0 copy-done.1
  53.2 0.0 copy-done
  53.2 2.3 %attend.2 = (f32[8,72,128]{2,1,0:T(8,128)S(1)}, f32[64,128]{1,0:T(8,128)S(1)}, f32[8,128]{1,0:T(8,128)S(1)}, f32[8,128]{1,0:T(8,128)S(1)}) custom-call(s32[4]{0:T(128)S(1)} %broadcast_subtract_fusion.limit_ref, f32[8,8,1280]{2,1,0:T(8,128)S(1)} %all-to-all-done.1.in_ref, f32[8,128]{1,0:T(8,128)S(1)} %bitcast.24, f32[8,128]{1,0:T(8,128)S(1)} %bitcast.26, ...), custom_call_target="tpu_custom_call" | custom-call | tf_op jit(solution)/shard_map/attend/pallas_call | solution.py:331
  55.5 0.0 copy-start.10
  55.5 9.7 %all_to_all.51.in_ref = f32[8,72,128]{2,1,0:T(8,128)S(1)} all-to-all(f32[8,72,128]{2,1,0:T(8,128)S(1)} %get-tuple-element.19), channel_id=1, replica_groups=mesh['z_high'=8,'z_low'=2,'y'=4,'head'=8] {'z_low','y'}, dimensions={0} | all-to-all | bytes 589824 | tf_op jit(solution)/shard_map/all_to_all | solution.py:293
  65.2 0.9 pass_merge.2
  66.1 6.8 %all-to-all-start.3 = ((f32[8,72,128]{2,1,0:T(8,128)}), f32[8,72,128]{2,1,0:T(8,128)S(1)}, u32[]{:S(2)}, u32[]{:S(2)}) async-start(f32[8,72,128]{2,1,0:T(8,128)} %pass_merge.2), calls=%async_computation.3 | async-start | bytes 589824 | tf_op jit(solution)/shard_map/all_to_all | solution.py:293
  72.9 0.0 copy-done.10
  72.9 0.0 copy-start.5
  72.9 1.0 copy-done.5
  74.0 0.0 copy-start.8
  74.0 1.2 decode_out.1.w_ref
  75.2 16.2 %all-to-all-done.3.in_ref = f32[8,72,128]{2,1,0:T(8,128)S(1)} async-done(((f32[8,72,128]{2,1,0:T(8,128)}), f32[8,72,128]{2,1,0:T(8,128)S(1)}, u32[]{:S(2)}, u32[]{:S(2)}) %all-to-all-start.3) | async-done | bytes 294944 | tf_op jit(solution)/shard_map/all_to_all | solution.py:293
  91.4 1.1 finish.2
  92.4 13.6 %all_to_all.52.in_ref = f32[8,8,128]{2,1,0:T(8,128)S(1)} all-to-all(f32[8,8,128]{2,1,0:T(8,128)S(1)} %finish.2), channel_id=1, replica_groups=mesh['z_high'=8,'z_low'=2,'y'=4,'head'=8] {'head'}, dimensions={0} | all-to-all | bytes 65536 | tf_op jit(solution)/shard_map/all_to_all | solution.py:293
  106.0 0.0 copy-done.8
  106.0 0.0 copy-done.3
  106.0 0.4 next_step.1
  106.5 9.2 %all_to_all.53.in_ref = f32[8,8,1280]{2,1,0:T(8,128)S(1)} all-to-all(f32[8,8,1280]{2,1,0:T(8,128)S(1)} %get-tuple-element.25), channel_id=1, replica_groups=mesh['z_high'=8,'z_low'=2,'y'=4,'head'=8] {'z_low','y'}, dimensions={0} | all-to-all | bytes 655360 | tf_op jit(solution)/shard_map/all_to_all | solution.py:293
  115.8 24.1 %all_to_all.54.in_ref = f32[8,8,1280]{2,1,0:T(8,128)S(1)} all-to-all(f32[8,8,1280]{2,1,0:T(8,128)S(1)} %pass_sum.3), channel_id=1, replica_groups=mesh['z_high'=8,'z_low'=2,'y'=4,'head'=8] {'z_high'}, dimensions={0} | all-to-all | bytes 655360 | tf_op jit(solution)/shard_map/all_to_all | solution.py:293
  139.9 2.3 %attend.3 = (f32[8,72,128]{2,1,0:T(8,128)S(1)}, f32[64,128]{1,0:T(8,128)S(1)}, f32[8,128]{1,0:T(8,128)S(1)}, f32[8,128]{1,0:T(8,128)S(1)}) custom-call(s32[4]{0:T(128)S(1)} %broadcast_subtract_fusion.limit_ref, f32[8,8,1280]{2,1,0:T(8,128)S(1)} %all_to_all.54.in_ref, f32[8,128]{1,0:T(8,128)S(1)} %bitcast.23, f32[8,128]{1,0:T(8,128)S(1)} %bitcast.25, ...), custom_call_target="tpu_custom_call" | custom-call | tf_op jit(solution)/shard_map/attend/pallas_call | solution.py:331
  142.2 8.9 %all_to_all.55.in_ref = f32[8,72,128]{2,1,0:T(8,128)S(1)} all-to-all(f32[8,72,128]{2,1,0:T(8,128)S(1)} %get-tuple-element.26), channel_id=1, replica_groups=mesh['z_high'=8,'z_low'=2,'y'=4,'head'=8] {'z_low','y'}, dimensions={0} | all-to-all | bytes 589824 | tf_op jit(solution)/shard_map/all_to_all | solution.py:293
  151.1 0.2 pass_merge.3
  151.3 25.2 %all_to_all.56.in_ref = f32[8,72,128]{2,1,0:T(8,128)S(1)} all-to-all(f32[8,72,128]{2,1,0:T(8,128)S(1)} %pass_merge.3), channel_id=1, replica_groups=mesh['z_high'=8,'z_low'=2,'y'=4,'head'=8] {'z_high'}, dimensions={0} | all-to-all | bytes 589824 | tf_op jit(solution)/shard_map/all_to_all | solution.py:293
  176.5 1.1 finish.3
  177.6 11.3 %all_to_all.57.in_ref = f32[8,8,128]{2,1,0:T(8,128)S(1)} all-to-all(f32[8,8,128]{2,1,0:T(8,128)S(1)} %finish.3), channel_id=1, replica_groups=mesh['z_high'=8,'z_low'=2,'y'=4,'head'=8] {'head'}, dimensions={0} | all-to-all | bytes 65536 | tf_op jit(solution)/shard_map/all_to_all | solution.py:293
  188.8 0.6 last.1
  (9 shorter events, 0.1 us)
Async XLA Ops:
  0.0 1.1 copy-start.4
  1.1 0.7 copy-start.6
  1.8 0.7 copy-start.7
  2.5 0.7 copy-start.9
  3.1 30.3 %copy-start.11 = (s32[4]{0:T(128)S(1)}, s32[4]{0:T(128)}, u32[]{:S(2)}) copy-start(s32[4]{0:T(128)} %param.17) | copy-start | bytes 52
  3.1 50.0 %copy-start.1 = (bf16[4,1024,1,128]{3,1,2,0:T(8,128)(2,1)S(1)}, bf16[4,1024,1,128]{3,1,2,0:T(8,128)(2,1)}, u32[]{:S(2)}) copy-start(bf16[4,1024,1,128]{3,1,2,0:T(8,128)(2,1)} %param.16) | copy-start | bytes 3145732
  4.7 1.0 copy-start.2
  5.7 47.5 %copy-start = (bf16[4,1024,1,128]{3,1,2,0:T(8,128)(2,1)S(1)}, bf16[4,1024,1,128]{3,1,2,0:T(8,128)(2,1)}, u32[]{:S(2)}) copy-start(bf16[4,1024,1,128]{3,1,2,0:T(8,128)(2,1)} %param.15) | copy-start | bytes 3145732
  19.3 33.8 %all-to-all-start.1 = ((f32[8,8,1280]{2,1,0:T(8,128)}), f32[8,8,1280]{2,1,0:T(8,128)S(1)}, u32[]{:S(2)}, u32[]{:S(2)}) async-start(f32[8,8,1280]{2,1,0:T(8,128)} %pass_sum.2), calls=%async_computation.1 | async-start | bytes 655360 | tf_op jit(solution)/shard_map/all_to_all | solution.py:293
  55.5 17.4 %copy-start.10 = (f32[256]{0:T(256)S(1)}, f32[256]{0:T(256)}, u32[]{:S(2)}) copy-start(f32[256]{0:T(256)} %param.14) | copy-start | bytes 3076
  66.1 25.3 %all-to-all-start.3 = ((f32[8,72,128]{2,1,0:T(8,128)}), f32[8,72,128]{2,1,0:T(8,128)S(1)}, u32[]{:S(2)}, u32[]{:S(2)}) async-start(f32[8,72,128]{2,1,0:T(8,128)} %pass_merge.2), calls=%async_computation.3 | async-start | bytes 589824 | tf_op jit(solution)/shard_map/all_to_all | solution.py:293
  72.9 1.0 copy-start.5
  74.0 32.1 %copy-start.8 = (f32[256]{0:T(256)S(1)}, f32[256]{0:T(256)}, u32[]{:S(2)}) copy-start(f32[256]{0:T(256)} %param.10) | copy-start | bytes 3076
  91.4 14.7 %copy-start.3 = (bf16[2304,256]{1,0:T(8,128)(2,1)S(1)}, bf16[2304,256]{1,0:T(8,128)(2,1)}, u32[]{:S(2)}) copy-start(bf16[2304,256]{1,0:T(8,128)(2,1)} %copy-done.2) | copy-start | bytes 3538948

commit v2 on v1

v2 whole, which is shorter than its diff:
```python
import functools
import math

import jax
import jax.numpy as jnp
from jax import lax
from jax.experimental import pallas as pl
from jax.experimental.pallas import tpu as pltpu
from jax.sharding import Mesh
from jax.sharding import PartitionSpec as P

HEAD_DIM = 128
GROUPS = 16
DECODE_STEPS = 2
NEAR = ("z_low", "y")
FAR = "z_high"
SEQ = (FAR, *NEAR)

CODE_NORM = 147.8
EPSILON = 1e-05
ROPE_BASE = 500000.0
SCORE_SCALE = HEAD_DIM ** (-0.5)

f32 = jnp.float32
bf16 = jnp.bfloat16
NT = (((1,), (1,)), ((), ()))


def iota(shape, axis):
    return lax.broadcasted_iota(jnp.int32, shape, axis)


def call(kernel, outs, name, arrays, scalars=()):
    specs = [pl.BlockSpec(memory_space=pltpu.SMEM) for _ in scalars]
    specs += [pl.BlockSpec(memory_space=pltpu.VMEM) for _ in arrays]
    return pl.pallas_call(
        kernel,
        out_shape=outs,
        in_specs=specs,
        name=name,
        compiler_params=pltpu.CompilerParams(vmem_limit_bytes=32 * 1024 * 1024),
    )(*scalars, *arrays)


def shape_of(shape, dtype=f32):
    return jax.ShapeDtypeStruct(shape, dtype)


def byte_sum(state):
    x = state * 34038481 + 76625530
    pairs = (x & 0x00FF00FF) + ((x >> 8) & 0x00FF00FF)
    total = (pairs + (pairs >> 16)) & 0x7FF
    return (total - 510).astype(f32)


def interleave():
    row = iota((128, 128), 0)
    column = iota((128, 128), 1)
    return (column == 4 * (row & 31) + (row >> 5)).astype(f32).astype(bf16)


def by_sequence():
    row = iota((64, 64), 0)
    column = iota((64, 64), 1)
    return (column == 4 * (row & 15) + (row >> 4)).astype(f32).astype(bf16)


def by_place():
    row = iota((32, 32), 0)
    column = iota((32, 32), 1)
    source = 8 * (row & 3) + (row & 4) + (row >> 3)
    return (column == source).astype(f32).astype(bf16)


def exact_product(x, ones):
    rows = x.shape[0]
    high = x.astype(bf16).astype(f32)
    rest = x - high
    middle = rest.astype(bf16).astype(f32)
    low = rest - middle
    parts = jnp.concatenate([high, middle, low], axis=0).astype(bf16)
    product = jnp.dot(parts, ones, preferred_element_type=f32)
    return product[:rows] + product[rows : 2 * rows] + product[2 * rows :]


def tile_of(x, k):
    return x[:, k * 128 : k * 128 + 128]


def send_halves(out_ref, halves):
    copies = out_ref.shape[0] // 2
    for s in range(2):
        for j in range(copies):
            for k in range(5):
                out_ref[s * copies + j, :, k * 128 : k * 128 + 128] = halves[s][k]


def project(hidden, gain, weights, out_ref):
    squares = jnp.sum(hidden * hidden, axis=1, keepdims=True)
    normed = (hidden * gain).astype(bf16)
    y = lax.dot_general(normed, weights, NT, preferred_element_type=f32)
    first = iota((8, 128), 0) < 4
    spread = jnp.broadcast_to(squares, (8, 128))
    halves = []
    for s in range(2):
        tiles = [
            jnp.where(first, tile_of(y, 8 * s + 2 * i), tile_of(y, 8 * s + 2 * i + 1))
            for i in range(4)
        ]
        halves.append(tiles + [jnp.where(first, tile_of(y, 16 + s), spread)])
    send_halves(out_ref, halves)


def decode_qkv_kernel(hidden_ref, gain_ref, codes_ref, scale_ref, w_ref, hid_ref, out_ref):
    lane = iota((32, 128), 1)
    word = iota((32, 128), 0)
    for tile in range(18):
        codes = codes_ref[tile * 32 : tile * 32 + 32, :]
        window = (codes << 16) | (pltpu.roll(codes, 31, 0) << 8) | pltpu.roll(codes, 30, 0)
        scales = jnp.broadcast_to(scale_ref[tile : tile + 1, :], (32, 128)) * (1.0 / CODE_NORM)
        for r in range(4):
            column = jnp.sum(
                jnp.where(lane == 4 * word + r, scales, 0.0), axis=1, keepdims=True
            )
            values = byte_sum((window >> (8 - 2 * r)) & 0xFFFF) * column
            at = tile * 128 + r * 32
            w_ref[at : at + 32, :] = values.astype(bf16)
    hidden = hidden_ref[...].astype(f32)
    hidden = jnp.concatenate([hidden, hidden], axis=0)
    hid_ref[...] = hidden
    project(hidden, gain_ref[...], w_ref[...], out_ref)


def decode_out_kernel(info_ref, codes_ref, scale_ref, other_ref, w_ref):
    s = info_ref[5]
    lane = iota((32, 128), 1)
    within = lane & 31
    for block in range(16):
        own = block < 8
        rows = slice(block % 8 * 32, block % 8 * 32 + 32)
        across = iota((32, 256), 1) == iota((32, 256), 0) + block % 8 * 32
        scale = scale_ref[...] if own else other_ref[256:257, :]
        scale = jnp.broadcast_to(scale, (32, 256)) * (1.0 / CODE_NORM)
        column = jnp.sum(jnp.where(across, scale, 0.0), axis=1, keepdims=True)
        for group in range(2):
            if own:
                codes = jnp.where(
                    s == 0,
                    codes_ref[rows, group * 128 : group * 128 + 128],
                    codes_ref[rows, group * 128 + 256 : group * 128 + 384],
                )
            else:
                codes = other_ref[rows, group * 128 : group * 128 + 128].astype(jnp.int32)
            second = jnp.where(within < 31, pltpu.roll(codes, 127, 1), pltpu.roll(codes, 31, 1))
            third = jnp.where(within < 30, pltpu.roll(codes, 126, 1), pltpu.roll(codes, 30, 1))
            window = (codes << 16) | (second << 8) | third
            for r in range(4):
                values = byte_sum((window >> (8 - 2 * r)) & 0xFFFF) * column
                at = group * 512 + r * 128
                w_ref[block * 32 : block * 32 + 32, at : at + 128] = values.astype(bf16)


def total_of(ref):
    total = ref[0]
    for j in range(1, ref.shape[0]):
        total = total + ref[j]
    return total


def pass_sum_kernel(in_ref, out_ref):
    total = total_of(in_ref)
    for j in range(out_ref.shape[0]):
        out_ref[j] = total


def merged(in_ref):
    parts = range(in_ref.shape[0])
    stats = [in_ref[j, :, 512:] for j in parts]
    top = functools.reduce(jnp.maximum, stats)
    factors = [jnp.exp(x - top) for x in stats]
    sums = stats[0] * pltpu.roll(factors[0], 4, 1)
    for j in parts[1:]:
        sums = sums + stats[j] * pltpu.roll(factors[j], 4, 1)
    accs = []
    for b in range(4):
        at = slice(b * 128, b * 128 + 128)
        acc = in_ref[0, :, at] * factors[0][:, b : b + 1]
        for j in parts[1:]:
            acc = acc + in_ref[j, :, at] * factors[j][:, b : b + 1]
        accs.append(acc)
    return top, sums, accs


def pass_merge_kernel(in_ref, out_ref):
    top, sums, accs = merged(in_ref)
    lane = iota((8, 128), 1)
    stats = jnp.where(lane < 4, top, jnp.where(lane < 8, sums, 0.0))
    for j in range(out_ref.shape[0]):
        for b in range(4):
            out_ref[j, :, b * 128 : b * 128 + 128] = accs[b]
        out_ref[j, :, 512:] = stats


def attend_kernel(features, earlier, info_ref, in_ref, cos_ref, sin_ref, keys_ref, values_ref,
                  *refs):
    out_ref, k_ref, v_ref = refs[2 * earlier :]
    first = iota((8, 128), 0) < 4
    last = in_ref[0, :, 512:]
    squares = jnp.where(first, pltpu.roll(last, 4, 0), last)
    rms = lax.rsqrt(squares / features + EPSILON)
    tiles = [tile_of(in_ref[s], i) * rms for s in range(2) for i in range(4)]
    tiles += [in_ref[s, :, 512:] * rms for s in range(2)]
    x = exact_product(jnp.concatenate(tiles, axis=0), interleave())
    cos = jnp.concatenate([cos_ref[...]] * 9, axis=0)
    sin = jnp.concatenate([sin_ref[...]] * 9, axis=0)
    turned = x[:72] * cos + pltpu.roll(x[:72], 64, 1) * sin
    turned = turned.astype(bf16)
    new_key = turned[64:72].astype(f32)
    new_value = x[72:].astype(bf16).astype(f32)
    k_ref[...] = new_key
    v_ref[...] = new_value
    queries = jnp.dot(by_sequence(), turned[:64], preferred_element_type=f32)
    new_keys = [refs[2 * u][...] for u in range(earlier)] + [new_key]
    new_values = [refs[2 * u + 1][...] for u in range(earlier)] + [new_value]
    owner = info_ref[4] == 0
    length = keys_ref.shape[1]
    place = iota((16, length), 1)
    lane = iota((8, 128), 1)
    halves = [[], []]
    stats = [jnp.zeros((8, 128), f32)] * 2
    for b in range(4):
        query = queries[b * 16 : b * 16 + 16]
        scores = lax.dot_general(
            query.astype(bf16), keys_ref[b], NT, preferred_element_type=f32
        ) * SCORE_SCALE
        live = place < info_ref[b]
        top = jnp.max(jnp.where(live, scores, -1e30), axis=1, keepdims=True)
        weights = jnp.where(live, jnp.exp(scores - top), 0.0)
        total = jnp.sum(weights, axis=1, keepdims=True)
        acc = jnp.dot(weights.astype(bf16), values_ref[b], preferred_element_type=f32)
        fresh = [
            jnp.where(
                owner,
                jnp.sum(query * key[b : b + 1, :], axis=1, keepdims=True) * SCORE_SCALE,
                -1e30,
            )
            for key in new_keys
        ]
        peak = functools.reduce(jnp.maximum, fresh, top)
        factor = jnp.exp(top - peak)
        total = total * factor
        acc = acc * factor
        for score, value in zip(fresh, new_values):
            weight = jnp.where(owner, jnp.exp(score - peak), 0.0)
            total = total + weight
            acc = acc + weight * value[b : b + 1, :]
        for s in range(2):
            rows = slice(8 * s, 8 * s + 8)
            halves[s].append(acc[rows])
            stats[s] = jnp.where(lane == b, peak[rows], stats[s])
            stats[s] = jnp.where(lane == 4 + b, total[rows], stats[s])
    send_halves(out_ref, [halves[s] + [stats[s]] for s in range(2)])


def finish_kernel(info_ref, in_ref, w_ref, out_ref):
    _, sums, accs = merged(in_ref)
    attended = jnp.concatenate(
        [accs[b] / sums[:, 4 + b : 5 + b] for b in range(4)], axis=0
    ).astype(bf16)
    attended = jnp.dot(by_place(), attended, preferred_element_type=f32).astype(bf16)
    attended = lax.dot_general(attended, interleave(), NT, preferred_element_type=f32)
    block = iota((8, 128), 1) >> 5
    chunks = []
    for r in range(4):
        chunk = jnp.zeros((8, 128), f32)
        for t in range(4):
            part = attended[t * 8 : t * 8 + 8]
            if t != r:
                part = pltpu.roll(part, (t - r) % 4 * 32, 1)
            chunk = jnp.where(block == t, part, chunk)
        chunks.append(chunk)
    columns = jnp.concatenate(chunks, axis=1)
    high = iota((8, 512), 0) >= 4
    columns = jnp.concatenate(
        [jnp.where(high, 0.0, columns), jnp.where(high, columns, 0.0)], axis=1
    ).astype(bf16)
    update = lax.dot_general(columns, w_ref[...], NT, preferred_element_type=f32)
    update = update + pltpu.roll(update, 4, 0)
    first = iota((8, 128), 0) < 4
    own = jnp.where(first, tile_of(update, 0), tile_of(update, 1))
    other = jnp.where(first, tile_of(update, 2), tile_of(update, 3))
    same = info_ref[5] == 0
    blocks = [jnp.where(same, own, other), jnp.where(same, other, own)]
    copies = out_ref.shape[0] // 2
    for s in range(2):
        for j in range(copies):
            out_ref[s * copies + j] = blocks[s]


def updated(in_ref, hid_ref):
    update = total_of(in_ref)
    turned = pltpu.roll(update, 4, 0)
    first = iota((8, 128), 0) < 4
    update = jnp.concatenate(
        [jnp.where(first, update, turned), jnp.where(first, turned, update)], axis=1
    )
    return (hid_ref[...] + update).astype(bf16)


def next_kernel(in_ref, hid_ref, gain_ref, w_ref, new_ref, out_ref):
    hidden = updated(in_ref, hid_ref).astype(f32)
    new_ref[...] = hidden
    project(hidden, gain_ref[...], w_ref[...], out_ref)


def last_kernel(in_ref, hid_ref, out_ref):
    out_ref[...] = updated(in_ref, hid_ref)[:4]


def exchange(value, axes):
    return lax.all_to_all(value, axes, split_axis=0, concat_axis=0, tiled=True)


def shards(features, hidden_in, norm_gain, qkv_codes, qkv_scale, out_codes, out_scale,
           cache_keys, cache_values, lengths):
    near = lax.axis_size(NEAR)
    far = lax.axis_size(FAR)
    heads = lax.axis_size("head")
    gain = norm_gain.reshape(1, -1)
    batch, block_len = cache_keys.shape[:2]
    keys = cache_keys.reshape(batch, block_len, HEAD_DIM)
    values = cache_values.reshape(batch, block_len, HEAD_DIM)
    place = lax.axis_index(SEQ)
    low = lax.axis_index("z_low")
    info = jnp.concatenate(
        [lengths - place * block_len, jnp.stack([place, low]).astype(jnp.int32)]
    )
    wanted = lax.dynamic_slice_in_dim(out_codes, (1 - low) * 256, 256, axis=1)
    wanted = jnp.concatenate(
        [wanted.astype(f32), jnp.broadcast_to(out_scale[None, :], (8, 256))], axis=0
    )
    other = lax.ppermute(wanted, "z_low", [(0, 1), (1, 0)])

    half_dim = HEAD_DIM // 2
    freqs = jnp.exp(
        -(jnp.arange(half_dim, dtype=f32) * (2.0 / HEAD_DIM)) * math.log(ROPE_BASE)
    )
    steps = jnp.arange(DECODE_STEPS, dtype=jnp.int32)
    positions = lengths[None, :] + steps[:, None]
    angles = positions.astype(f32)[:, :, None] * freqs
    cosines, sines = jnp.cos(angles), jnp.sin(angles)
    cosines = jnp.tile(jnp.concatenate([cosines, cosines], axis=-1), (1, 2, 1))
    sines = jnp.tile(jnp.concatenate([-sines, sines], axis=-1), (1, 2, 1))

    w_qkv, hidden, partial = call(
        decode_qkv_kernel,
        (shape_of((2304, 256), bf16), shape_of((8, 256)), shape_of((near, 8, 640))),
        "decode_qkv",
        (hidden_in, gain, qkv_codes.T, qkv_scale.reshape(18, 128)),
    )
    w_out = call(
        decode_out_kernel,
        shape_of((512, 1024), bf16),
        "decode_out",
        (out_codes, out_scale.reshape(1, -1), other),
        (info,),
    )
    fresh = ()
    for step in range(DECODE_STEPS):
        partial = exchange(partial, NEAR)
        partial = call(pass_sum_kernel, shape_of((far, 8, 640)), "sum_near", (partial,))
        partial = exchange(partial, FAR)
        partial = call(pass_sum_kernel, shape_of((2, 8, 640)), "sum_far", (partial,))
        partial = exchange(partial, "z_low")
        part, new_key, new_value = call(
            functools.partial(attend_kernel, features, step),
            (shape_of((near, 8, 640)), shape_of((8, 128)), shape_of((8, 128))),
            "attend",
            (partial, cosines[step], sines[step], keys, values, *fresh),
            (info,),
        )
        fresh += (new_key, new_value)
        part = exchange(part, NEAR)
        part = call(pass_merge_kernel, shape_of((far, 8, 640)), "merge_near", (part,))
        part = exchange(part, FAR)
        update = call(
            finish_kernel, shape_of((2 * heads, 8, 128)), "finish", (part, w_out), (info,)
        )
        update = exchange(update, ("z_low", "head"))
        if step + 1 < DECODE_STEPS:
            hidden, partial = call(
                next_kernel,
                (shape_of((8, 256)), shape_of((near, 8, 640))),
                "next_step",
                (update, hidden, gain, w_qkv),
            )
    return call(last_kernel, shape_of((4, 256), bf16), "last", (update, hidden))


def solution(mesh):
    seq, head = mesh.shape["seq"], mesh.shape["head"]
    far = seq // 8
    split = Mesh(mesh.devices.reshape(far, 2, 4, head), (*SEQ, "head"))
    placed = (
        P(None, SEQ),
        P(SEQ),
        P(SEQ, "head"),
        P("head"),
        P(SEQ, "head"),
        P(SEQ),
        P(None, SEQ, "head", None),
        P(None, SEQ, "head", None),
        P(),
    )

    def run(hidden_in, *others):
        features = hidden_in.shape[1]
        return jax.shard_map(
            functools.partial(shards, float(features)),
            mesh=split,
            in_specs=placed,
            out_specs=P(None, SEQ),
            check_vma=False,
        )(hidden_in, *others)

    return run
```

time: 190 us -> 184 us (0.968)
  blocking collectives: 115 us -> 99.4 us
  starting transfers between devices: 20.8 us -> 30.3 us
  waiting for transfers between devices: 35.7 us -> 31.4 us
  Pallas kernels: 12.4 us -> 15 us
    all_to_all x8, blocking collectives: 115 us -> 99.4 us  [exchange(): return lax.all_to_all(value, axes, split_axis=0, concat_axis=0, tiled=True)]
    all_to_all x2 -> x4, waiting for transfers between devices: 35.7 us -> 21.7 us  [exchange(): return lax.all_to_all(value, axes, split_axis=0, concat_axis=0, tiled=True)]
    ppermute x0 -> x1, waiting for transfers between devices: none -> 9.75 us  [shards(): other = lax.ppermute(wanted, 'z_low', [(0, 1), (1, 0)])]
    all_to_all x2 -> x4, starting transfers between devices: 20.8 us -> 28.1 us  [exchange(): return lax.all_to_all(value, axes, split_axis=0, concat_axis=0, tiled=True)]
    pallas_call x12 -> x14, Pallas kernels: 12.4 us -> 15 us  [call(): pl.pallas_call(kernel, out_shape=outs, in_specs=specs, name=name, compile...]
    ppermute x0 -> x1, starting transfers between devices: none -> 2.26 us  [shards(): other = lax.ppermute(wanted, 'z_low', [(0, 1), (1, 0)])]
  transfers between devices with their start and end apart: 2 -> 5, of which waited for: 2 -> 4; matrix products, arithmetic and copies ran while one was open for 0% -> 1% of each run, Pallas kernels for 1% -> 1%
where the time goes in v2:
time: 184 us; the launch traced here: 183 us
  blocking collectives  99.4 us (54%)
  waiting for transfers between devices  31.4 us (17%)
  starting transfers between devices  30.3 us (16%)
  Pallas kernels  15 us (8%)
  local copies, waits for them, and re-layouts  5.51 us (3%)
    all_to_all x8, blocking collectives, exchange(): return lax.all_to_all(value, axes, split_axis=0, concat_axis=0, tiled=True)  99.4 us
    all_to_all x4, starting transfers between devices, exchange(): return lax.all_to_all(value, axes, split_axis=0, concat_axis=0, tiled=True)  28.1 us
    all_to_all x4, waiting for transfers between devices, exchange(): return lax.all_to_all(value, axes, split_axis=0, concat_axis=0, tiled=True)  21.7 us
    pallas_call x14, Pallas kernels, call(): pl.pallas_call(kernel, out_shape=outs, in_specs=specs, name=name, compile...  15 us
    ppermute x1, waiting for transfers between devices, shards(): other = lax.ppermute(wanted, 'z_low', [(0, 1), (1, 0)])  9.75 us
    unnamed x24, local copies, waits for them, and re-layouts  5.5 us
  transfers between devices with their start and end apart: 5, of which 4 were waited for; matrix products, arithmetic and copies ran while one was open for 1% of the time, Pallas kernels for 1%

profile of v2, /device:TPU:1, one launch (start us, length us, event | category | flops | bytes accessed | tf_op | source)
XLA Modules:
  0.0 182.8 jit_solution(14807668873216564793)
XLA Ops:
  0.0 0.0 copy-start
  0.0 0.0 copy-start.5
  0.0 1.2 copy-done.5
  1.2 0.7 copy-done.6
  1.9 0.7 copy-done.8
  2.5 0.7 copy-done.10
  3.2 2.2 %decode_qkv.1 = (bf16[2304,256]{1,0:T(8,128)(2,1)S(1)}, f32[8,256]{1,0:T(8,128)S(1)}, f32[8,8,640]{2,1,0:T(8,128)}) custom-call(bf16[4,256]{1,0:T(4,128)(2,1)S(1)} %copy-done.10, f32[1,256]{1,0:T(1,128)S(1)} %bitcast.31, s32[576,256]{1,0:T(8,128)S(1)} %bitcast.24, f32[18,128]{1,0:T(8,128)S(1)} %bitcast.29), custom_call_target="tpu_custom_call" | custom-call | tf_op jit(solution)/shard_map/decode_qkv/pallas_call | solution.py:36
  5.4 6.4 %all-to-all-start = ((f32[8,8,640]{2,1,0:T(8,128)}), f32[8,8,640]{2,1,0:T(8,128)S(1)}, u32[]{:S(2)}, u32[]{:S(2)}) async-start(f32[8,8,640]{2,1,0:T(8,128)} %get-tuple-element.14), calls=%async_computation | async-start | bytes 327680 | tf_op jit(solution)/shard_map/all_to_all | solution.py:321
  11.8 0.7 add_convert_fusion
  12.5 4.9 %all-to-all-done.in_ref = f32[8,8,640]{2,1,0:T(8,128)S(1)} async-done(((f32[8,8,640]{2,1,0:T(8,128)}), f32[8,8,640]{2,1,0:T(8,128)S(1)}, u32[]{:S(2)}, u32[]{:S(2)}) %all-to-all-start) | async-done | bytes 163872 | tf_op jit(solution)/shard_map/all_to_all | solution.py:321
  17.4 0.7 sum_near.2
  18.1 13.9 %all-to-all-start.1 = ((f32[8,8,640]{2,1,0:T(8,128)}), f32[8,8,640]{2,1,0:T(8,128)S(1)}, u32[]{:S(2)}, u32[]{:S(2)}) async-start(f32[8,8,640]{2,1,0:T(8,128)} %sum_near.2), calls=%async_computation.1 | async-start | bytes 327680 | tf_op jit(solution)/shard_map/all_to_all | solution.py:321
  32.1 0.1 multiply_sine_fusion
  32.2 0.1 fusion.4
  32.3 0.0 copy-done.11
  32.3 14.0 %all-to-all-done.1.in_ref = f32[8,8,640]{2,1,0:T(8,128)S(1)} async-done(((f32[8,8,640]{2,1,0:T(8,128)}), f32[8,8,640]{2,1,0:T(8,128)S(1)}, u32[]{:S(2)}, u32[]{:S(2)}) %all-to-all-start.1) | async-done | bytes 163872 | tf_op jit(solution)/shard_map/all_to_all | solution.py:321
  46.2 0.6 sum_far.2
  46.9 3.3 %all-to-all-start.2 = ((f32[2,8,640]{2,1,0:T(8,128)}), f32[2,8,640]{2,1,0:T(8,128)S(1)}, u32[]{:S(2)}, u32[]{:S(2)}) async-start(f32[2,8,640]{2,1,0:T(8,128)} %sum_far.2), calls=%async_computation.2 | async-start | bytes 81920 | tf_op jit(solution)/shard_map/all_to_all | solution.py:321
  50.1 0.1 pad_add_fusion.info_ref
  50.2 2.7 %all-to-all-done.2.in_ref = f32[2,8,640]{2,1,0:T(8,128)S(1)} async-done(((f32[2,8,640]{2,1,0:T(8,128)}), f32[2,8,640]{2,1,0:T(8,128)S(1)}, u32[]{:S(2)}, u32[]{:S(2)}) %all-to-all-start.2) | async-done | bytes 40992 | tf_op jit(solution)/shard_map/all_to_all | solution.py:321
  53.0 0.0 copy-done
  53.0 1.2 copy-done.1
  54.2 2.2 %attend.2 = (f32[8,8,640]{2,1,0:T(8,128)S(1)}, f32[8,128]{1,0:T(8,128)S(1)}, f32[8,128]{1,0:T(8,128)S(1)}) custom-call(s32[6]{0:T(128)S(1)} %pad_add_fusion.info_ref, f32[2,8,640]{2,1,0:T(8,128)S(1)} %all-to-all-done.2.in_ref, f32[8,128]{1,0:T(8,128)S(1)} %bitcast.28, f32[8,128]{1,0:T(8,128)S(1)} %bitcast.27, bf16[4,1024,128]{2,1,0:T(8,128)(2,1)S(1)} %bitcast.20, ...), custom_call_target="tpu_custom_call" | custom-call | tf_op jit(solution)/shard_map/attend/pallas_call | solution.py:36
  56.4 8.1 %all_to_all.60.in_ref = f32[8,8,640]{2,1,0:T(8,128)S(1)} all-to-all(f32[8,8,640]{2,1,0:T(8,128)S(1)} %get-tuple-element.15), channel_id=1, replica_groups=mesh['z_high'=8,'z_low'=2,'y'=4,'head'=8] {'z_low','y'}, dimensions={0} | all-to-all | bytes 327680 | tf_op jit(solution)/shard_map/all_to_all | solution.py:321
  64.6 0.8 merge_near.2
  65.4 4.5 %all-to-all-start.4 = ((f32[8,8,640]{2,1,0:T(8,128)}), f32[8,8,640]{2,1,0:T(8,128)S(1)}, u32[]{:S(2)}, u32[]{:S(2)}) async-start(f32[8,8,640]{2,1,0:T(8,128)} %merge_near.2), calls=%async_computation.4 | async-start | bytes 327680 | tf_op jit(solution)/shard_map/all_to_all | solution.py:321
  69.9 0.0 copy-done.3
  69.9 0.0 copy-done.7
  70.0 2.3 %collective-permute-start = (f32[264,256]{1,0:T(8,128)S(1)}, f32[264,256]{1,0:T(8,128)S(1)}, u32[]{:S(2)}, u32[]{:S(2)}) collective-permute-start(f32[264,256]{1,0:T(8,128)S(1)} %pad_maximum_fusion), channel_id=1, source_target_pairs={{0,32},{32,0},{1,33},{33,1},{2,34},{34,2},{3,35},{35,3},{4,36},{36... | collective-permute-start | bytes 811016 | tf_op jit(solution)/shard_map/ppermute | solution.py:342
  72.2 9.8 %collective-permute-done.other_ref = f32[264,256]{1,0:T(8,128)S(1)} collective-permute-done((f32[264,256]{1,0:T(8,128)S(1)}, f32[264,256]{1,0:T(8,128)S(1)}, u32[]{:S(2)}, u32[]{:S(2)}) %collective-permute-start) | collective-permute-done | bytes 270368 | tf_op jit(solution)/shard_map/ppermute | solution.py:342
  82.0 1.0 copy-done.4
  83.0 1.9 %decode_out.1.w_ref = bf16[512,1024]{1,0:T(8,128)(2,1)S(1)} custom-call(s32[6]{0:T(128)S(1)} %pad_add_fusion.info_ref, s32[256,512]{1,0:T(8,128)S(1)} %copy-done.4, f32[1,256]{1,0:T(1,128)S(1)} %bitcast.30, f32[264,256]{1,0:T(8,128)S(1)} %collective-permute-done.other_ref), custom_call_target="tpu_custom_call" | custom-call | tf_op jit(solution)/shard_map/decode_out/pallas_call | solution.py:36
  84.9 0.0 all-to-all-done.4.in_ref
  84.9 1.3 finish.2
  86.3 16.8 %all_to_all.61.in_ref = f32[16,8,128]{2,1,0:T(8,128)S(1)} all-to-all(f32[16,8,128]{2,1,0:T(8,128)S(1)} %finish.2), channel_id=1, replica_groups=mesh['z_high'=8,'z_low'=2,'y'=4,'head'=8] {'z_low','head'}, dimensions={0} | all-to-all | bytes 131072 | tf_op jit(solution)/shard_map/all_to_all | solution.py:321
  103.1 0.0 copy-done.9
  103.1 0.4 next_step.1
  103.5 8.1 %all_to_all.62.in_ref = f32[8,8,640]{2,1,0:T(8,128)S(1)} all-to-all(f32[8,8,640]{2,1,0:T(8,128)S(1)} %get-tuple-element.18), channel_id=1, replica_groups=mesh['z_high'=8,'z_low'=2,'y'=4,'head'=8] {'z_low','y'}, dimensions={0} | all-to-all | bytes 327680 | tf_op jit(solution)/shard_map/all_to_all | solution.py:321
  111.6 20.7 %all_to_all.63.in_ref = f32[8,8,640]{2,1,0:T(8,128)S(1)} all-to-all(f32[8,8,640]{2,1,0:T(8,128)S(1)} %sum_near.3), channel_id=1, replica_groups=mesh['z_high'=8,'z_low'=2,'y'=4,'head'=8] {'z_high'}, dimensions={0} | all-to-all | bytes 327680 | tf_op jit(solution)/shard_map/all_to_all | solution.py:321
  132.4 5.2 %all_to_all.64.in_ref = f32[2,8,640]{2,1,0:T(8,128)S(1)} all-to-all(f32[2,8,640]{2,1,0:T(8,128)S(1)} %sum_far.3), channel_id=1, replica_groups=mesh['z_high'=8,'z_low'=2,'y'=4,'head'=8] {'z_low'}, dimensions={0} | all-to-all | bytes 81920 | tf_op jit(solution)/shard_map/all_to_all | solution.py:321
  137.6 0.0 copy-done.2
  137.6 2.7 %attend.3 = (f32[8,8,640]{2,1,0:T(8,128)S(1)}, f32[8,128]{1,0:T(8,128)}, f32[8,128]{1,0:T(8,128)}) custom-call(s32[6]{0:T(128)S(1)} %pad_add_fusion.info_ref, f32[2,8,640]{2,1,0:T(8,128)S(1)} %all_to_all.64.in_ref, f32[8,128]{1,0:T(8,128)S(1)} %bitcast.26, f32[8,128]{1,0:T(8,128)S(1)} %bitcast.25, bf16[4,1024,128]{2,1,0:T(8,128)(2,1)S(1)} %bitcast.21, ...), custom_call_target="tpu_custom_call" | custom-call | tf_op jit(solution)/shard_map/attend/pallas_call | solution.py:36
  140.3 8.0 %all_to_all.65.in_ref = f32[8,8,640]{2,1,0:T(8,128)S(1)} all-to-all(f32[8,8,640]{2,1,0:T(8,128)S(1)} %get-tuple-element.21), channel_id=1, replica_groups=mesh['z_high'=8,'z_low'=2,'y'=4,'head'=8] {'z_low','y'}, dimensions={0} | all-to-all | bytes 327680 | tf_op jit(solution)/shard_map/all_to_all | solution.py:321
  148.2 0.1 merge_near.3
  148.4 19.1 %all_to_all.66.in_ref = f32[8,8,640]{2,1,0:T(8,128)S(1)} all-to-all(f32[8,8,640]{2,1,0:T(8,128)S(1)} %merge_near.3), channel_id=1, replica_groups=mesh['z_high'=8,'z_low'=2,'y'=4,'head'=8] {'z_high'}, dimensions={0} | all-to-all | bytes 327680 | tf_op jit(solution)/shard_map/all_to_all | solution.py:321
  167.5 1.3 finish.3
  168.8 13.3 %all_to_all.67.in_ref = f32[16,8,128]{2,1,0:T(8,128)S(1)} all-to-all(f32[16,8,128]{2,1,0:T(8,128)S(1)} %finish.3), channel_id=1, replica_groups=mesh['z_high'=8,'z_low'=2,'y'=4,'head'=8] {'z_low','head'}, dimensions={0} | all-to-all | bytes 131072 | tf_op jit(solution)/shard_map/all_to_all | solution.py:321
  182.2 0.6 last.1
  (21 shorter events, 0.1 us)
Async XLA Ops:
  0.0 53.0 %copy-start = (bf16[4,1024,1,128]{3,1,2,0:T(8,128)(2,1)S(1)}, bf16[4,1024,1,128]{3,1,2,0:T(8,128)(2,1)}, u32[]{:S(2)}) copy-start(bf16[4,1024,1,128]{3,1,2,0:T(8,128)(2,1)} %param.15) | copy-start | bytes 3145732
  0.0 1.2 copy-start.5
  1.2 0.7 copy-start.6
  1.9 0.7 copy-start.8
  2.5 0.7 copy-start.10
  3.2 29.0 %copy-start.11 = (s32[4]{0:T(128)S(1)}, s32[4]{0:T(128)}, u32[]{:S(2)}) copy-start(s32[4]{0:T(128)} %param.17) | copy-start | bytes 52
  5.4 12.0 %all-to-all-start = ((f32[8,8,640]{2,1,0:T(8,128)}), f32[8,8,640]{2,1,0:T(8,128)S(1)}, u32[]{:S(2)}, u32[]{:S(2)}) async-start(f32[8,8,640]{2,1,0:T(8,128)} %get-tuple-element.14), calls=%async_computation | async-start | bytes 327680 | tf_op jit(solution)/shard_map/all_to_all | solution.py:321
  18.1 28.1 %all-to-all-start.1 = ((f32[8,8,640]{2,1,0:T(8,128)}), f32[8,8,640]{2,1,0:T(8,128)S(1)}, u32[]{:S(2)}, u32[]{:S(2)}) async-start(f32[8,8,640]{2,1,0:T(8,128)} %sum_near.2), calls=%async_computation.1 | async-start | bytes 327680 | tf_op jit(solution)/shard_map/all_to_all | solution.py:321
  46.9 6.1 %all-to-all-start.2 = ((f32[2,8,640]{2,1,0:T(8,128)}), f32[2,8,640]{2,1,0:T(8,128)S(1)}, u32[]{:S(2)}, u32[]{:S(2)}) async-start(f32[2,8,640]{2,1,0:T(8,128)} %sum_far.2), calls=%async_computation.2 | async-start | bytes 81920 | tf_op jit(solution)/shard_map/all_to_all | solution.py:321
  53.0 1.2 copy-start.1
  54.2 15.7 %copy-start.3 = (s32[256,512]{1,0:T(8,128)S(1)}, s32[256,512]{1,0:T(8,128)}, u32[]{:S(2)}) copy-start(s32[256,512]{1,0:T(8,128)} %codes_ref.1) | copy-start | bytes 1572868
  56.4 13.5 %copy-start.7 = (f32[256]{0:T(256)S(1)}, f32[256]{0:T(256)}, u32[]{:S(2)}) copy-start(f32[256]{0:T(256)} %param.14) | copy-start | bytes 3076
  65.4 19.5 %all-to-all-start.4 = ((f32[8,8,640]{2,1,0:T(8,128)}), f32[8,8,640]{2,1,0:T(8,128)S(1)}, u32[]{:S(2)}, u32[]{:S(2)}) async-start(f32[8,8,640]{2,1,0:T(8,128)} %merge_near.2), calls=%async_computation.4 | async-start | bytes 327680 | tf_op jit(solution)/shard_map/all_to_all | solution.py:321
  70.0 12.0 %collective-permute-start = (f32[264,256]{1,0:T(8,128)S(1)}, f32[264,256]{1,0:T(8,128)S(1)}, u32[]{:S(2)}, u32[]{:S(2)}) collective-permute-start(f32[264,256]{1,0:T(8,128)S(1)} %pad_maximum_fusion), channel_id=1, source_target_pairs={{0,32},{32,0},{1,33},{33,1},{2,34},{34,2},{3,35},{35,3},{4,36},{36... | collective-permute-start | bytes 811016 | tf_op jit(solution)/shard_map/ppermute | solution.py:342
  82.0 1.0 copy-start.4
  83.0 20.0 %copy-start.9 = (f32[256]{0:T(256)S(1)}, f32[256]{0:T(256)}, u32[]{:S(2)}) copy-start(f32[256]{0:T(256)} %param.10) | copy-start | bytes 3076
  103.1 34.5 %copy-start.2 = (bf16[4,1024,1,128]{3,1,2,0:T(8,128)(2,1)S(1)}, bf16[4,1024,1,128]{3,1,2,0:T(8,128)(2,1)}, u32[]{:S(2)}) copy-start(bf16[4,1024,1,128]{3,1,2,0:T(8,128)(2,1)} %param.16) | copy-start | bytes 3145732

commit v3 on v2

--- a/solution.py
+++ b/solution.py
@@ -30,16 +30,19 @@
     return lax.broadcasted_iota(jnp.int32, shape, axis)
 
 
-def call(kernel, outs, name, arrays, scalars=()):
+def call(kernel, outs, name, arrays, scalars=(), remote=(), scratch=()):
     specs = [pl.BlockSpec(memory_space=pltpu.SMEM) for _ in scalars]
+    specs += [pl.BlockSpec(memory_space=pltpu.HBM) for _ in remote]
     specs += [pl.BlockSpec(memory_space=pltpu.VMEM) for _ in arrays]
+    remote = [pltpu.with_memory_space_constraint(x, pltpu.HBM) for x in remote]
     return pl.pallas_call(
         kernel,
         out_shape=outs,
         in_specs=specs,
+        scratch_shapes=scratch,
         name=name,
-        compiler_params=pltpu.CompilerParams(vmem_limit_bytes=32 * 1024 * 1024),
-    )(*scalars, *arrays)
+        compiler_params=pltpu.CompilerParams(vmem_limit_bytes=16 * 1024 * 1024),
+    )(*scalars, *remote, *arrays)
 
 
 def shape_of(shape, dtype=f32):
@@ -111,10 +114,28 @@
     send_halves(out_ref, halves)
 
 
-def decode_qkv_kernel(hidden_ref, gain_ref, codes_ref, scale_ref, w_ref, hid_ref, out_ref):
+def decode_qkv_kernel(codes_hbm, scale_hbm, gain_hbm, hidden_ref, w_ref, hid_ref, out_ref,
+                      codes_ref, scale_ref, gain_ref, code_sems, scale_sem, gain_sem):
+    chunks = code_sems.shape[0]
+    chunk_rows = codes_ref.shape[0] // chunks
+    copies = []
+    for i in range(chunks):
+        rows = pl.ds(i * chunk_rows, chunk_rows)
+        copies.append(
+            pltpu.make_async_copy(codes_hbm.at[rows], codes_ref.at[rows], code_sems.at[i])
+        )
+    scale_copy = pltpu.make_async_copy(scale_hbm, scale_ref, scale_sem)
+    gain_copy = pltpu.make_async_copy(gain_hbm, gain_ref, gain_sem)
+    scale_copy.start()
+    for copy in copies:
+        copy.start()
+    gain_copy.start()
+    scale_copy.wait()
     lane = iota((32, 128), 1)
     word = iota((32, 128), 0)
     for tile in range(18):
+        if tile * 32 % chunk_rows == 0:
+            copies[tile * 32 // chunk_rows].wait()
         codes = codes_ref[tile * 32 : tile * 32 + 32, :]
         window = (codes << 16) | (pltpu.roll(codes, 31, 0) << 8) | pltpu.roll(codes, 30, 0)
         scales = jnp.broadcast_to(scale_ref[tile : tile + 1, :], (32, 128)) * (1.0 / CODE_NORM)
@@ -128,6 +149,7 @@
     hidden = hidden_ref[...].astype(f32)
     hidden = jnp.concatenate([hidden, hidden], axis=0)
     hid_ref[...] = hidden
+    gain_copy.wait()
     project(hidden, gain_ref[...], w_ref[...], out_ref)
 
 
@@ -201,9 +223,19 @@
         out_ref[j, :, 512:] = stats
 
 
-def attend_kernel(features, earlier, info_ref, in_ref, cos_ref, sin_ref, keys_ref, values_ref,
+def attend_kernel(features, earlier, info_ref, keys_hbm, values_hbm, in_ref, cos_ref, sin_ref,
                   *refs):
-    out_ref, k_ref, v_ref = refs[2 * earlier :]
+    out_ref, k_ref, v_ref, keys_ref, values_ref, key_sems, value_sems = refs[2 * earlier :]
+    key_copies = [
+        pltpu.make_async_copy(keys_hbm.at[b], keys_ref.at[b], key_sems.at[b]) for b in range(4)
+    ]
+    value_copies = [
+        pltpu.make_async_copy(values_hbm.at[b], values_ref.at[b], value_sems.at[b])
+        for b in range(4)
+    ]
+    for b in range(4):
+        key_copies[b].start()
+        value_copies[b].start()
     first = iota((8, 128), 0) < 4
     last = in_ref[0, :, 512:]
     squares = jnp.where(first, pltpu.roll(last, 4, 0), last)
@@ -211,8 +243,8 @@
     tiles = [tile_of(in_ref[s], i) * rms for s in range(2) for i in range(4)]
     tiles += [in_ref[s, :, 512:] * rms for s in range(2)]
     x = exact_product(jnp.concatenate(tiles, axis=0), interleave())
-    cos = jnp.concatenate([cos_ref[...]] * 9, axis=0)
-    sin = jnp.concatenate([sin_ref[...]] * 9, axis=0)
+    cos = jnp.concatenate([cos_ref[...]] * 18, axis=0)
+    sin = jnp.concatenate([sin_ref[...]] * 18, axis=0)
     turned = x[:72] * cos + pltpu.roll(x[:72], 64, 1) * sin
     turned = turned.astype(bf16)
     new_key = turned[64:72].astype(f32)
@@ -230,6 +262,7 @@
     stats = [jnp.zeros((8, 128), f32)] * 2
     for b in range(4):
         query = queries[b * 16 : b * 16 + 16]
+        key_copies[b].wait()
         scores = lax.dot_general(
             query.astype(bf16), keys_ref[b], NT, preferred_element_type=f32
         ) * SCORE_SCALE
@@ -237,6 +270,7 @@
         top = jnp.max(jnp.where(live, scores, -1e30), axis=1, keepdims=True)
         weights = jnp.where(live, jnp.exp(scores - top), 0.0)
         total = jnp.sum(weights, axis=1, keepdims=True)
+        value_copies[b].wait()
         acc = jnp.dot(weights.astype(bf16), values_ref[b], preferred_element_type=f32)
         fresh = [
             jnp.where(
@@ -349,25 +383,36 @@
     positions = lengths[None, :] + steps[:, None]
     angles = positions.astype(f32)[:, :, None] * freqs
     cosines, sines = jnp.cos(angles), jnp.sin(angles)
-    cosines = jnp.tile(jnp.concatenate([cosines, cosines], axis=-1), (1, 2, 1))
-    sines = jnp.tile(jnp.concatenate([-sines, sines], axis=-1), (1, 2, 1))
+    cosines = jnp.concatenate([cosines, cosines], axis=-1)
+    sines = jnp.concatenate([-sines, sines], axis=-1)
 
     w_qkv, hidden, partial = call(
         decode_qkv_kernel,
         (shape_of((2304, 256), bf16), shape_of((8, 256)), shape_of((near, 8, 640))),
         "decode_qkv",
-        (hidden_in, gain, qkv_codes.T, qkv_scale.reshape(18, 128)),
-    )
-    w_out = call(
-        decode_out_kernel,
-        shape_of((512, 1024), bf16),
-        "decode_out",
-        (out_codes, out_scale.reshape(1, -1), other),
-        (info,),
+        (hidden_in,),
+        remote=(qkv_codes.T, qkv_scale.reshape(18, 128), gain),
+        scratch=(
+            pltpu.VMEM((576, 256), jnp.int32),
+            pltpu.VMEM((18, 128), f32),
+            pltpu.VMEM((1, 256), f32),
+            pltpu.SemaphoreType.DMA((6,)),
+            pltpu.SemaphoreType.DMA,
+            pltpu.SemaphoreType.DMA,
+        ),
     )
     fresh = ()
     for step in range(DECODE_STEPS):
         partial = exchange(partial, NEAR)
+        if step == 0:
+            partial, other = lax.optimization_barrier((partial, other))
+            w_out = call(
+                decode_out_kernel,
+                shape_of((512, 1024), bf16),
+                "decode_out",
+                (out_codes, out_scale.reshape(1, -1), other),
+                (info,),
+            )
         partial = call(pass_sum_kernel, shape_of((far, 8, 640)), "sum_near", (partial,))
         partial = exchange(partial, FAR)
         partial = call(pass_sum_kernel, shape_of((2, 8, 640)), "sum_far", (partial,))
@@ -376,8 +421,15 @@
             functools.partial(attend_kernel, features, step),
             (shape_of((near, 8, 640)), shape_of((8, 128)), shape_of((8, 128))),
             "attend",
-            (partial, cosines[step], sines[step], keys, values, *fresh),
+            (partial, cosines[step], sines[step], *fresh),
             (info,),
+            (keys, values),
+            (
+                pltpu.VMEM(keys.shape, bf16),
+                pltpu.VMEM(keys.shape, bf16),
+                pltpu.SemaphoreType.DMA((4,)),
+                pltpu.SemaphoreType.DMA((4,)),
+            ),
         )
         fresh += (new_key, new_value)
         part = exchange(part, NEAR)

time: 184 us -> 185 us (level)
  local copies, waits for them, and re-layouts: 5.51 us -> 0.73 us
  Pallas kernels: 15 us -> 19.6 us
    all_to_all x4, waiting for transfers between devices: 21.7 us -> 28.1 us  [exchange(): return lax.all_to_all(value, axes, split_axis=0, concat_axis=0, tiled=True)]
    unnamed x24 -> x10, local copies, waits for them, and re-layouts: 5.5 us -> 0.72 us
    ppermute x1, waiting for transfers between devices: 9.75 us -> 4.98 us  [shards(): other = lax.ppermute(wanted, 'z_low', [(0, 1), (1, 0)])]
    pallas_call x14, Pallas kernels: 15 us -> 19.6 us  [call(): pl.pallas_call(kernel, out_shape=outs, in_specs=specs, scratch_shapes=scr...]
where the time goes in v3:
time: 185 us; the launch traced here: 184 us
  blocking collectives  98 us (53%)
  waiting for transfers between devices  33.1 us (18%)
  starting transfers between devices  31.2 us (17%)
  Pallas kernels  19.6 us (11%)
    all_to_all x8, blocking collectives, exchange(): return lax.all_to_all(value, axes, split_axis=0, concat_axis=0, tiled=True)  98 us
    all_to_all x4, waiting for transfers between devices, exchange(): return lax.all_to_all(value, axes, split_axis=0, concat_axis=0, tiled=True)  28.1 us
    all_to_all x4, starting transfers between devices, exchange(): return lax.all_to_all(value, axes, split_axis=0, concat_axis=0, tiled=True)  27.8 us
    pallas_call x14, Pallas kernels, call(): pl.pallas_call(kernel, out_shape=outs, in_specs=specs, scratch_shapes=scr...  19.6 us
    ppermute x1, waiting for transfers between devices, shards(): other = lax.ppermute(wanted, 'z_low', [(0, 1), (1, 0)])  4.98 us
  transfers between devices with their start and end apart: 5, of which 4 were waited for; matrix products, arithmetic and copies ran while one was open for 1% of the time, Pallas kernels for 1%

profile of v3, /device:TPU:1, one launch (start us, length us, event | category | flops | bytes accessed | tf_op | source)
XLA Modules:
  0.0 184.1 jit_solution(13339123459641443475)
XLA Ops:
  0.0 0.0 copy-start.1
  0.0 0.0 copy-start.4
  0.0 0.0 copy-start.3
  0.0 0.7 copy-done.3
  0.7 3.5 %decode_qkv.1 = (bf16[2304,256]{1,0:T(8,128)(2,1)S(1)}, f32[8,256]{1,0:T(8,128)S(1)}, f32[8,8,640]{2,1,0:T(8,128)}) custom-call(s32[576,256]{1,0:T(8,128)} %bitcast.23, f32[18,128]{1,0:T(8,128)} %bitcast.24, f32[1,256]{1,0:T(1,128)} %bitcast.17, bf16[4,256]{1,0:T(4,128)(2,1)S(1)} %copy-done.3), custom_call_target="tpu_custom_call" | custom-call | tf_op jit(solution)/shard_map/decode_qkv/pallas_call | solution.py:38
  4.2 6.4 %all-to-all-start = ((f32[8,8,640]{2,1,0:T(8,128)}), f32[8,8,640]{2,1,0:T(8,128)S(1)}, u32[]{:S(2)}, u32[]{:S(2)}) async-start(f32[8,8,640]{2,1,0:T(8,128)} %get-tuple-element.16), calls=%async_computation | async-start | bytes 327680 | tf_op jit(solution)/shard_map/all_to_all | solution.py:355
  10.6 1.0 dynamic-slice_convert_fusion
  11.6 0.0 copy-done.1
  11.6 3.4 %collective-permute-start = (f32[264,256]{1,0:T(8,128)S(1)}, f32[264,256]{1,0:T(8,128)S(1)}, u32[]{:S(2)}, u32[]{:S(2)}) collective-permute-start(f32[264,256]{1,0:T(8,128)S(1)} %pad_maximum_fusion), channel_id=1, source_target_pairs={{0,32},{32,0},{1,33},{33,1},{2,34},{34,2},{3,35},{35,3},{4,36},{36... | collective-permute-start | bytes 811016 | tf_op jit(solution)/shard_map/ppermute | solution.py:376
  15.0 0.0 copy-done.4
  15.0 5.0 %collective-permute-done.other_ref = f32[264,256]{1,0:T(8,128)S(1)} collective-permute-done((f32[264,256]{1,0:T(8,128)S(1)}, f32[264,256]{1,0:T(8,128)S(1)}, u32[]{:S(2)}, u32[]{:S(2)}) %collective-permute-start) | collective-permute-done | bytes 270368 | tf_op jit(solution)/shard_map/ppermute | solution.py:376
  20.0 0.0 all-to-all-done.in_ref
  20.0 0.7 sum_near.2
  20.7 14.5 %all-to-all-start.1 = ((f32[8,8,640]{2,1,0:T(8,128)}), f32[8,8,640]{2,1,0:T(8,128)S(1)}, u32[]{:S(2)}, u32[]{:S(2)}) async-start(f32[8,8,640]{2,1,0:T(8,128)} %sum_near.2), calls=%async_computation.1 | async-start | bytes 327680 | tf_op jit(solution)/shard_map/all_to_all | solution.py:355
  35.2 0.1 multiply_sine_fusion
  35.3 0.1 fusion.4
  35.4 13.5 %all-to-all-done.1.in_ref = f32[8,8,640]{2,1,0:T(8,128)S(1)} async-done(((f32[8,8,640]{2,1,0:T(8,128)}), f32[8,8,640]{2,1,0:T(8,128)S(1)}, u32[]{:S(2)}, u32[]{:S(2)}) %all-to-all-start.1) | async-done | bytes 163872 | tf_op jit(solution)/shard_map/all_to_all | solution.py:355
  48.9 0.6 sum_far.2
  49.5 3.3 %all-to-all-start.2 = ((f32[2,8,640]{2,1,0:T(8,128)}), f32[2,8,640]{2,1,0:T(8,128)S(1)}, u32[]{:S(2)}, u32[]{:S(2)}) async-start(f32[2,8,640]{2,1,0:T(8,128)} %sum_far.2), calls=%async_computation.2 | async-start | bytes 81920 | tf_op jit(solution)/shard_map/all_to_all | solution.py:355
  52.8 0.1 pad_add_fusion.info_ref
  52.9 2.7 %all-to-all-done.2.in_ref = f32[2,8,640]{2,1,0:T(8,128)S(1)} async-done(((f32[2,8,640]{2,1,0:T(8,128)}), f32[2,8,640]{2,1,0:T(8,128)S(1)}, u32[]{:S(2)}, u32[]{:S(2)}) %all-to-all-start.2) | async-done | bytes 40992 | tf_op jit(solution)/shard_map/all_to_all | solution.py:355
  55.6 0.0 copy-start
  55.6 4.0 %attend.2 = (f32[8,8,640]{2,1,0:T(8,128)S(1)}, f32[8,128]{1,0:T(8,128)S(1)}, f32[8,128]{1,0:T(8,128)S(1)}) custom-call(s32[6]{0:T(128)S(1)} %pad_add_fusion.info_ref, bf16[4,1024,128]{2,1,0:T(8,128)(2,1)} %bitcast.19, bf16[4,1024,128]{2,1,0:T(8,128)(2,1)} %bitcast.21, f32[2,8,640]{2,1,0:T(8,128)S(1)} %all-to-all-done.2.in_ref, ...), custom_call_target="tpu_custom_call" | custom-call | tf_op jit(solution)/shard_map/attend/pallas_call | solution.py:38
  59.7 9.8 %all_to_all.60.in_ref = f32[8,8,640]{2,1,0:T(8,128)S(1)} all-to-all(f32[8,8,640]{2,1,0:T(8,128)S(1)} %get-tuple-element.18), channel_id=1, replica_groups=mesh['z_high'=8,'z_low'=2,'y'=4,'head'=8] {'z_low','y'}, dimensions={0} | all-to-all | bytes 327680 | tf_op jit(solution)/shard_map/all_to_all | solution.py:355
  69.5 0.8 merge_near.2
  70.3 3.7 %all-to-all-start.4 = ((f32[8,8,640]{2,1,0:T(8,128)}), f32[8,8,640]{2,1,0:T(8,128)S(1)}, u32[]{:S(2)}, u32[]{:S(2)}) async-start(f32[8,8,640]{2,1,0:T(8,128)} %merge_near.2), calls=%async_computation.4 | async-start | bytes 327680 | tf_op jit(solution)/shard_map/all_to_all | solution.py:355
  74.0 0.0 copy-done
  74.0 0.0 copy-start.2
  74.0 1.9 %decode_out.1.w_ref = bf16[512,1024]{1,0:T(8,128)(2,1)S(1)} custom-call(s32[6]{0:T(128)S(1)} %pad_add_fusion.info_ref, s32[256,512]{1,0:T(8,128)S(1)} %copy-done, f32[1,256]{1,0:T(1,128)S(1)} %bitcast.16, f32[264,256]{1,0:T(8,128)S(1)} %collective-permute-done.other_ref), custom_call_target="tpu_custom_call" | custom-call | tf_op jit(solution)/shard_map/decode_out/pallas_call | solution.py:38
  75.8 11.9 %all-to-all-done.4.in_ref = f32[8,8,640]{2,1,0:T(8,128)S(1)} async-done(((f32[8,8,640]{2,1,0:T(8,128)}), f32[8,8,640]{2,1,0:T(8,128)S(1)}, u32[]{:S(2)}, u32[]{:S(2)}) %all-to-all-start.4) | async-done | bytes 163872 | tf_op jit(solution)/shard_map/all_to_all | solution.py:355
  87.7 1.3 finish.2
  89.0 18.1 %all_to_all.61.in_ref = f32[16,8,128]{2,1,0:T(8,128)S(1)} all-to-all(f32[16,8,128]{2,1,0:T(8,128)S(1)} %finish.2), channel_id=1, replica_groups=mesh['z_high'=8,'z_low'=2,'y'=4,'head'=8] {'z_low','head'}, dimensions={0} | all-to-all | bytes 131072 | tf_op jit(solution)/shard_map/all_to_all | solution.py:355
  107.2 0.0 copy-done.2
  107.2 0.4 next_step.1
  107.6 8.1 %all_to_all.62.in_ref = f32[8,8,640]{2,1,0:T(8,128)S(1)} all-to-all(f32[8,8,640]{2,1,0:T(8,128)S(1)} %get-tuple-element.22), channel_id=1, replica_groups=mesh['z_high'=8,'z_low'=2,'y'=4,'head'=8] {'z_low','y'}, dimensions={0} | all-to-all | bytes 327680 | tf_op jit(solution)/shard_map/all_to_all | solution.py:355
  115.7 15.9 %all_to_all.63.in_ref = f32[8,8,640]{2,1,0:T(8,128)S(1)} all-to-all(f32[8,8,640]{2,1,0:T(8,128)S(1)} %sum_near.3), channel_id=1, replica_groups=mesh['z_high'=8,'z_low'=2,'y'=4,'head'=8] {'z_high'}, dimensions={0} | all-to-all | bytes 327680 | tf_op jit(solution)/shard_map/all_to_all | solution.py:355
  131.6 5.2 %all_to_all.64.in_ref = f32[2,8,640]{2,1,0:T(8,128)S(1)} all-to-all(f32[2,8,640]{2,1,0:T(8,128)S(1)} %sum_far.3), channel_id=1, replica_groups=mesh['z_high'=8,'z_low'=2,'y'=4,'head'=8] {'z_low'}, dimensions={0} | all-to-all | bytes 81920 | tf_op jit(solution)/shard_map/all_to_all | solution.py:355
  136.8 4.3 %attend.3 = (f32[8,8,640]{2,1,0:T(8,128)S(1)}, f32[8,128]{1,0:T(8,128)}, f32[8,128]{1,0:T(8,128)}) custom-call(s32[6]{0:T(128)S(1)} %pad_add_fusion.info_ref, bf16[4,1024,128]{2,1,0:T(8,128)(2,1)} %bitcast.20, bf16[4,1024,128]{2,1,0:T(8,128)(2,1)} %bitcast.22, f32[2,8,640]{2,1,0:T(8,128)S(1)} %all_to_all.64.in_ref, f32[4,128]{1,0:T(4,128)S(1)} %get-tuple-element.35.cos_ref, ...), custom_call_target="tpu_custom_call" | custom-call | tf_op jit(solution)/shard_map/attend/pallas_call | solution.py:38
  141.1 8.2 %all_to_all.65.in_ref = f32[8,8,640]{2,1,0:T(8,128)S(1)} all-to-all(f32[8,8,640]{2,1,0:T(8,128)S(1)} %get-tuple-element.25), channel_id=1, replica_groups=mesh['z_high'=8,'z_low'=2,'y'=4,'head'=8] {'z_low','y'}, dimensions={0} | all-to-all | bytes 327680 | tf_op jit(solution)/shard_map/all_to_all | solution.py:355
  149.3 0.1 merge_near.3
  149.4 19.1 %all_to_all.66.in_ref = f32[8,8,640]{2,1,0:T(8,128)S(1)} all-to-all(f32[8,8,640]{2,1,0:T(8,128)S(1)} %merge_near.3), channel_id=1, replica_groups=mesh['z_high'=8,'z_low'=2,'y'=4,'head'=8] {'z_high'}, dimensions={0} | all-to-all | bytes 327680 | tf_op jit(solution)/shard_map/all_to_all | solution.py:355
  168.5 1.3 finish.3
  169.9 13.6 %all_to_all.67.in_ref = f32[16,8,128]{2,1,0:T(8,128)S(1)} all-to-all(f32[16,8,128]{2,1,0:T(8,128)S(1)} %finish.3), channel_id=1, replica_groups=mesh['z_high'=8,'z_low'=2,'y'=4,'head'=8] {'z_low','head'}, dimensions={0} | all-to-all | bytes 131072 | tf_op jit(solution)/shard_map/all_to_all | solution.py:355
  183.5 0.6 last.1
  (7 shorter events, 0.1 us)
Async XLA Ops:
  0.0 11.6 %copy-start.1 = (f32[256]{0:T(256)S(1)}, f32[256]{0:T(256)}, u32[]{:S(2)}) copy-start(f32[256]{0:T(256)} %param.14) | copy-start | bytes 3076
  0.0 15.0 %copy-start.4 = (s32[4]{0:T(128)S(1)}, s32[4]{0:T(128)}, u32[]{:S(2)}) copy-start(s32[4]{0:T(128)} %param.17) | copy-start | bytes 52
  0.0 0.7 copy-start.3
  4.2 15.8 %all-to-all-start = ((f32[8,8,640]{2,1,0:T(8,128)}), f32[8,8,640]{2,1,0:T(8,128)S(1)}, u32[]{:S(2)}, u32[]{:S(2)}) async-start(f32[8,8,640]{2,1,0:T(8,128)} %get-tuple-element.16), calls=%async_computation | async-start | bytes 327680 | tf_op jit(solution)/shard_map/all_to_all | solution.py:355
  11.6 8.4 %collective-permute-start = (f32[264,256]{1,0:T(8,128)S(1)}, f32[264,256]{1,0:T(8,128)S(1)}, u32[]{:S(2)}, u32[]{:S(2)}) collective-permute-start(f32[264,256]{1,0:T(8,128)S(1)} %pad_maximum_fusion), channel_id=1, source_target_pairs={{0,32},{32,0},{1,33},{33,1},{2,34},{34,2},{3,35},{35,3},{4,36},{36... | collective-permute-start | bytes 811016 | tf_op jit(solution)/shard_map/ppermute | solution.py:376
  20.7 28.2 %all-to-all-start.1 = ((f32[8,8,640]{2,1,0:T(8,128)}), f32[8,8,640]{2,1,0:T(8,128)S(1)}, u32[]{:S(2)}, u32[]{:S(2)}) async-start(f32[8,8,640]{2,1,0:T(8,128)} %sum_near.2), calls=%async_computation.1 | async-start | bytes 327680 | tf_op jit(solution)/shard_map/all_to_all | solution.py:355
  49.5 6.1 %all-to-all-start.2 = ((f32[2,8,640]{2,1,0:T(8,128)}), f32[2,8,640]{2,1,0:T(8,128)S(1)}, u32[]{:S(2)}, u32[]{:S(2)}) async-start(f32[2,8,640]{2,1,0:T(8,128)} %sum_far.2), calls=%async_computation.2 | async-start | bytes 81920 | tf_op jit(solution)/shard_map/all_to_all | solution.py:355
  55.6 18.3 %copy-start = (s32[256,512]{1,0:T(8,128)S(1)}, s32[256,512]{1,0:T(8,128)}, u32[]{:S(2)}) copy-start(s32[256,512]{1,0:T(8,128)} %codes_ref.1) | copy-start | bytes 1572868
  70.3 17.4 %all-to-all-start.4 = ((f32[8,8,640]{2,1,0:T(8,128)}), f32[8,8,640]{2,1,0:T(8,128)S(1)}, u32[]{:S(2)}, u32[]{:S(2)}) async-start(f32[8,8,640]{2,1,0:T(8,128)} %merge_near.2), calls=%async_computation.4 | async-start | bytes 327680 | tf_op jit(solution)/shard_map/all_to_all | solution.py:355
  74.0 33.2 %copy-start.2 = (f32[256]{0:T(256)S(1)}, f32[256]{0:T(256)}, u32[]{:S(2)}) copy-start(f32[256]{0:T(256)} %param.10) | copy-start | bytes 3076

commit v4 on v3

--- a/solution.py
+++ b/solution.py
@@ -14,6 +14,7 @@
 DECODE_STEPS = 2
 NEAR = ("z_low", "y")
 FAR = "z_high"
+Z = ("z_high", "z_low")
 SEQ = (FAR, *NEAR)
 
 CODE_NORM = 147.8
@@ -30,7 +31,7 @@
     return lax.broadcasted_iota(jnp.int32, shape, axis)
 
 
-def call(kernel, outs, name, arrays, scalars=(), remote=(), scratch=()):
+def call(kernel, outs, name, arrays, scalars=(), remote=(), scratch=(), out_specs=None):
     specs = [pl.BlockSpec(memory_space=pltpu.SMEM) for _ in scalars]
     specs += [pl.BlockSpec(memory_space=pltpu.HBM) for _ in remote]
     specs += [pl.BlockSpec(memory_space=pltpu.VMEM) for _ in arrays]
@@ -39,6 +40,7 @@
         kernel,
         out_shape=outs,
         in_specs=specs,
+        out_specs=out_specs or jax.tree.map(lambda _: pl.BlockSpec(memory_space=pltpu.VMEM), outs),
         scratch_shapes=scratch,
         name=name,
         compiler_params=pltpu.CompilerParams(vmem_limit_bytes=16 * 1024 * 1024),
@@ -60,19 +62,6 @@
     row = iota((128, 128), 0)
     column = iota((128, 128), 1)
     return (column == 4 * (row & 31) + (row >> 5)).astype(f32).astype(bf16)
-
-
-def by_sequence():
-    row = iota((64, 64), 0)
-    column = iota((64, 64), 1)
-    return (column == 4 * (row & 15) + (row >> 4)).astype(f32).astype(bf16)
-
-
-def by_place():
-    row = iota((32, 32), 0)
-    column = iota((32, 32), 1)
-    source = 8 * (row & 3) + (row & 4) + (row >> 3)
-    return (column == source).astype(f32).astype(bf16)
 
 
 def exact_product(x, ones):
@@ -114,8 +103,9 @@
     send_halves(out_ref, halves)
 
 
-def decode_qkv_kernel(codes_hbm, scale_hbm, gain_hbm, hidden_ref, w_ref, hid_ref, out_ref,
-                      codes_ref, scale_ref, gain_ref, code_sems, scale_sem, gain_sem):
+def decode_qkv_kernel(codes_hbm, scale_hbm, gain_hbm, hidden_ref, w_hbm, hid_ref, out_ref,
+                      codes_ref, scale_ref, gain_ref, w_ref, code_sems, scale_sem, gain_sem,
+                      w_sems):
     chunks = code_sems.shape[0]
     chunk_rows = codes_ref.shape[0] // chunks
     copies = []
@@ -133,6 +123,7 @@
     scale_copy.wait()
     lane = iota((32, 128), 1)
     word = iota((32, 128), 0)
+    kept = []
     for tile in range(18):
         if tile * 32 % chunk_rows == 0:
             copies[tile * 32 // chunk_rows].wait()
@@ -146,11 +137,18 @@
             values = byte_sum((window >> (8 - 2 * r)) & 0xFFFF) * column
             at = tile * 128 + r * 32
             w_ref[at : at + 32, :] = values.astype(bf16)
+        if (tile + 1) * 32 % chunk_rows == 0:
+            done = tile * 32 // chunk_rows
+            rows = pl.ds(done * 4 * chunk_rows, 4 * chunk_rows)
+            kept.append(pltpu.make_async_copy(w_ref.at[rows], w_hbm.at[rows], w_sems.at[done]))
+            kept[-1].start()
     hidden = hidden_ref[...].astype(f32)
     hidden = jnp.concatenate([hidden, hidden], axis=0)
     hid_ref[...] = hidden
     gain_copy.wait()
     project(hidden, gain_ref[...], w_ref[...], out_ref)
+    for copy in kept:
+        copy.wait()
 
 
 def decode_out_kernel(info_ref, codes_ref, scale_ref, other_ref, w_ref):
@@ -223,35 +221,31 @@
         out_ref[j, :, 512:] = stats
 
 
-def attend_kernel(features, earlier, info_ref, keys_hbm, values_hbm, in_ref, cos_ref, sin_ref,
+def attend_kernel(features, earlier, info_ref, in_ref, cos_ref, sin_ref, keys_ref, values_ref,
                   *refs):
-    out_ref, k_ref, v_ref, keys_ref, values_ref, key_sems, value_sems = refs[2 * earlier :]
-    key_copies = [
-        pltpu.make_async_copy(keys_hbm.at[b], keys_ref.at[b], key_sems.at[b]) for b in range(4)
-    ]
-    value_copies = [
-        pltpu.make_async_copy(values_hbm.at[b], values_ref.at[b], value_sems.at[b])
-        for b in range(4)
-    ]
-    for b in range(4):
-        key_copies[b].start()
-        value_copies[b].start()
+    out_ref, k_ref, v_ref, q_ref = refs[2 * earlier :]
+    halves = []
+    for s in range(2):
+        total = in_ref[s]
+        for j in range(2 + s, in_ref.shape[0], 2):
+            total = total + in_ref[j]
+        halves.append(total)
     first = iota((8, 128), 0) < 4
-    last = in_ref[0, :, 512:]
+    last = tile_of(halves[0], 4)
     squares = jnp.where(first, pltpu.roll(last, 4, 0), last)
     rms = lax.rsqrt(squares / features + EPSILON)
-    tiles = [tile_of(in_ref[s], i) * rms for s in range(2) for i in range(4)]
-    tiles += [in_ref[s, :, 512:] * rms for s in range(2)]
+    tiles = [tile_of(half, i) * rms for half in halves for i in range(4)]
+    tiles += [tile_of(half, 4) * rms for half in halves]
     x = exact_product(jnp.concatenate(tiles, axis=0), interleave())
     cos = jnp.concatenate([cos_ref[...]] * 18, axis=0)
     sin = jnp.concatenate([sin_ref[...]] * 18, axis=0)
     turned = x[:72] * cos + pltpu.roll(x[:72], 64, 1) * sin
-    turned = turned.astype(bf16)
-    new_key = turned[64:72].astype(f32)
+    turned = turned.astype(bf16).astype(f32)
+    q_ref[...] = turned[:64]
+    new_key = turned[64:]
     new_value = x[72:].astype(bf16).astype(f32)
     k_ref[...] = new_key
     v_ref[...] = new_value
-    queries = jnp.dot(by_sequence(), turned[:64], preferred_element_type=f32)
     new_keys = [refs[2 * u][...] for u in range(earlier)] + [new_key]
     new_values = [refs[2 * u + 1][...] for u in range(earlier)] + [new_value]
     owner = info_ref[4] == 0
@@ -261,8 +255,7 @@
     halves = [[], []]
     stats = [jnp.zeros((8, 128), f32)] * 2
     for b in range(4):
-        query = queries[b * 16 : b * 16 + 16]
-        key_copies[b].wait()
+        query = q_ref[pl.ds(b, 16, stride=4), :]
         scores = lax.dot_general(
             query.astype(bf16), keys_ref[b], NT, preferred_element_type=f32
         ) * SCORE_SCALE
@@ -270,7 +263,6 @@
         top = jnp.max(jnp.where(live, scores, -1e30), axis=1, keepdims=True)
         weights = jnp.where(live, jnp.exp(scores - top), 0.0)
         total = jnp.sum(weights, axis=1, keepdims=True)
-        value_copies[b].wait()
         acc = jnp.dot(weights.astype(bf16), values_ref[b], preferred_element_type=f32)
         fresh = [
             jnp.where(
@@ -296,30 +288,30 @@
     send_halves(out_ref, [halves[s] + [stats[s]] for s in range(2)])
 
 
-def finish_kernel(info_ref, in_ref, w_ref, out_ref):
+def finish_kernel(info_ref, in_ref, w_ref, out_ref, rows_ref):
     _, sums, accs = merged(in_ref)
+    for b in range(4):
+        attended = (accs[b] / sums[:, 4 + b : 5 + b]).astype(bf16).astype(f32)
+        rows_ref[b * 8 : b * 8 + 8, :] = attended
+        rows_ref[b * 8 + 32 : b * 8 + 40, :] = attended
     attended = jnp.concatenate(
-        [accs[b] / sums[:, 4 + b : 5 + b] for b in range(4)], axis=0
+        [rows_ref[pl.ds(t, 8, stride=8), :] for t in range(8)], axis=0
     ).astype(bf16)
-    attended = jnp.dot(by_place(), attended, preferred_element_type=f32).astype(bf16)
     attended = lax.dot_general(attended, interleave(), NT, preferred_element_type=f32)
     block = iota((8, 128), 1) >> 5
     chunks = []
-    for r in range(4):
-        chunk = jnp.zeros((8, 128), f32)
-        for t in range(4):
-            part = attended[t * 8 : t * 8 + 8]
-            if t != r:
-                part = pltpu.roll(part, (t - r) % 4 * 32, 1)
-            chunk = jnp.where(block == t, part, chunk)
-        chunks.append(chunk)
-    columns = jnp.concatenate(chunks, axis=1)
-    high = iota((8, 512), 0) >= 4
-    columns = jnp.concatenate(
-        [jnp.where(high, 0.0, columns), jnp.where(high, columns, 0.0)], axis=1
-    ).astype(bf16)
+    for group in range(2):
+        for r in range(4):
+            chunk = jnp.zeros((8, 128), f32)
+            for t in range(4):
+                at = (group * 4 + t) * 8
+                part = attended[at : at + 8]
+                if t != r:
+                    part = pltpu.roll(part, (t - r) % 4 * 32, 1)
+                chunk = jnp.where(block == t, part, chunk)
+            chunks.append(chunk)
+    columns = jnp.concatenate(chunks, axis=1).astype(bf16)
     update = lax.dot_general(columns, w_ref[...], NT, preferred_element_type=f32)
-    update = update + pltpu.roll(update, 4, 0)
     first = iota((8, 128), 0) < 4
     own = jnp.where(first, tile_of(update, 0), tile_of(update, 1))
     other = jnp.where(first, tile_of(update, 2), tile_of(update, 3))
@@ -385,10 +377,12 @@
     cosines, sines = jnp.cos(angles), jnp.sin(angles)
     cosines = jnp.concatenate([cosines, cosines], axis=-1)
     sines = jnp.concatenate([-sines, sines], axis=-1)
+    cosines = tuple(cosines[step] for step in range(DECODE_STEPS))
+    sines = tuple(sines[step] for step in range(DECODE_STEPS))
 
     w_qkv, hidden, partial = call(
         decode_qkv_kernel,
-        (shape_of((2304, 256), bf16), shape_of((8, 256)), shape_of((near, 8, 640))),
+        (pltpu.HBM((2304, 256), bf16), shape_of((8, 256)), shape_of((near, 8, 640))),
         "decode_qkv",
         (hidden_in,),
         remote=(qkv_codes.T, qkv_scale.reshape(18, 128), gain),
@@ -396,16 +390,25 @@
             pltpu.VMEM((576, 256), jnp.int32),
             pltpu.VMEM((18, 128), f32),
             pltpu.VMEM((1, 256), f32),
+            pltpu.VMEM((2304, 256), bf16),
             pltpu.SemaphoreType.DMA((6,)),
             pltpu.SemaphoreType.DMA,
             pltpu.SemaphoreType.DMA,
+            pltpu.SemaphoreType.DMA((6,)),
+        ),
+        out_specs=(
+            pl.BlockSpec(memory_space=pltpu.HBM),
+            pl.BlockSpec(memory_space=pltpu.VMEM),
+            pl.BlockSpec(memory_space=pltpu.VMEM),
         ),
     )
     fresh = ()
     for step in range(DECODE_STEPS):
         partial = exchange(partial, NEAR)
         if step == 0:
-            partial, other = lax.optimization_barrier((partial, other))
+            partial, other, info, cosines, sines = lax.optimization_barrier(
+                (partial, other, info, cosines, sines)
+            )
             w_out = call(
                 decode_out_kernel,
                 shape_of((512, 1024), bf16),
@@ -413,30 +416,27 @@
                 (out_codes, out_scale.reshape(1, -1), other),
                 (info,),
             )
-        partial = call(pass_sum_kernel, shape_of((far, 8, 640)), "sum_near", (partial,))
-        partial = exchange(partial, FAR)
-        partial = call(pass_sum_kernel, shape_of((2, 8, 640)), "sum_far", (partial,))
-        partial = exchange(partial, "z_low")
+        partial = call(pass_sum_kernel, shape_of((2 * far, 8, 640)), "sum_near", (partial,))
+        partial = exchange(partial, Z)
         part, new_key, new_value = call(
             functools.partial(attend_kernel, features, step),
             (shape_of((near, 8, 640)), shape_of((8, 128)), shape_of((8, 128))),
             "attend",
-            (partial, cosines[step], sines[step], *fresh),
+            (partial, cosines[step], sines[step], keys, values, *fresh),
             (info,),
-            (keys, values),
-            (
-                pltpu.VMEM(keys.shape, bf16),
-                pltpu.VMEM(keys.shape, bf16),
-                pltpu.SemaphoreType.DMA((4,)),
-                pltpu.SemaphoreType.DMA((4,)),
-            ),
+            scratch=(pltpu.VMEM((64, 128), f32),),
         )
         fresh += (new_key, new_value)
         part = exchange(part, NEAR)
         part = call(pass_merge_kernel, shape_of((far, 8, 640)), "merge_near", (part,))
         part = exchange(part, FAR)
         update = call(
-            finish_kernel, shape_of((2 * heads, 8, 128)), "finish", (part, w_out), (info,)
+            finish_kernel,
+            shape_of((2 * heads, 8, 128)),
+            "finish",
+            (part, w_out),
+            (info,),
+            scratch=(pltpu.VMEM((64, 128), f32),),
         )
         update = exchange(update, ("z_low", "head"))
         if step + 1 < DECODE_STEPS:

time: 185 us -> 179 us (0.968)
  blocking collectives: 98 us -> 128 us
  waiting for transfers between devices: 33.1 us -> 15.2 us
  starting transfers between devices: 31.2 us -> 15.6 us
  Pallas kernels: 19.6 us -> 14.8 us
  local copies, waits for them, and re-layouts: 0.73 us -> 3.38 us
    all_to_all x8, blocking collectives: 98 us -> 128 us  [exchange(): return lax.all_to_all(value, axes, split_axis=0, concat_axis=0, tiled=True)]
    all_to_all x4 -> x2, starting transfers between devices: 27.8 us -> 11.1 us  [exchange(): return lax.all_to_all(value, axes, split_axis=0, concat_axis=0, tiled=True)]
    all_to_all x4 -> x2, waiting for transfers between devices: 28.1 us -> 15.2 us  [exchange(): return lax.all_to_all(value, axes, split_axis=0, concat_axis=0, tiled=True)]
    ppermute x1, waiting for transfers between devices: 4.98 us -> 0.01 us  [shards(): other = lax.ppermute(wanted, 'z_low', [(0, 1), (1, 0)])]
    pallas_call x14 -> x12, Pallas kernels: 19.6 us -> 14.8 us  [call(): pl.pallas_call(kernel, out_shape=outs, in_specs=specs, out_specs=out_spec...]
    unnamed x10 -> x20, local copies, waits for them, and re-layouts: 0.72 us -> 2.7 us
  transfers between devices with their start and end apart: 5 -> 3, of which waited for: 4 -> 2; matrix products, arithmetic and copies ran while one was open for 1% -> 0% of each run, Pallas kernels for 1% -> 3%
where the time goes in v4:
time: 179 us; the launch traced here: 178 us
  blocking collectives  128 us (72%)
  starting transfers between devices  15.6 us (9%)
  waiting for transfers between devices  15.2 us (8%)
  Pallas kernels  14.8 us (8%)
  local copies, waits for them, and re-layouts  3.38 us (2%)
    all_to_all x8, blocking collectives, exchange(): return lax.all_to_all(value, axes, split_axis=0, concat_axis=0, tiled=True)  128 us
    all_to_all x2, waiting for transfers between devices, exchange(): return lax.all_to_all(value, axes, split_axis=0, concat_axis=0, tiled=True)  15.2 us
    pallas_call x12, Pallas kernels, call(): pl.pallas_call(kernel, out_shape=outs, in_specs=specs, out_specs=out_spec...  14.8 us
    all_to_all x2, starting transfers between devices, exchange(): return lax.all_to_all(value, axes, split_axis=0, concat_axis=0, tiled=True)  11.1 us
    ppermute x1, starting transfers between devices, shards(): other = lax.ppermute(wanted, 'z_low', [(0, 1), (1, 0)])  4.51 us
  transfers between devices with their start and end apart: 3, of which 2 were waited for; matrix products, arithmetic and copies ran while one was open for 0% of the time, Pallas kernels for 3%

profile of v4, /device:TPU:1, one launch (start us, length us, event | category | flops | bytes accessed | tf_op | source)
XLA Modules:
  0.0 178.4 jit_solution(1953824105699106568)
XLA Ops:
  0.0 0.0 copy-start.9
  0.0 1.0 dynamic-slice_convert_fusion
  1.0 0.7 broadcast_in_dim.4
  1.7 0.0 copy-start
  1.7 0.0 copy-start.1
  1.7 4.5 %collective-permute-start = (f32[264,256]{1,0:T(8,128)S(1)}, f32[264,256]{1,0:T(8,128)S(1)}, u32[]{:S(2)}, u32[]{:S(2)}) collective-permute-start(f32[264,256]{1,0:T(8,128)S(1)} %pad_maximum_fusion), channel_id=1, source_target_pairs={{0,32},{32,0},{1,33},{33,1},{2,34},{34,2},{3,35},{35,3},{4,36},{36... | collective-permute-start | bytes 811016 | tf_op jit(solution)/shard_map/ppermute | solution.py:368
  6.2 0.0 copy-start.8
  6.2 0.7 copy-done.8
  6.9 3.8 %decode_qkv.1 = (bf16[2304,256]{1,0:T(8,128)(2,1)}, f32[8,256]{1,0:T(8,128)S(1)}, f32[8,8,640]{2,1,0:T(8,128)}) custom-call(s32[576,256]{1,0:T(8,128)} %bitcast.23, f32[18,128]{1,0:T(8,128)} %bitcast.24, f32[1,256]{1,0:T(1,128)} %bitcast.21, bf16[4,256]{1,0:T(4,128)(2,1)S(1)} %copy-done.8), custom_call_target="tpu_custom_call" | custom-call | tf_op jit(solution)/shard_map/decode_qkv/pallas_call | solution.py:39
  10.8 4.2 %all-to-all-start = ((f32[8,8,640]{2,1,0:T(8,128)}), f32[8,8,640]{2,1,0:T(8,128)S(1)}, u32[]{:S(2)}, u32[]{:S(2)}) async-start(f32[8,8,640]{2,1,0:T(8,128)} %get-tuple-element.21), calls=%async_computation | async-start | bytes 327680 | tf_op jit(solution)/shard_map/all_to_all | solution.py:347
  15.0 0.0 copy-done.9
  15.0 0.1 multiply_sine_fusion
  15.1 0.1 pad_add_fusion.info_ref
  15.2 0.1 fusion.4
  15.3 0.0 collective-permute-done.other_ref
  15.3 0.0 copy-start.4
  15.3 5.3 %all-to-all-done.in_ref = f32[8,8,640]{2,1,0:T(8,128)S(1)} async-done(((f32[8,8,640]{2,1,0:T(8,128)}), f32[8,8,640]{2,1,0:T(8,128)S(1)}, u32[]{:S(2)}, u32[]{:S(2)}) %all-to-all-start) | async-done | bytes 163872 | tf_op jit(solution)/shard_map/all_to_all | solution.py:347
  20.6 27.8 %all_to_all.50.in_ref = f32[16,8,640]{2,1,0:T(8,128)S(1)} all-to-all(f32[16,8,640]{2,1,0:T(8,128)S(1)} %sum_near.2), channel_id=1, replica_groups=mesh['z_high'=8,'z_low'=2,'y'=4,'head'=8] {'z_high','z_low'}, dimensions={0} | all-to-all | bytes 655360 | tf_op jit(solution)/shard_map/all_to_all | solution.py:347
  48.4 0.0 copy-done
  48.4 0.0 copy-done.1
  48.4 2.1 %attend.2 = (f32[8,8,640]{2,1,0:T(8,128)S(1)}, f32[8,128]{1,0:T(8,128)S(1)}, f32[8,128]{1,0:T(8,128)S(1)}) custom-call(s32[6]{0:T(128)S(1)} %pad_add_fusion.info_ref, f32[16,8,640]{2,1,0:T(8,128)S(1)} %all_to_all.50.in_ref, f32[4,128]{1,0:T(4,128)S(1)} %get-tuple-element.24.cos_ref, f32[4,128]{1,0:T(4,128)S(1)} %get-tuple-element.25.sin_ref, ...), custom_call_target="tpu_custom_call" | custom-call | tf_op jit(solution)/shard_map/attend/pallas_call | solution.py:39
  50.5 0.0 copy-done.4
  50.5 13.7 %all_to_all.51.in_ref = f32[8,8,640]{2,1,0:T(8,128)S(1)} all-to-all(f32[8,8,640]{2,1,0:T(8,128)S(1)} %get-tuple-element.26), channel_id=1, replica_groups=mesh['z_high'=8,'z_low'=2,'y'=4,'head'=8] {'z_low','y'}, dimensions={0} | all-to-all | bytes 327680 | tf_op jit(solution)/shard_map/all_to_all | solution.py:347
  64.2 0.8 merge_near.2
  65.0 6.9 %all-to-all-start.3 = ((f32[8,8,640]{2,1,0:T(8,128)}), f32[8,8,640]{2,1,0:T(8,128)S(1)}, u32[]{:S(2)}, u32[]{:S(2)}) async-start(f32[8,8,640]{2,1,0:T(8,128)} %merge_near.2), calls=%async_computation.3 | async-start | bytes 327680 | tf_op jit(solution)/shard_map/all_to_all | solution.py:347
  71.9 0.0 copy-done.6
  71.9 0.0 copy-start.3
  71.9 1.0 copy-done.3
  72.9 0.0 copy-start.5
  72.9 1.0 copy-done.5
  73.9 0.0 copy-start.7
  73.9 1.9 %decode_out.1.w_ref = bf16[512,1024]{1,0:T(8,128)(2,1)S(1)} custom-call(s32[6]{0:T(128)S(1)} %pad_add_fusion.info_ref, s32[256,512]{1,0:T(8,128)S(1)} %copy-done.3, f32[1,256]{1,0:T(1,128)S(1)} %bitcast.20, f32[264,256]{1,0:T(8,128)S(1)} %copy-done.5), custom_call_target="tpu_custom_call" | custom-call | tf_op jit(solution)/shard_map/decode_out/pallas_call | solution.py:39
  75.8 9.9 %all-to-all-done.3.in_ref = f32[8,8,640]{2,1,0:T(8,128)S(1)} async-done(((f32[8,8,640]{2,1,0:T(8,128)}), f32[8,8,640]{2,1,0:T(8,128)S(1)}, u32[]{:S(2)}, u32[]{:S(2)}) %all-to-all-start.3) | async-done | bytes 163872 | tf_op jit(solution)/shard_map/all_to_all | solution.py:347
  85.7 0.0 copy-start.2
  85.7 1.2 finish.2
  86.9 14.6 %all_to_all.52.in_ref = f32[16,8,128]{2,1,0:T(8,128)S(1)} all-to-all(f32[16,8,128]{2,1,0:T(8,128)S(1)} %finish.2), channel_id=1, replica_groups=mesh['z_high'=8,'z_low'=2,'y'=4,'head'=8] {'z_low','head'}, dimensions={0} | all-to-all | bytes 131072 | tf_op jit(solution)/shard_map/all_to_all | solution.py:347
  101.5 0.0 copy-done.7
  101.5 0.0 copy-done.2
  101.5 0.4 next_step.1
  102.0 8.1 %all_to_all.53.in_ref = f32[8,8,640]{2,1,0:T(8,128)S(1)} all-to-all(f32[8,8,640]{2,1,0:T(8,128)S(1)} %get-tuple-element.30), channel_id=1, replica_groups=mesh['z_high'=8,'z_low'=2,'y'=4,'head'=8] {'z_low','y'}, dimensions={0} | all-to-all | bytes 327680 | tf_op jit(solution)/shard_map/all_to_all | solution.py:347
  110.1 16.6 %all_to_all.54.in_ref = f32[16,8,640]{2,1,0:T(8,128)S(1)} all-to-all(f32[16,8,640]{2,1,0:T(8,128)S(1)} %sum_near.3), channel_id=1, replica_groups=mesh['z_high'=8,'z_low'=2,'y'=4,'head'=8] {'z_high','z_low'}, dimensions={0} | all-to-all | bytes 655360 | tf_op jit(solution)/shard_map/all_to_all | solution.py:347
  126.7 2.6 %attend.3 = (f32[8,8,640]{2,1,0:T(8,128)S(1)}, f32[8,128]{1,0:T(8,128)}, f32[8,128]{1,0:T(8,128)}) custom-call(s32[6]{0:T(128)S(1)} %pad_add_fusion.info_ref, f32[16,8,640]{2,1,0:T(8,128)S(1)} %all_to_all.54.in_ref, f32[4,128]{1,0:T(4,128)S(1)} %get-tuple-element.31.cos_ref, f32[4,128]{1,0:T(4,128)S(1)} %get-tuple-element.32.sin_ref, ...), custom_call_target="tpu_custom_call" | custom-call | tf_op jit(solution)/shard_map/attend/pallas_call | solution.py:39
  129.3 14.4 %all_to_all.55.in_ref = f32[8,8,640]{2,1,0:T(8,128)S(1)} all-to-all(f32[8,8,640]{2,1,0:T(8,128)S(1)} %get-tuple-element.35), channel_id=1, replica_groups=mesh['z_high'=8,'z_low'=2,'y'=4,'head'=8] {'z_low','y'}, dimensions={0} | all-to-all | bytes 327680 | tf_op jit(solution)/shard_map/all_to_all | solution.py:347
  143.7 0.1 merge_near.3
  143.8 20.0 %all_to_all.56.in_ref = f32[8,8,640]{2,1,0:T(8,128)S(1)} all-to-all(f32[8,8,640]{2,1,0:T(8,128)S(1)} %merge_near.3), channel_id=1, replica_groups=mesh['z_high'=8,'z_low'=2,'y'=4,'head'=8] {'z_high'}, dimensions={0} | all-to-all | bytes 327680 | tf_op jit(solution)/shard_map/all_to_all | solution.py:347
  163.9 1.2 finish.3
  165.1 12.8 %all_to_all.57.in_ref = f32[16,8,128]{2,1,0:T(8,128)S(1)} all-to-all(f32[16,8,128]{2,1,0:T(8,128)S(1)} %finish.3), channel_id=1, replica_groups=mesh['z_high'=8,'z_low'=2,'y'=4,'head'=8] {'z_low','head'}, dimensions={0} | all-to-all | bytes 131072 | tf_op jit(solution)/shard_map/all_to_all | solution.py:347
  177.8 0.6 last.1
  (7 shorter events, 0.1 us)
Async XLA Ops:
  0.0 15.0 %copy-start.9 = (s32[4]{0:T(128)S(1)}, s32[4]{0:T(128)}, u32[]{:S(2)}) copy-start(s32[4]{0:T(128)} %param.17) | copy-start | bytes 52
  1.7 46.7 %copy-start = (bf16[4,1024,1,128]{3,1,2,0:T(8,128)(2,1)S(1)}, bf16[4,1024,1,128]{3,1,2,0:T(8,128)(2,1)}, u32[]{:S(2)}) copy-start(bf16[4,1024,1,128]{3,1,2,0:T(8,128)(2,1)} %param.15) | copy-start | bytes 3145732
  1.7 46.7 %copy-start.1 = (bf16[4,1024,1,128]{3,1,2,0:T(8,128)(2,1)S(1)}, bf16[4,1024,1,128]{3,1,2,0:T(8,128)(2,1)}, u32[]{:S(2)}) copy-start(bf16[4,1024,1,128]{3,1,2,0:T(8,128)(2,1)} %param.16) | copy-start | bytes 3145732
  1.7 13.6 %collective-permute-start = (f32[264,256]{1,0:T(8,128)S(1)}, f32[264,256]{1,0:T(8,128)S(1)}, u32[]{:S(2)}, u32[]{:S(2)}) collective-permute-start(f32[264,256]{1,0:T(8,128)S(1)} %pad_maximum_fusion), channel_id=1, source_target_pairs={{0,32},{32,0},{1,33},{33,1},{2,34},{34,2},{3,35},{35,3},{4,36},{36... | collective-permute-start | bytes 811016 | tf_op jit(solution)/shard_map/ppermute | solution.py:368
  6.2 0.7 copy-start.8
  10.8 9.8 %all-to-all-start = ((f32[8,8,640]{2,1,0:T(8,128)}), f32[8,8,640]{2,1,0:T(8,128)S(1)}, u32[]{:S(2)}, u32[]{:S(2)}) async-start(f32[8,8,640]{2,1,0:T(8,128)} %get-tuple-element.21), calls=%async_computation | async-start | bytes 327680 | tf_op jit(solution)/shard_map/all_to_all | solution.py:347
  15.3 35.2 %copy-start.4 = (f32[264,256]{1,0:T(8,128)}, f32[264,256]{1,0:T(8,128)S(1)}, u32[]{:S(2)}) copy-start(f32[264,256]{1,0:T(8,128)S(1)} %collective-permute-done.other_ref) | copy-start | bytes 811012
  48.4 23.5 %copy-start.6 = (f32[256]{0:T(256)S(1)}, f32[256]{0:T(256)}, u32[]{:S(2)}) copy-start(f32[256]{0:T(256)} %param.14) | copy-start | bytes 3076
  65.0 20.7 %all-to-all-start.3 = ((f32[8,8,640]{2,1,0:T(8,128)}), f32[8,8,640]{2,1,0:T(8,128)S(1)}, u32[]{:S(2)}, u32[]{:S(2)}) async-start(f32[8,8,640]{2,1,0:T(8,128)} %merge_near.2), calls=%async_computation.3 | async-start | bytes 327680 | tf_op jit(solution)/shard_map/all_to_all | solution.py:347
  71.9 1.0 copy-start.3
  72.9 1.0 copy-start.5
  73.9 27.6 %copy-start.7 = (f32[256]{0:T(256)S(1)}, f32[256]{0:T(256)}, u32[]{:S(2)}) copy-start(f32[256]{0:T(256)} %param.10) | copy-start | bytes 3076
  85.7 15.9 %copy-start.2 = (bf16[2304,256]{1,0:T(8,128)(2,1)S(1)}, bf16[2304,256]{1,0:T(8,128)(2,1)}, u32[]{:S(2)}) copy-start(bf16[2304,256]{1,0:T(8,128)(2,1)} %get-tuple-element.29.w_ref) | copy-start | bytes 3538948

commit v5 on v4

--- a/solution.py
+++ b/solution.py
@@ -14,7 +14,6 @@
 DECODE_STEPS = 2
 NEAR = ("z_low", "y")
 FAR = "z_high"
-Z = ("z_high", "z_low")
 SEQ = (FAR, *NEAR)
 
 CODE_NORM = 147.8
@@ -92,15 +91,16 @@
     normed = (hidden * gain).astype(bf16)
     y = lax.dot_general(normed, weights, NT, preferred_element_type=f32)
     first = iota((8, 128), 0) < 4
+    few = iota((8, 128), 1) < 16
     spread = jnp.broadcast_to(squares, (8, 128))
-    halves = []
-    for s in range(2):
-        tiles = [
-            jnp.where(first, tile_of(y, 8 * s + 2 * i), tile_of(y, 8 * s + 2 * i + 1))
-            for i in range(4)
-        ]
-        halves.append(tiles + [jnp.where(first, tile_of(y, 16 + s), spread)])
-    send_halves(out_ref, halves)
+    tails = [tile_of(y, 16 + k) for k in range(2)]
+    tails = [jnp.where(first, tail, pltpu.roll(tail, 112, 1)) for tail in tails]
+    for p in range(8):
+        tail = tails[p // 4]
+        if p % 4:
+            tail = pltpu.roll(tail, 128 - 32 * (p % 4), 1)
+        out_ref[p, :, :128] = jnp.where(first, tile_of(y, 2 * p), tile_of(y, 2 * p + 1))
+        out_ref[p, :, 128:] = jnp.where(few, tail, spread)
 
 
 def decode_qkv_kernel(codes_hbm, scale_hbm, gain_hbm, hidden_ref, w_hbm, hid_ref, out_ref,
@@ -224,18 +224,18 @@
 def attend_kernel(features, earlier, info_ref, in_ref, cos_ref, sin_ref, keys_ref, values_ref,
                   *refs):
     out_ref, k_ref, v_ref, q_ref = refs[2 * earlier :]
-    halves = []
-    for s in range(2):
-        total = in_ref[s]
-        for j in range(2 + s, in_ref.shape[0], 2):
-            total = total + in_ref[j]
-        halves.append(total)
     first = iota((8, 128), 0) < 4
-    last = tile_of(halves[0], 4)
-    squares = jnp.where(first, pltpu.roll(last, 4, 0), last)
-    rms = lax.rsqrt(squares / features + EPSILON)
-    tiles = [tile_of(half, i) * rms for half in halves for i in range(4)]
-    tiles += [tile_of(half, 4) * rms for half in halves]
+    lane = iota((8, 128), 1)
+    rms = lax.rsqrt(in_ref[0, :, 144:145] / features + EPSILON)
+    tiles = [in_ref[p, :, :128] for p in range(8)]
+    for k in range(2):
+        tail = in_ref[4 * k, :, 128:]
+        for p in range(1, 4):
+            part = pltpu.roll(in_ref[4 * k + p, :, 128:], 32 * p, 1)
+            tail = jnp.where(lane >> 5 == p, part, tail)
+        tail = jnp.where(first, tail, pltpu.roll(tail, 16, 1))
+        tiles.append(jnp.where(lane & 31 < 16, tail, pltpu.roll(tail, 4, 0)))
+    tiles = [tile * rms for tile in tiles]
     x = exact_product(jnp.concatenate(tiles, axis=0), interleave())
     cos = jnp.concatenate([cos_ref[...]] * 18, axis=0)
     sin = jnp.concatenate([sin_ref[...]] * 18, axis=0)
@@ -251,7 +251,6 @@
     owner = info_ref[4] == 0
     length = keys_ref.shape[1]
     place = iota((16, length), 1)
-    lane = iota((8, 128), 1)
     halves = [[], []]
     stats = [jnp.zeros((8, 128), f32)] * 2
     for b in range(4):
@@ -382,7 +381,7 @@
 
     w_qkv, hidden, partial = call(
         decode_qkv_kernel,
-        (pltpu.HBM((2304, 256), bf16), shape_of((8, 256)), shape_of((near, 8, 640))),
+        (pltpu.HBM((2304, 256), bf16), shape_of((8, 256)), shape_of((near, 8, 256))),
         "decode_qkv",
         (hidden_in,),
         remote=(qkv_codes.T, qkv_scale.reshape(18, 128), gain),
@@ -416,8 +415,10 @@
                 (out_codes, out_scale.reshape(1, -1), other),
                 (info,),
             )
-        partial = call(pass_sum_kernel, shape_of((2 * far, 8, 640)), "sum_near", (partial,))
-        partial = exchange(partial, Z)
+        partial = call(pass_sum_kernel, shape_of((far, 8, 256)), "sum_near", (partial,))
+        partial = exchange(partial, FAR)
+        partial = call(pass_sum_kernel, shape_of((near, 8, 256)), "sum_far", (partial,))
+        partial = exchange(partial, NEAR)
         part, new_key, new_value = call(
             functools.partial(attend_kernel, features, step),
             (shape_of((near, 8, 640)), shape_of((8, 128)), shape_of((8, 128))),
@@ -442,7 +443,7 @@
         if step + 1 < DECODE_STEPS:
             hidden, partial = call(
                 next_kernel,
-                (shape_of((8, 256)), shape_of((near, 8, 640))),
+                (shape_of((8, 256)), shape_of((near, 8, 256))),
                 "next_step",
                 (update, hidden, gain, w_qkv),
             )

time: 179 us -> 176 us (0.983)
  starting transfers between devices: 15.6 us -> 12 us
    all_to_all x2, starting transfers between devices: 11.1 us -> 7.58 us  [exchange(): return lax.all_to_all(value, axes, split_axis=0, concat_axis=0, tiled=True)]
    all_to_all x8 -> x10, blocking collectives: 128 us -> 129 us  [exchange(): return lax.all_to_all(value, axes, split_axis=0, concat_axis=0, tiled=True)]
    pallas_call x12 -> x14, Pallas kernels: 14.8 us -> 15.1 us  [call(): pl.pallas_call(kernel, out_shape=outs, in_specs=specs, out_specs=out_spec...]
where the time goes in v5:
time: 176 us
  blocking collectives  129 us (73%)
  Pallas kernels  15.1 us (9%)
  waiting for transfers between devices  14.7 us (8%)
  starting transfers between devices  12 us (7%)
  local copies, waits for them, and re-layouts  3.37 us (2%)
    all_to_all x10, blocking collectives, exchange(): return lax.all_to_all(value, axes, split_axis=0, concat_axis=0, tiled=True)  129 us
    pallas_call x14, Pallas kernels, call(): pl.pallas_call(kernel, out_shape=outs, in_specs=specs, out_specs=out_spec...  15.1 us
    all_to_all x2, waiting for transfers between devices, exchange(): return lax.all_to_all(value, axes, split_axis=0, concat_axis=0, tiled=True)  14.7 us
    all_to_all x2, starting transfers between devices, exchange(): return lax.all_to_all(value, axes, split_axis=0, concat_axis=0, tiled=True)  7.58 us
    ppermute x1, starting transfers between devices, shards(): other = lax.ppermute(wanted, 'z_low', [(0, 1), (1, 0)])  4.38 us
  transfers between devices with their start and end apart: 3, of which 2 were waited for; matrix products, arithmetic and copies ran while one was open for 0% of the time, Pallas kernels for 3%

profile of v5, /device:TPU:1, one launch (start us, length us, event | category | flops | bytes accessed | tf_op | source)
XLA Modules:
  0.0 175.6 jit_solution(1134063749922603740)
XLA Ops:
  0.0 0.0 copy-start.9
  0.0 0.0 copy-start
  0.0 1.1 dynamic-slice_convert_fusion
  1.1 0.7 broadcast_in_dim.4
  1.8 4.4 %collective-permute-start = (f32[264,256]{1,0:T(8,128)S(1)}, f32[264,256]{1,0:T(8,128)S(1)}, u32[]{:S(2)}, u32[]{:S(2)}) collective-permute-start(f32[264,256]{1,0:T(8,128)S(1)} %pad_maximum_fusion), channel_id=1, source_target_pairs={{0,32},{32,0},{1,33},{33,1},{2,34},{34,2},{3,35},{35,3},{4,36},{36... | collective-permute-start | bytes 811016 | tf_op jit(solution)/shard_map/ppermute | solution.py:367
  6.2 0.0 copy-start.8
  6.2 0.7 copy-done.8
  6.9 3.8 %decode_qkv.1 = (bf16[2304,256]{1,0:T(8,128)(2,1)}, f32[8,256]{1,0:T(8,128)S(1)}, f32[8,8,256]{2,1,0:T(8,128)}) custom-call(s32[576,256]{1,0:T(8,128)} %bitcast.23, f32[18,128]{1,0:T(8,128)} %bitcast.24, f32[1,256]{1,0:T(1,128)} %bitcast.21, bf16[4,256]{1,0:T(4,128)(2,1)S(1)} %copy-done.8), custom_call_target="tpu_custom_call" | custom-call | tf_op jit(solution)/shard_map/decode_qkv/pallas_call | solution.py:38
  10.7 4.2 %all-to-all-start = ((f32[8,8,256]{2,1,0:T(8,128)}), f32[8,8,256]{2,1,0:T(8,128)S(1)}, u32[]{:S(2)}, u32[]{:S(2)}) async-start(f32[8,8,256]{2,1,0:T(8,128)} %get-tuple-element.21), calls=%async_computation | async-start | bytes 131072 | tf_op jit(solution)/shard_map/all_to_all | solution.py:346
  14.9 0.0 copy-done.9
  15.0 0.1 multiply_sine_fusion
  15.1 0.1 pad_add_fusion.info_ref
  15.2 0.1 fusion.4
  15.3 4.9 %all-to-all-done.in_ref = f32[8,8,256]{2,1,0:T(8,128)S(1)} async-done(((f32[8,8,256]{2,1,0:T(8,128)}), f32[8,8,256]{2,1,0:T(8,128)S(1)}, u32[]{:S(2)}, u32[]{:S(2)}) %all-to-all-start) | async-done | bytes 65568 | tf_op jit(solution)/shard_map/all_to_all | solution.py:346
  20.1 0.0 collective-permute-done.other_ref
  20.1 0.0 copy-start.4
  20.1 26.4 %all_to_all.60.in_ref = f32[8,8,256]{2,1,0:T(8,128)S(1)} all-to-all(f32[8,8,256]{2,1,0:T(8,128)S(1)} %sum_near.2), channel_id=1, replica_groups=mesh['z_high'=8,'z_low'=2,'y'=4,'head'=8] {'z_high'}, dimensions={0} | all-to-all | bytes 131072 | tf_op jit(solution)/shard_map/all_to_all | solution.py:346
  46.6 7.6 %all_to_all.61.in_ref = f32[8,8,256]{2,1,0:T(8,128)S(1)} all-to-all(f32[8,8,256]{2,1,0:T(8,128)S(1)} %sum_far.2), channel_id=1, replica_groups=mesh['z_high'=8,'z_low'=2,'y'=4,'head'=8] {'z_low','y'}, dimensions={0} | all-to-all | bytes 131072 | tf_op jit(solution)/shard_map/all_to_all | solution.py:346
  54.2 0.0 copy-done
  54.2 0.0 copy-done.1
  54.2 2.2 %attend.2 = (f32[8,8,640]{2,1,0:T(8,128)S(1)}, f32[8,128]{1,0:T(8,128)S(1)}, f32[8,128]{1,0:T(8,128)S(1)}) custom-call(s32[6]{0:T(128)S(1)} %pad_add_fusion.info_ref, f32[8,8,256]{2,1,0:T(8,128)S(1)} %all_to_all.61.in_ref, f32[4,128]{1,0:T(4,128)S(1)} %get-tuple-element.24.cos_ref, f32[4,128]{1,0:T(4,128)S(1)} %get-tuple-element.25.sin_ref, ...), custom_call_target="tpu_custom_call" | custom-call | tf_op jit(solution)/shard_map/attend/pallas_call | solution.py:38
  56.4 0.0 copy-done.4
  56.4 8.0 %all_to_all.62.in_ref = f32[8,8,640]{2,1,0:T(8,128)S(1)} all-to-all(f32[8,8,640]{2,1,0:T(8,128)S(1)} %get-tuple-element.26), channel_id=1, replica_groups=mesh['z_high'=8,'z_low'=2,'y'=4,'head'=8] {'z_low','y'}, dimensions={0} | all-to-all | bytes 327680 | tf_op jit(solution)/shard_map/all_to_all | solution.py:346
  64.4 0.8 merge_near.2
  65.2 3.4 %all-to-all-start.4 = ((f32[8,8,640]{2,1,0:T(8,128)}), f32[8,8,640]{2,1,0:T(8,128)S(1)}, u32[]{:S(2)}, u32[]{:S(2)}) async-start(f32[8,8,640]{2,1,0:T(8,128)} %merge_near.2), calls=%async_computation.4 | async-start | bytes 327680 | tf_op jit(solution)/shard_map/all_to_all | solution.py:346
  68.6 0.0 copy-done.6
  68.6 0.0 copy-start.3
  68.6 1.0 copy-done.3
  69.7 0.0 copy-start.5
  69.7 1.0 copy-done.5
  70.6 0.0 copy-start.7
  70.6 1.9 %decode_out.1.w_ref = bf16[512,1024]{1,0:T(8,128)(2,1)S(1)} custom-call(s32[6]{0:T(128)S(1)} %pad_add_fusion.info_ref, s32[256,512]{1,0:T(8,128)S(1)} %copy-done.3, f32[1,256]{1,0:T(1,128)S(1)} %bitcast.20, f32[264,256]{1,0:T(8,128)S(1)} %copy-done.5), custom_call_target="tpu_custom_call" | custom-call | tf_op jit(solution)/shard_map/decode_out/pallas_call | solution.py:38
  72.5 9.8 %all-to-all-done.4.in_ref = f32[8,8,640]{2,1,0:T(8,128)S(1)} async-done(((f32[8,8,640]{2,1,0:T(8,128)}), f32[8,8,640]{2,1,0:T(8,128)S(1)}, u32[]{:S(2)}, u32[]{:S(2)}) %all-to-all-start.4) | async-done | bytes 163872 | tf_op jit(solution)/shard_map/all_to_all | solution.py:346
  82.3 1.2 finish.2
  83.5 17.8 %all_to_all.63.in_ref = f32[16,8,128]{2,1,0:T(8,128)S(1)} all-to-all(f32[16,8,128]{2,1,0:T(8,128)S(1)} %finish.2), channel_id=1, replica_groups=mesh['z_high'=8,'z_low'=2,'y'=4,'head'=8] {'z_low','head'}, dimensions={0} | all-to-all | bytes 131072 | tf_op jit(solution)/shard_map/all_to_all | solution.py:346
  101.3 0.0 copy-done.7
  101.3 0.0 copy-done.2
  101.3 0.6 next_step.1
  101.9 7.7 %all_to_all.64.in_ref = f32[8,8,256]{2,1,0:T(8,128)S(1)} all-to-all(f32[8,8,256]{2,1,0:T(8,128)S(1)} %get-tuple-element.30), channel_id=1, replica_groups=mesh['z_high'=8,'z_low'=2,'y'=4,'head'=8] {'z_low','y'}, dimensions={0} | all-to-all | bytes 131072 | tf_op jit(solution)/shard_map/all_to_all | solution.py:346
  109.6 14.7 %all_to_all.65.in_ref = f32[8,8,256]{2,1,0:T(8,128)S(1)} all-to-all(f32[8,8,256]{2,1,0:T(8,128)S(1)} %sum_near.3), channel_id=1, replica_groups=mesh['z_high'=8,'z_low'=2,'y'=4,'head'=8] {'z_high'}, dimensions={0} | all-to-all | bytes 131072 | tf_op jit(solution)/shard_map/all_to_all | solution.py:346
  124.3 7.6 %all_to_all.66.in_ref = f32[8,8,256]{2,1,0:T(8,128)S(1)} all-to-all(f32[8,8,256]{2,1,0:T(8,128)S(1)} %sum_far.3), channel_id=1, replica_groups=mesh['z_high'=8,'z_low'=2,'y'=4,'head'=8] {'z_low','y'}, dimensions={0} | all-to-all | bytes 131072 | tf_op jit(solution)/shard_map/all_to_all | solution.py:346
  131.8 2.7 %attend.3 = (f32[8,8,640]{2,1,0:T(8,128)S(1)}, f32[8,128]{1,0:T(8,128)}, f32[8,128]{1,0:T(8,128)}) custom-call(s32[6]{0:T(128)S(1)} %pad_add_fusion.info_ref, f32[8,8,256]{2,1,0:T(8,128)S(1)} %all_to_all.66.in_ref, f32[4,128]{1,0:T(4,128)S(1)} %get-tuple-element.31.cos_ref, f32[4,128]{1,0:T(4,128)S(1)} %get-tuple-element.32.sin_ref, ...), custom_call_target="tpu_custom_call" | custom-call | tf_op jit(solution)/shard_map/attend/pallas_call | solution.py:38
  134.5 8.0 %all_to_all.67.in_ref = f32[8,8,640]{2,1,0:T(8,128)S(1)} all-to-all(f32[8,8,640]{2,1,0:T(8,128)S(1)} %get-tuple-element.35), channel_id=1, replica_groups=mesh['z_high'=8,'z_low'=2,'y'=4,'head'=8] {'z_low','y'}, dimensions={0} | all-to-all | bytes 327680 | tf_op jit(solution)/shard_map/all_to_all | solution.py:346
  142.5 0.1 merge_near.3
  142.6 16.1 %all_to_all.68.in_ref = f32[8,8,640]{2,1,0:T(8,128)S(1)} all-to-all(f32[8,8,640]{2,1,0:T(8,128)S(1)} %merge_near.3), channel_id=1, replica_groups=mesh['z_high'=8,'z_low'=2,'y'=4,'head'=8] {'z_high'}, dimensions={0} | all-to-all | bytes 327680 | tf_op jit(solution)/shard_map/all_to_all | solution.py:346
  158.8 1.2 finish.3
  160.0 15.1 %all_to_all.69.in_ref = f32[16,8,128]{2,1,0:T(8,128)S(1)} all-to-all(f32[16,8,128]{2,1,0:T(8,128)S(1)} %finish.3), channel_id=1, replica_groups=mesh['z_high'=8,'z_low'=2,'y'=4,'head'=8] {'z_low','head'}, dimensions={0} | all-to-all | bytes 131072 | tf_op jit(solution)/shard_map/all_to_all | solution.py:346
  175.0 0.6 last.1
  (11 shorter events, 0.1 us)
Async XLA Ops:
  0.0 14.9 %copy-start.9 = (s32[4]{0:T(128)S(1)}, s32[4]{0:T(128)}, u32[]{:S(2)}) copy-start(s32[4]{0:T(128)} %param.17) | copy-start | bytes 52
  0.0 54.2 %copy-start = (bf16[4,1024,1,128]{3,1,2,0:T(8,128)(2,1)S(1)}, bf16[4,1024,1,128]{3,1,2,0:T(8,128)(2,1)}, u32[]{:S(2)}) copy-start(bf16[4,1024,1,128]{3,1,2,0:T(8,128)(2,1)} %param.15) | copy-start | bytes 3145732
  0.0 54.2 %copy-start.1 = (bf16[4,1024,1,128]{3,1,2,0:T(8,128)(2,1)S(1)}, bf16[4,1024,1,128]{3,1,2,0:T(8,128)(2,1)}, u32[]{:S(2)}) copy-start(bf16[4,1024,1,128]{3,1,2,0:T(8,128)(2,1)} %param.16) | copy-start | bytes 3145732
  1.8 18.3 %collective-permute-start = (f32[264,256]{1,0:T(8,128)S(1)}, f32[264,256]{1,0:T(8,128)S(1)}, u32[]{:S(2)}, u32[]{:S(2)}) collective-permute-start(f32[264,256]{1,0:T(8,128)S(1)} %pad_maximum_fusion), channel_id=1, source_target_pairs={{0,32},{32,0},{1,33},{33,1},{2,34},{34,2},{3,35},{35,3},{4,36},{36... | collective-permute-start | bytes 811016 | tf_op jit(solution)/shard_map/ppermute | solution.py:367
  6.2 0.7 copy-start.8
  10.7 9.4 %all-to-all-start = ((f32[8,8,256]{2,1,0:T(8,128)}), f32[8,8,256]{2,1,0:T(8,128)S(1)}, u32[]{:S(2)}, u32[]{:S(2)}) async-start(f32[8,8,256]{2,1,0:T(8,128)} %get-tuple-element.21), calls=%async_computation | async-start | bytes 131072 | tf_op jit(solution)/shard_map/all_to_all | solution.py:346
  20.1 36.3 %copy-start.4 = (f32[264,256]{1,0:T(8,128)}, f32[264,256]{1,0:T(8,128)S(1)}, u32[]{:S(2)}) copy-start(f32[264,256]{1,0:T(8,128)S(1)} %collective-permute-done.other_ref) | copy-start | bytes 811012
  54.2 14.4 %copy-start.6 = (f32[256]{0:T(256)S(1)}, f32[256]{0:T(256)}, u32[]{:S(2)}) copy-start(f32[256]{0:T(256)} %param.14) | copy-start | bytes 3076
  65.2 17.1 %all-to-all-start.4 = ((f32[8,8,640]{2,1,0:T(8,128)}), f32[8,8,640]{2,1,0:T(8,128)S(1)}, u32[]{:S(2)}, u32[]{:S(2)}) async-start(f32[8,8,640]{2,1,0:T(8,128)} %merge_near.2), calls=%async_computation.4 | async-start | bytes 327680 | tf_op jit(solution)/shard_map/all_to_all | solution.py:346
  68.6 1.0 copy-start.3
  69.7 1.0 copy-start.5
  70.6 30.7 %copy-start.7 = (f32[256]{0:T(256)S(1)}, f32[256]{0:T(256)}, u32[]{:S(2)}) copy-start(f32[256]{0:T(256)} %param.10) | copy-start | bytes 3076
  82.3 19.0 %copy-start.2 = (bf16[2304,256]{1,0:T(8,128)(2,1)S(1)}, bf16[2304,256]{1,0:T(8,128)(2,1)}, u32[]{:S(2)}) copy-start(bf16[2304,256]{1,0:T(8,128)(2,1)} %get-tuple-element.29.w_ref) | copy-start | bytes 3538948

commit v6 on v5

--- a/solution.py
+++ b/solution.py
@@ -253,16 +253,36 @@
     place = iota((16, length), 1)
     halves = [[], []]
     stats = [jnp.zeros((8, 128), f32)] * 2
+    tops, totals, pair_accs = [], [], []
+    for pair in (0, 2):
+        queries = [q_ref[pl.ds(b, 16, stride=4), :] for b in (pair, pair + 1)]
+        empty = jnp.zeros((16, 128), f32)
+        both = jnp.concatenate(
+            [
+                jnp.concatenate([queries[0], empty], axis=1),
+                jnp.concatenate([empty, queries[1]], axis=1),
+            ],
+            axis=0,
+        ).astype(bf16)
+        keys = jnp.concatenate([keys_ref[pair], keys_ref[pair + 1]], axis=1)
+        values = jnp.concatenate([values_ref[pair], values_ref[pair + 1]], axis=1)
+        scores = lax.dot_general(both, keys, NT, preferred_element_type=f32) * SCORE_SCALE
+        rounded = []
+        for k in range(2):
+            score = scores[16 * k : 16 * k + 16]
+            live = place < info_ref[pair + k]
+            top = jnp.max(jnp.where(live, score, -1e30), axis=1, keepdims=True)
+            weights = jnp.where(live, jnp.exp(score - top), 0.0)
+            tops.append(top)
+            totals.append(jnp.sum(weights, axis=1, keepdims=True))
+            rounded.append(weights.astype(bf16))
+        acc = jnp.dot(
+            jnp.concatenate(rounded, axis=0), values, preferred_element_type=f32
+        )
+        pair_accs += [acc[:16, :128], acc[16:, 128:]]
     for b in range(4):
         query = q_ref[pl.ds(b, 16, stride=4), :]
-        scores = lax.dot_general(
-            query.astype(bf16), keys_ref[b], NT, preferred_element_type=f32
-        ) * SCORE_SCALE
-        live = place < info_ref[b]
-        top = jnp.max(jnp.where(live, scores, -1e30), axis=1, keepdims=True)
-        weights = jnp.where(live, jnp.exp(scores - top), 0.0)
-        total = jnp.sum(weights, axis=1, keepdims=True)
-        acc = jnp.dot(weights.astype(bf16), values_ref[b], preferred_element_type=f32)
+        top, total, acc = tops[b], totals[b], pair_accs[b]
         fresh = [
             jnp.where(
                 owner,
@@ -364,7 +384,6 @@
     wanted = jnp.concatenate(
         [wanted.astype(f32), jnp.broadcast_to(out_scale[None, :], (8, 256))], axis=0
     )
-    other = lax.ppermute(wanted, "z_low", [(0, 1), (1, 0)])
 
     half_dim = HEAD_DIM // 2
     freqs = jnp.exp(
@@ -405,20 +424,16 @@
     for step in range(DECODE_STEPS):
         partial = exchange(partial, NEAR)
         if step == 0:
-            partial, other, info, cosines, sines = lax.optimization_barrier(
-                (partial, other, info, cosines, sines)
+            partial, wanted, info, cosines, sines = lax.optimization_barrier(
+                (partial, wanted, info, cosines, sines)
             )
-            w_out = call(
-                decode_out_kernel,
-                shape_of((512, 1024), bf16),
-                "decode_out",
-                (out_codes, out_scale.reshape(1, -1), other),
-                (info,),
-            )
+            other = lax.ppermute(wanted, "z_low", [(0, 1), (1, 0)])
         partial = call(pass_sum_kernel, shape_of((far, 8, 256)), "sum_near", (partial,))
         partial = exchange(partial, FAR)
         partial = call(pass_sum_kernel, shape_of((near, 8, 256)), "sum_far", (partial,))
         partial = exchange(partial, NEAR)
+        if step == 0:
+            partial, other = lax.optimization_barrier((partial, other))
         part, new_key, new_value = call(
             functools.partial(attend_kernel, features, step),
             (shape_of((near, 8, 640)), shape_of((8, 128)), shape_of((8, 128))),
@@ -429,6 +444,14 @@
         )
         fresh += (new_key, new_value)
         part = exchange(part, NEAR)
+        if step == 0:
+            w_out = call(
+                decode_out_kernel,
+                shape_of((512, 1024), bf16),
+                "decode_out",
+                (out_codes, out_scale.reshape(1, -1), other),
+                (info,),
+            )
         part = call(pass_merge_kernel, shape_of((far, 8, 640)), "merge_near", (part,))
         part = exchange(part, FAR)
         update = call(

time: 176 us -> 174 us (0.989)
  blocking collectives: 129 us -> 94.6 us
  starting transfers between devices: 12 us -> 29.3 us
  waiting for transfers between devices: 14.7 us -> 27.5 us
    all_to_all x10 -> x8, blocking collectives: 129 us -> 94.6 us  [exchange(): return lax.all_to_all(value, axes, split_axis=0, concat_axis=0, tiled=True)]
    all_to_all x2 -> x4, starting transfers between devices: 7.58 us -> 27 us  [exchange(): return lax.all_to_all(value, axes, split_axis=0, concat_axis=0, tiled=True)]
    all_to_all x2 -> x4, waiting for transfers between devices: 14.7 us -> 27.5 us  [exchange(): return lax.all_to_all(value, axes, split_axis=0, concat_axis=0, tiled=True)]
    ppermute x1, starting transfers between devices: 4.38 us -> 2.27 us  [shards(): other = lax.ppermute(wanted, 'z_low', [(0, 1), (1, 0)])]
  transfers between devices with their start and end apart: 3 -> 5, of which waited for: 2 -> 4; matrix products, arithmetic and copies ran while one was open for 0% -> 2% of each run, Pallas kernels for 3% -> 1%
where the time goes in v6:
time: 174 us; the launch traced here: 173 us
  blocking collectives  94.6 us (54%)
  starting transfers between devices  29.3 us (17%)
  waiting for transfers between devices  27.5 us (16%)
  Pallas kernels  15.8 us (9%)
  local copies, waits for them, and re-layouts  2.71 us (2%)
  other arithmetic  2.59 us (1%)
    all_to_all x8, blocking collectives, exchange(): return lax.all_to_all(value, axes, split_axis=0, concat_axis=0, tiled=True)  94.6 us
    all_to_all x4, waiting for transfers between devices, exchange(): return lax.all_to_all(value, axes, split_axis=0, concat_axis=0, tiled=True)  27.5 us
    all_to_all x4, starting transfers between devices, exchange(): return lax.all_to_all(value, axes, split_axis=0, concat_axis=0, tiled=True)  27 us
    pallas_call x14, Pallas kernels, call(): pl.pallas_call(kernel, out_shape=outs, in_specs=specs, out_specs=out_spec...  15.8 us
  transfers between devices with their start and end apart: 5, of which 4 were waited for; matrix products, arithmetic and copies ran while one was open for 2% of the time, Pallas kernels for 1%

profile of v6, /device:TPU:1, one launch (start us, length us, event | category | flops | bytes accessed | tf_op | source)
XLA Modules:
  0.0 172.6 jit_solution(998019600639710594)
XLA Ops:
  0.0 0.0 copy-start.6
  0.0 0.7 copy-done.8
  0.7 3.9 %decode_qkv.1 = (bf16[2304,256]{1,0:T(8,128)(2,1)}, f32[8,256]{1,0:T(8,128)S(1)}, f32[8,8,256]{2,1,0:T(8,128)}) custom-call(s32[576,256]{1,0:T(8,128)} %bitcast.23, f32[18,128]{1,0:T(8,128)} %bitcast.24, f32[1,256]{1,0:T(1,128)} %bitcast.21, bf16[4,256]{1,0:T(4,128)(2,1)S(1)} %copy-done.8), custom_call_target="tpu_custom_call" | custom-call | tf_op jit(solution)/shard_map/decode_qkv/pallas_call | solution.py:38
  4.6 6.4 %all-to-all-start = ((f32[8,8,256]{2,1,0:T(8,128)}), f32[8,8,256]{2,1,0:T(8,128)S(1)}, u32[]{:S(2)}, u32[]{:S(2)}) async-start(f32[8,8,256]{2,1,0:T(8,128)} %get-tuple-element.23), calls=%async_computation | async-start | bytes 131072 | tf_op jit(solution)/shard_map/all_to_all | solution.py:366
  11.0 0.7 add_convert_fusion
  11.7 0.7 broadcast_subtract_fusion
  12.3 1.0 dynamic-slice_convert_fusion
  13.3 0.1 multiply_sine_fusion
  13.4 0.1 fusion.4
  13.5 0.1 pad_add_fusion.info_ref
  13.6 0.0 copy-done.6
  13.6 2.6 %all-to-all-done.in_ref = f32[8,8,256]{2,1,0:T(8,128)S(1)} async-done(((f32[8,8,256]{2,1,0:T(8,128)}), f32[8,8,256]{2,1,0:T(8,128)S(1)}, u32[]{:S(2)}, u32[]{:S(2)}) %all-to-all-start) | async-done | bytes 65568 | tf_op jit(solution)/shard_map/all_to_all | solution.py:366
  16.2 0.6 sum_near.2
  16.8 13.9 %all-to-all-start.1 = ((f32[8,8,256]{2,1,0:T(8,128)}), f32[8,8,256]{2,1,0:T(8,128)S(1)}, u32[]{:S(2)}, u32[]{:S(2)}) async-start(f32[8,8,256]{2,1,0:T(8,128)} %sum_near.2), calls=%async_computation.1 | async-start | bytes 131072 | tf_op jit(solution)/shard_map/all_to_all | solution.py:366
  30.7 2.3 %collective-permute-start = (f32[264,256]{1,0:T(8,128)S(1)}, f32[264,256]{1,0:T(8,128)S(1)}, u32[]{:S(2)}, u32[]{:S(2)}) collective-permute-start(f32[264,256]{1,0:T(8,128)S(1)} %pad_maximum_fusion), channel_id=1, source_target_pairs={{0,32},{32,0},{1,33},{33,1},{2,34},{34,2},{3,35},{35,3},{4,36},{36... | collective-permute-start | bytes 811016 | tf_op jit(solution)/shard_map/ppermute | solution.py:430
  33.0 10.0 %all-to-all-done.1.in_ref = f32[8,8,256]{2,1,0:T(8,128)S(1)} async-done(((f32[8,8,256]{2,1,0:T(8,128)}), f32[8,8,256]{2,1,0:T(8,128)S(1)}, u32[]{:S(2)}, u32[]{:S(2)}) %all-to-all-start.1) | async-done | bytes 65568 | tf_op jit(solution)/shard_map/all_to_all | solution.py:366
  43.0 0.6 sum_far.2
  43.6 3.3 %all-to-all-start.2 = ((f32[8,8,256]{2,1,0:T(8,128)}), f32[8,8,256]{2,1,0:T(8,128)S(1)}, u32[]{:S(2)}, u32[]{:S(2)}) async-start(f32[8,8,256]{2,1,0:T(8,128)} %sum_far.2), calls=%async_computation.2 | async-start | bytes 131072 | tf_op jit(solution)/shard_map/all_to_all | solution.py:366
  47.0 0.0 collective-permute-done.other_ref
  47.0 0.0 copy-start.4
  47.0 5.1 %all-to-all-done.2.in_ref = f32[8,8,256]{2,1,0:T(8,128)S(1)} async-done(((f32[8,8,256]{2,1,0:T(8,128)}), f32[8,8,256]{2,1,0:T(8,128)S(1)}, u32[]{:S(2)}, u32[]{:S(2)}) %all-to-all-start.2) | async-done | bytes 65568 | tf_op jit(solution)/shard_map/all_to_all | solution.py:366
  52.1 0.0 copy-done
  52.1 0.0 copy-done.1
  52.1 1.9 %attend.2 = (f32[8,8,640]{2,1,0:T(8,128)S(1)}, f32[8,128]{1,0:T(8,128)S(1)}, f32[8,128]{1,0:T(8,128)S(1)}) custom-call(s32[6]{0:T(128)S(1)} %pad_add_fusion.info_ref, f32[8,8,256]{2,1,0:T(8,128)S(1)} %all-to-all-done.2.in_ref, f32[4,128]{1,0:T(4,128)S(1)} %get-tuple-element.28.cos_ref, f32[4,128]{1,0:T(4,128)S(1)} %get-tuple-element.29.sin_ref, ...), custom_call_target="tpu_custom_call" | custom-call | tf_op jit(solution)/shard_map/attend/pallas_call | solution.py:38
  54.0 8.0 %all_to_all.60.in_ref = f32[8,8,640]{2,1,0:T(8,128)S(1)} all-to-all(f32[8,8,640]{2,1,0:T(8,128)S(1)} %get-tuple-element.30), channel_id=1, replica_groups=mesh['z_high'=8,'z_low'=2,'y'=4,'head'=8] {'z_low','y'}, dimensions={0} | all-to-all | bytes 327680 | tf_op jit(solution)/shard_map/all_to_all | solution.py:366
  62.0 0.0 copy-done.4
  62.0 0.8 merge_near.2
  62.8 3.4 %all-to-all-start.4 = ((f32[8,8,640]{2,1,0:T(8,128)}), f32[8,8,640]{2,1,0:T(8,128)S(1)}, u32[]{:S(2)}, u32[]{:S(2)}) async-start(f32[8,8,640]{2,1,0:T(8,128)} %merge_near.2), calls=%async_computation.4 | async-start | bytes 327680 | tf_op jit(solution)/shard_map/all_to_all | solution.py:366
  66.2 0.0 copy-start.3
  66.2 1.0 copy-done.3
  67.2 1.0 copy-done.5
  68.2 1.9 %decode_out.1.w_ref = bf16[512,1024]{1,0:T(8,128)(2,1)S(1)} custom-call(s32[6]{0:T(128)S(1)} %pad_add_fusion.info_ref, s32[256,512]{1,0:T(8,128)S(1)} %copy-done.3, f32[1,256]{1,0:T(1,128)S(1)} %bitcast.20, f32[264,256]{1,0:T(8,128)S(1)} %copy-done.5), custom_call_target="tpu_custom_call" | custom-call | tf_op jit(solution)/shard_map/decode_out/pallas_call | solution.py:38
  70.0 9.8 %all-to-all-done.4.in_ref = f32[8,8,640]{2,1,0:T(8,128)S(1)} async-done(((f32[8,8,640]{2,1,0:T(8,128)}), f32[8,8,640]{2,1,0:T(8,128)S(1)}, u32[]{:S(2)}, u32[]{:S(2)}) %all-to-all-start.4) | async-done | bytes 163872 | tf_op jit(solution)/shard_map/all_to_all | solution.py:366
  79.9 1.2 finish.2
  81.1 17.5 %all_to_all.61.in_ref = f32[16,8,128]{2,1,0:T(8,128)S(1)} all-to-all(f32[16,8,128]{2,1,0:T(8,128)S(1)} %finish.2), channel_id=1, replica_groups=mesh['z_high'=8,'z_low'=2,'y'=4,'head'=8] {'z_low','head'}, dimensions={0} | all-to-all | bytes 131072 | tf_op jit(solution)/shard_map/all_to_all | solution.py:366
  98.6 0.0 copy-done.7
  98.6 0.0 copy-done.2
  98.6 0.6 next_step.1
  99.2 7.7 %all_to_all.62.in_ref = f32[8,8,256]{2,1,0:T(8,128)S(1)} all-to-all(f32[8,8,256]{2,1,0:T(8,128)S(1)} %get-tuple-element.34), channel_id=1, replica_groups=mesh['z_high'=8,'z_low'=2,'y'=4,'head'=8] {'z_low','y'}, dimensions={0} | all-to-all | bytes 131072 | tf_op jit(solution)/shard_map/all_to_all | solution.py:366
  106.9 14.7 %all_to_all.63.in_ref = f32[8,8,256]{2,1,0:T(8,128)S(1)} all-to-all(f32[8,8,256]{2,1,0:T(8,128)S(1)} %sum_near.3), channel_id=1, replica_groups=mesh['z_high'=8,'z_low'=2,'y'=4,'head'=8] {'z_high'}, dimensions={0} | all-to-all | bytes 131072 | tf_op jit(solution)/shard_map/all_to_all | solution.py:366
  121.6 7.6 %all_to_all.64.in_ref = f32[8,8,256]{2,1,0:T(8,128)S(1)} all-to-all(f32[8,8,256]{2,1,0:T(8,128)S(1)} %sum_far.3), channel_id=1, replica_groups=mesh['z_high'=8,'z_low'=2,'y'=4,'head'=8] {'z_low','y'}, dimensions={0} | all-to-all | bytes 131072 | tf_op jit(solution)/shard_map/all_to_all | solution.py:366
  129.2 2.3 %attend.3 = (f32[8,8,640]{2,1,0:T(8,128)S(1)}, f32[8,128]{1,0:T(8,128)}, f32[8,128]{1,0:T(8,128)}) custom-call(s32[6]{0:T(128)S(1)} %pad_add_fusion.info_ref, f32[8,8,256]{2,1,0:T(8,128)S(1)} %all_to_all.64.in_ref, f32[4,128]{1,0:T(4,128)S(1)} %get-tuple-element.35.cos_ref, f32[4,128]{1,0:T(4,128)S(1)} %get-tuple-element.36.sin_ref, ...), custom_call_target="tpu_custom_call" | custom-call | tf_op jit(solution)/shard_map/attend/pallas_call | solution.py:38
  131.5 8.0 %all_to_all.65.in_ref = f32[8,8,640]{2,1,0:T(8,128)S(1)} all-to-all(f32[8,8,640]{2,1,0:T(8,128)S(1)} %get-tuple-element.39), channel_id=1, replica_groups=mesh['z_high'=8,'z_low'=2,'y'=4,'head'=8] {'z_low','y'}, dimensions={0} | all-to-all | bytes 327680 | tf_op jit(solution)/shard_map/all_to_all | solution.py:366
  139.5 0.1 merge_near.3
  139.6 16.1 %all_to_all.66.in_ref = f32[8,8,640]{2,1,0:T(8,128)S(1)} all-to-all(f32[8,8,640]{2,1,0:T(8,128)S(1)} %merge_near.3), channel_id=1, replica_groups=mesh['z_high'=8,'z_low'=2,'y'=4,'head'=8] {'z_high'}, dimensions={0} | all-to-all | bytes 327680 | tf_op jit(solution)/shard_map/all_to_all | solution.py:366
  155.8 1.2 finish.3
  157.0 15.1 %all_to_all.67.in_ref = f32[16,8,128]{2,1,0:T(8,128)S(1)} all-to-all(f32[16,8,128]{2,1,0:T(8,128)S(1)} %finish.3), channel_id=1, replica_groups=mesh['z_high'=8,'z_low'=2,'y'=4,'head'=8] {'z_low','head'}, dimensions={0} | all-to-all | bytes 131072 | tf_op jit(solution)/shard_map/all_to_all | solution.py:366
  172.1 0.6 last.1
  (11 shorter events, 0.1 us)
Async XLA Ops:
  0.0 13.6 %copy-start.6 = (f32[256]{0:T(256)S(1)}, f32[256]{0:T(256)}, u32[]{:S(2)}) copy-start(f32[256]{0:T(256)} %param.14) | copy-start | bytes 3076
  0.0 0.7 copy-start.8
  0.7 51.4 %copy-start = (bf16[4,1024,1,128]{3,1,2,0:T(8,128)(2,1)S(1)}, bf16[4,1024,1,128]{3,1,2,0:T(8,128)(2,1)}, u32[]{:S(2)}) copy-start(bf16[4,1024,1,128]{3,1,2,0:T(8,128)(2,1)} %param.15) | copy-start | bytes 3145732
  0.7 51.4 %copy-start.1 = (bf16[4,1024,1,128]{3,1,2,0:T(8,128)(2,1)S(1)}, bf16[4,1024,1,128]{3,1,2,0:T(8,128)(2,1)}, u32[]{:S(2)}) copy-start(bf16[4,1024,1,128]{3,1,2,0:T(8,128)(2,1)} %param.16) | copy-start | bytes 3145732
  4.6 11.6 %all-to-all-start = ((f32[8,8,256]{2,1,0:T(8,128)}), f32[8,8,256]{2,1,0:T(8,128)S(1)}, u32[]{:S(2)}, u32[]{:S(2)}) async-start(f32[8,8,256]{2,1,0:T(8,128)} %get-tuple-element.23), calls=%async_computation | async-start | bytes 131072 | tf_op jit(solution)/shard_map/all_to_all | solution.py:366
  16.8 26.1 %all-to-all-start.1 = ((f32[8,8,256]{2,1,0:T(8,128)}), f32[8,8,256]{2,1,0:T(8,128)S(1)}, u32[]{:S(2)}, u32[]{:S(2)}) async-start(f32[8,8,256]{2,1,0:T(8,128)} %sum_near.2), calls=%async_computation.1 | async-start | bytes 131072 | tf_op jit(solution)/shard_map/all_to_all | solution.py:366
  30.7 16.2 %collective-permute-start = (f32[264,256]{1,0:T(8,128)S(1)}, f32[264,256]{1,0:T(8,128)S(1)}, u32[]{:S(2)}, u32[]{:S(2)}) collective-permute-start(f32[264,256]{1,0:T(8,128)S(1)} %pad_maximum_fusion), channel_id=1, source_target_pairs={{0,32},{32,0},{1,33},{33,1},{2,34},{34,2},{3,35},{35,3},{4,36},{36... | collective-permute-start | bytes 811016 | tf_op jit(solution)/shard_map/ppermute | solution.py:430
  43.6 8.5 %all-to-all-start.2 = ((f32[8,8,256]{2,1,0:T(8,128)}), f32[8,8,256]{2,1,0:T(8,128)S(1)}, u32[]{:S(2)}, u32[]{:S(2)}) async-start(f32[8,8,256]{2,1,0:T(8,128)} %sum_far.2), calls=%async_computation.2 | async-start | bytes 131072 | tf_op jit(solution)/shard_map/all_to_all | solution.py:366
  47.0 15.0 %copy-start.4 = (f32[264,256]{1,0:T(8,128)}, f32[264,256]{1,0:T(8,128)S(1)}, u32[]{:S(2)}) copy-start(f32[264,256]{1,0:T(8,128)S(1)} %collective-permute-done.other_ref) | copy-start | bytes 811012
  62.8 17.1 %all-to-all-start.4 = ((f32[8,8,640]{2,1,0:T(8,128)}), f32[8,8,640]{2,1,0:T(8,128)S(1)}, u32[]{:S(2)}, u32[]{:S(2)}) async-start(f32[8,8,640]{2,1,0:T(8,128)} %merge_near.2), calls=%async_computation.4 | async-start | bytes 327680 | tf_op jit(solution)/shard_map/all_to_all | solution.py:366
  66.2 1.0 copy-start.3
  67.2 1.0 copy-start.5
  68.2 30.5 %copy-start.7 = (f32[256]{0:T(256)S(1)}, f32[256]{0:T(256)}, u32[]{:S(2)}) copy-start(f32[256]{0:T(256)} %param.10) | copy-start | bytes 3076
  79.9 18.8 %copy-start.2 = (bf16[2304,256]{1,0:T(8,128)(2,1)S(1)}, bf16[2304,256]{1,0:T(8,128)(2,1)}, u32[]{:S(2)}) copy-start(bf16[2304,256]{1,0:T(8,128)(2,1)} %get-tuple-element.33.w_ref) | copy-start | bytes 3538948

commit v7 on v6

--- a/solution.py
+++ b/solution.py
@@ -86,10 +86,12 @@
                 out_ref[s * copies + j, :, k * 128 : k * 128 + 128] = halves[s][k]
 
 
-def project(hidden, gain, weights, out_ref):
+def norm(hidden, gain):
     squares = jnp.sum(hidden * hidden, axis=1, keepdims=True)
-    normed = (hidden * gain).astype(bf16)
-    y = lax.dot_general(normed, weights, NT, preferred_element_type=f32)
+    return (hidden * gain).astype(bf16), squares
+
+
+def pack(y, squares, out_ref):
     first = iota((8, 128), 0) < 4
     few = iota((8, 128), 1) < 16
     spread = jnp.broadcast_to(squares, (8, 128))
@@ -117,13 +119,18 @@
     scale_copy = pltpu.make_async_copy(scale_hbm, scale_ref, scale_sem)
     gain_copy = pltpu.make_async_copy(gain_hbm, gain_ref, gain_sem)
     scale_copy.start()
+    gain_copy.start()
     for copy in copies:
         copy.start()
-    gain_copy.start()
+    hidden = hidden_ref[...].astype(f32)
+    hidden = jnp.concatenate([hidden, hidden], axis=0)
+    hid_ref[...] = hidden
     scale_copy.wait()
+    gain_copy.wait()
+    normed, squares = norm(hidden, gain_ref[...])
     lane = iota((32, 128), 1)
     word = iota((32, 128), 0)
-    kept = []
+    kept, products = [], []
     for tile in range(18):
         if tile * 32 % chunk_rows == 0:
             copies[tile * 32 // chunk_rows].wait()
@@ -142,11 +149,10 @@
             rows = pl.ds(done * 4 * chunk_rows, 4 * chunk_rows)
             kept.append(pltpu.make_async_copy(w_ref.at[rows], w_hbm.at[rows], w_sems.at[done]))
             kept[-1].start()
-    hidden = hidden_ref[...].astype(f32)
-    hidden = jnp.concatenate([hidden, hidden], axis=0)
-    hid_ref[...] = hidden
-    gain_copy.wait()
-    project(hidden, gain_ref[...], w_ref[...], out_ref)
+            products.append(
+                lax.dot_general(normed, w_ref[rows, :], NT, preferred_element_type=f32)
+            )
+    pack(jnp.concatenate(products, axis=1), squares, out_ref)
     for copy in kept:
         copy.wait()
 
@@ -249,18 +255,33 @@
     new_keys = [refs[2 * u][...] for u in range(earlier)] + [new_key]
     new_values = [refs[2 * u + 1][...] for u in range(earlier)] + [new_value]
     owner = info_ref[4] == 0
+
+    def by_head(rows):
+        return jnp.concatenate(
+            [jnp.broadcast_to(rows[b : b + 1, :], (16, 128)) for b in range(4)], axis=0
+        )
+
+    by_sequence = [q_ref[pl.ds(b, 16, stride=4), :] for b in range(4)]
+    queries = jnp.concatenate(by_sequence, axis=0)
+    fresh = [
+        jnp.where(
+            owner,
+            jnp.sum(queries * by_head(key), axis=1, keepdims=True) * SCORE_SCALE,
+            -1e30,
+        )
+        for key in new_keys
+    ]
     length = keys_ref.shape[1]
     place = iota((16, length), 1)
     halves = [[], []]
     stats = [jnp.zeros((8, 128), f32)] * 2
     tops, totals, pair_accs = [], [], []
     for pair in (0, 2):
-        queries = [q_ref[pl.ds(b, 16, stride=4), :] for b in (pair, pair + 1)]
         empty = jnp.zeros((16, 128), f32)
         both = jnp.concatenate(
             [
-                jnp.concatenate([queries[0], empty], axis=1),
-                jnp.concatenate([empty, queries[1]], axis=1),
+                jnp.concatenate([by_sequence[pair], empty], axis=1),
+                jnp.concatenate([empty, by_sequence[pair + 1]], axis=1),
             ],
             axis=0,
         ).astype(bf16)
@@ -280,27 +301,19 @@
             jnp.concatenate(rounded, axis=0), values, preferred_element_type=f32
         )
         pair_accs += [acc[:16, :128], acc[16:, 128:]]
+    top = jnp.concatenate(tops, axis=0)
+    peak = functools.reduce(jnp.maximum, fresh, top)
+    factor = jnp.exp(top - peak)
+    total = jnp.concatenate(totals, axis=0) * factor
+    acc = jnp.concatenate(pair_accs, axis=0) * factor
+    for score, value in zip(fresh, new_values):
+        weight = jnp.where(owner, jnp.exp(score - peak), 0.0)
+        total = total + weight
+        acc = acc + weight * by_head(value)
     for b in range(4):
-        query = q_ref[pl.ds(b, 16, stride=4), :]
-        top, total, acc = tops[b], totals[b], pair_accs[b]
-        fresh = [
-            jnp.where(
-                owner,
-                jnp.sum(query * key[b : b + 1, :], axis=1, keepdims=True) * SCORE_SCALE,
-                -1e30,
-            )
-            for key in new_keys
-        ]
-        peak = functools.reduce(jnp.maximum, fresh, top)
-        factor = jnp.exp(top - peak)
-        total = total * factor
-        acc = acc * factor
-        for score, value in zip(fresh, new_values):
-            weight = jnp.where(owner, jnp.exp(score - peak), 0.0)
-            total = total + weight
-            acc = acc + weight * value[b : b + 1, :]
         for s in range(2):
-            rows = slice(8 * s, 8 * s + 8)
+            at = b * 16 + 8 * s
+            rows = slice(at, at + 8)
             halves[s].append(acc[rows])
             stats[s] = jnp.where(lane == b, peak[rows], stats[s])
             stats[s] = jnp.where(lane == 4 + b, total[rows], stats[s])
@@ -355,7 +368,8 @@
 def next_kernel(in_ref, hid_ref, gain_ref, w_ref, new_ref, out_ref):
     hidden = updated(in_ref, hid_ref).astype(f32)
     new_ref[...] = hidden
-    project(hidden, gain_ref[...], w_ref[...], out_ref)
+    normed, squares = norm(hidden, gain_ref[...])
+    pack(lax.dot_general(normed, w_ref[...], NT, preferred_element_type=f32), squares, out_ref)
 
 
 def last_kernel(in_ref, hid_ref, out_ref):
@@ -433,7 +447,14 @@
         partial = call(pass_sum_kernel, shape_of((near, 8, 256)), "sum_far", (partial,))
         partial = exchange(partial, NEAR)
         if step == 0:
-            partial, other = lax.optimization_barrier((partial, other))
+            w_out = call(
+                decode_out_kernel,
+                shape_of((512, 1024), bf16),
+                "decode_out",
+                (out_codes, out_scale.reshape(1, -1), other),
+                (info,),
+            )
+            partial, w_out = lax.optimization_barrier((partial, w_out))
         part, new_key, new_value = call(
             functools.partial(attend_kernel, features, step),
             (shape_of((near, 8, 640)), shape_of((8, 128)), shape_of((8, 128))),
@@ -444,14 +465,6 @@
         )
         fresh += (new_key, new_value)
         part = exchange(part, NEAR)
-        if step == 0:
-            w_out = call(
-                decode_out_kernel,
-                shape_of((512, 1024), bf16),
-                "decode_out",
-                (out_codes, out_scale.reshape(1, -1), other),
-                (info,),
-            )
         part = call(pass_merge_kernel, shape_of((far, 8, 640)), "merge_near", (part,))
         part = exchange(part, FAR)
         update = call(

time: 174 us -> 173 us (level)
  blocking collectives: 94.6 us -> 111 us
  waiting for transfers between devices: 27.5 us -> 14.7 us
  starting transfers between devices: 29.3 us -> 26 us
    all_to_all x8 -> x9, blocking collectives: 94.6 us -> 111 us  [exchange(): return lax.all_to_all(value, axes, split_axis=0, concat_axis=0, tiled=True)]
    all_to_all x4 -> x3, waiting for transfers between devices: 27.5 us -> 14.7 us  [exchange(): return lax.all_to_all(value, axes, split_axis=0, concat_axis=0, tiled=True)]
    all_to_all x4 -> x3, starting transfers between devices: 27 us -> 23.8 us  [exchange(): return lax.all_to_all(value, axes, split_axis=0, concat_axis=0, tiled=True)]
  transfers between devices with their start and end apart: 5 -> 4, of which waited for: 4 -> 3; matrix products, arithmetic and copies ran while one was open for 2% -> 2% of each run, Pallas kernels for 1% -> 1%
where the time goes in v7:
time: 173 us; the launch traced here: 172 us
  blocking collectives  111 us (64%)
  starting transfers between devices  26 us (15%)
  Pallas kernels  15.7 us (9%)
  waiting for transfers between devices  14.7 us (8%)
  other arithmetic  2.6 us (2%)
  local copies, waits for them, and re-layouts  1.76 us (1%)
    all_to_all x9, blocking collectives, exchange(): return lax.all_to_all(value, axes, split_axis=0, concat_axis=0, tiled=True)  111 us
    all_to_all x3, starting transfers between devices, exchange(): return lax.all_to_all(value, axes, split_axis=0, concat_axis=0, tiled=True)  23.8 us
    pallas_call x14, Pallas kernels, call(): pl.pallas_call(kernel, out_shape=outs, in_specs=specs, out_specs=out_spec...  15.7 us
    all_to_all x3, waiting for transfers between devices, exchange(): return lax.all_to_all(value, axes, split_axis=0, concat_axis=0, tiled=True)  14.7 us
  transfers between devices with their start and end apart: 4, of which 3 were waited for; matrix products, arithmetic and copies ran while one was open for 2% of the time, Pallas kernels for 1%

profile of v7, /device:TPU:1, one launch (start us, length us, event | category | flops | bytes accessed | tf_op | source)
XLA Modules:
  0.0 171.8 jit_solution(4462639399327028835)
XLA Ops:
  0.0 0.0 copy-start.4
  0.0 0.0 copy-start.6
  0.0 0.7 copy-done.6
  0.7 4.4 %decode_qkv.1 = (bf16[2304,256]{1,0:T(8,128)(2,1)}, f32[8,256]{1,0:T(8,128)S(1)}, f32[8,8,256]{2,1,0:T(8,128)}) custom-call(s32[576,256]{1,0:T(8,128)} %bitcast.23, f32[18,128]{1,0:T(8,128)} %bitcast.24, f32[1,256]{1,0:T(1,128)} %bitcast.21, bf16[4,256]{1,0:T(4,128)(2,1)S(1)} %copy-done.6), custom_call_target="tpu_custom_call" | custom-call | tf_op jit(solution)/shard_map/decode_qkv/pallas_call | solution.py:38
  5.1 6.4 %all-to-all-start = ((f32[8,8,256]{2,1,0:T(8,128)}), f32[8,8,256]{2,1,0:T(8,128)S(1)}, u32[]{:S(2)}, u32[]{:S(2)}) async-start(f32[8,8,256]{2,1,0:T(8,128)} %get-tuple-element.23), calls=%async_computation | async-start | bytes 131072 | tf_op jit(solution)/shard_map/all_to_all | solution.py:380
  11.5 0.7 add_convert_fusion
  12.2 0.7 broadcast_subtract_fusion
  12.9 0.1 multiply_sine_fusion
  13.0 1.0 dynamic-slice_convert_fusion
  14.0 0.1 fusion.4
  14.0 0.1 pad_add_fusion.info_ref
  14.1 0.0 copy-done.4
  14.2 2.6 %all-to-all-done.in_ref = f32[8,8,256]{2,1,0:T(8,128)S(1)} async-done(((f32[8,8,256]{2,1,0:T(8,128)}), f32[8,8,256]{2,1,0:T(8,128)S(1)}, u32[]{:S(2)}, u32[]{:S(2)}) %all-to-all-start) | async-done | bytes 65568 | tf_op jit(solution)/shard_map/all_to_all | solution.py:380
  16.7 0.0 copy-start
  16.7 0.6 sum_near.2
  17.4 14.0 %all-to-all-start.1 = ((f32[8,8,256]{2,1,0:T(8,128)}), f32[8,8,256]{2,1,0:T(8,128)S(1)}, u32[]{:S(2)}, u32[]{:S(2)}) async-start(f32[8,8,256]{2,1,0:T(8,128)} %sum_near.2), calls=%async_computation.1 | async-start | bytes 131072 | tf_op jit(solution)/shard_map/all_to_all | solution.py:380
  31.4 2.3 %collective-permute-start = (f32[264,256]{1,0:T(8,128)S(1)}, f32[264,256]{1,0:T(8,128)S(1)}, u32[]{:S(2)}, u32[]{:S(2)}) collective-permute-start(f32[264,256]{1,0:T(8,128)S(1)} %pad_maximum_fusion), channel_id=1, source_target_pairs={{0,32},{32,0},{1,33},{33,1},{2,34},{34,2},{3,35},{35,3},{4,36},{36... | collective-permute-start | bytes 811016 | tf_op jit(solution)/shard_map/ppermute | solution.py:444
  33.7 10.0 %all-to-all-done.1.in_ref = f32[8,8,256]{2,1,0:T(8,128)S(1)} async-done(((f32[8,8,256]{2,1,0:T(8,128)}), f32[8,8,256]{2,1,0:T(8,128)S(1)}, u32[]{:S(2)}, u32[]{:S(2)}) %all-to-all-start.1) | async-done | bytes 65568 | tf_op jit(solution)/shard_map/all_to_all | solution.py:380
  43.6 0.6 sum_far.2
  44.3 3.3 %all-to-all-start.2 = ((f32[8,8,256]{2,1,0:T(8,128)}), f32[8,8,256]{2,1,0:T(8,128)S(1)}, u32[]{:S(2)}, u32[]{:S(2)}) async-start(f32[8,8,256]{2,1,0:T(8,128)} %sum_far.2), calls=%async_computation.2 | async-start | bytes 131072 | tf_op jit(solution)/shard_map/all_to_all | solution.py:380
  47.6 0.0 collective-permute-done.other_ref
  47.6 0.0 copy-start.3
  47.6 1.0 copy-done.3
  48.7 1.9 %decode_out.1.w_ref = bf16[512,1024]{1,0:T(8,128)(2,1)S(1)} custom-call(s32[6]{0:T(128)S(1)} %pad_add_fusion.info_ref, s32[256,512]{1,0:T(8,128)S(1)} %copy-done.3, f32[1,256]{1,0:T(1,128)S(1)} %bitcast.20, f32[264,256]{1,0:T(8,128)S(1)} %collective-permute-done.other_ref), custom_call_target="tpu_custom_call" | custom-call | tf_op jit(solution)/shard_map/decode_out/pallas_call | solution.py:38
  50.5 2.2 %all-to-all-done.2.in_ref = f32[8,8,256]{2,1,0:T(8,128)S(1)} async-done(((f32[8,8,256]{2,1,0:T(8,128)}), f32[8,8,256]{2,1,0:T(8,128)S(1)}, u32[]{:S(2)}, u32[]{:S(2)}) %all-to-all-start.2) | async-done | bytes 65568 | tf_op jit(solution)/shard_map/all_to_all | solution.py:380
  52.7 0.0 copy-done
  52.8 0.0 copy-done.1
  52.8 1.9 %attend.2 = (f32[8,8,640]{2,1,0:T(8,128)S(1)}, f32[8,128]{1,0:T(8,128)S(1)}, f32[8,128]{1,0:T(8,128)S(1)}) custom-call(s32[6]{0:T(128)S(1)} %pad_add_fusion.info_ref, f32[8,8,256]{2,1,0:T(8,128)S(1)} %all-to-all-done.2.in_ref, f32[4,128]{1,0:T(4,128)S(1)} %get-tuple-element.28.cos_ref, f32[4,128]{1,0:T(4,128)S(1)} %get-tuple-element.29.sin_ref, ...), custom_call_target="tpu_custom_call" | custom-call | tf_op jit(solution)/shard_map/attend/pallas_call | solution.py:38
  54.7 0.0 copy-start.2
  54.7 0.0 copy-start.5
  54.7 8.4 %all_to_all.60.in_ref = f32[8,8,640]{2,1,0:T(8,128)S(1)} all-to-all(f32[8,8,640]{2,1,0:T(8,128)S(1)} %get-tuple-element.30), channel_id=1, replica_groups=mesh['z_high'=8,'z_low'=2,'y'=4,'head'=8] {'z_low','y'}, dimensions={0} | all-to-all | bytes 327680 | tf_op jit(solution)/shard_map/all_to_all | solution.py:380
  63.1 0.1 merge_near.2
  63.2 16.3 %all_to_all.61.in_ref = f32[8,8,640]{2,1,0:T(8,128)S(1)} all-to-all(f32[8,8,640]{2,1,0:T(8,128)S(1)} %merge_near.2), channel_id=1, replica_groups=mesh['z_high'=8,'z_low'=2,'y'=4,'head'=8] {'z_high'}, dimensions={0} | all-to-all | bytes 327680 | tf_op jit(solution)/shard_map/all_to_all | solution.py:380
  79.5 1.2 finish.2
  80.8 16.9 %all_to_all.62.in_ref = f32[16,8,128]{2,1,0:T(8,128)S(1)} all-to-all(f32[16,8,128]{2,1,0:T(8,128)S(1)} %finish.2), channel_id=1, replica_groups=mesh['z_high'=8,'z_low'=2,'y'=4,'head'=8] {'z_low','head'}, dimensions={0} | all-to-all | bytes 131072 | tf_op jit(solution)/shard_map/all_to_all | solution.py:380
  97.7 0.0 copy-done.2
  97.7 0.0 copy-done.5
  97.7 0.6 next_step.1
  98.2 7.6 %all_to_all.63.in_ref = f32[8,8,256]{2,1,0:T(8,128)S(1)} all-to-all(f32[8,8,256]{2,1,0:T(8,128)S(1)} %get-tuple-element.34), channel_id=1, replica_groups=mesh['z_high'=8,'z_low'=2,'y'=4,'head'=8] {'z_low','y'}, dimensions={0} | all-to-all | bytes 131072 | tf_op jit(solution)/shard_map/all_to_all | solution.py:380
  105.9 14.9 %all_to_all.64.in_ref = f32[8,8,256]{2,1,0:T(8,128)S(1)} all-to-all(f32[8,8,256]{2,1,0:T(8,128)S(1)} %sum_near.3), channel_id=1, replica_groups=mesh['z_high'=8,'z_low'=2,'y'=4,'head'=8] {'z_high'}, dimensions={0} | all-to-all | bytes 131072 | tf_op jit(solution)/shard_map/all_to_all | solution.py:380
  120.7 7.6 %all_to_all.65.in_ref = f32[8,8,256]{2,1,0:T(8,128)S(1)} all-to-all(f32[8,8,256]{2,1,0:T(8,128)S(1)} %sum_far.3), channel_id=1, replica_groups=mesh['z_high'=8,'z_low'=2,'y'=4,'head'=8] {'z_low','y'}, dimensions={0} | all-to-all | bytes 131072 | tf_op jit(solution)/shard_map/all_to_all | solution.py:380
  128.3 2.3 %attend.3 = (f32[8,8,640]{2,1,0:T(8,128)S(1)}, f32[8,128]{1,0:T(8,128)}, f32[8,128]{1,0:T(8,128)}) custom-call(s32[6]{0:T(128)S(1)} %pad_add_fusion.info_ref, f32[8,8,256]{2,1,0:T(8,128)S(1)} %all_to_all.65.in_ref, f32[4,128]{1,0:T(4,128)S(1)} %get-tuple-element.35.cos_ref, f32[4,128]{1,0:T(4,128)S(1)} %get-tuple-element.36.sin_ref, ...), custom_call_target="tpu_custom_call" | custom-call | tf_op jit(solution)/shard_map/attend/pallas_call | solution.py:38
  130.6 8.0 %all_to_all.66.in_ref = f32[8,8,640]{2,1,0:T(8,128)S(1)} all-to-all(f32[8,8,640]{2,1,0:T(8,128)S(1)} %get-tuple-element.39), channel_id=1, replica_groups=mesh['z_high'=8,'z_low'=2,'y'=4,'head'=8] {'z_low','y'}, dimensions={0} | all-to-all | bytes 327680 | tf_op jit(solution)/shard_map/all_to_all | solution.py:380
  138.6 0.1 merge_near.3
  138.8 16.1 %all_to_all.67.in_ref = f32[8,8,640]{2,1,0:T(8,128)S(1)} all-to-all(f32[8,8,640]{2,1,0:T(8,128)S(1)} %merge_near.3), channel_id=1, replica_groups=mesh['z_high'=8,'z_low'=2,'y'=4,'head'=8] {'z_high'}, dimensions={0} | all-to-all | bytes 327680 | tf_op jit(solution)/shard_map/all_to_all | solution.py:380
  154.9 1.2 finish.3
  156.1 15.1 %all_to_all.68.in_ref = f32[16,8,128]{2,1,0:T(8,128)S(1)} all-to-all(f32[16,8,128]{2,1,0:T(8,128)S(1)} %finish.3), channel_id=1, replica_groups=mesh['z_high'=8,'z_low'=2,'y'=4,'head'=8] {'z_low','head'}, dimensions={0} | all-to-all | bytes 131072 | tf_op jit(solution)/shard_map/all_to_all | solution.py:380
  171.2 0.6 last.1
  (6 shorter events, 0.1 us)
Async XLA Ops:
  0.0 14.1 %copy-start.4 = (f32[256]{0:T(256)S(1)}, f32[256]{0:T(256)}, u32[]{:S(2)}) copy-start(f32[256]{0:T(256)} %param.14) | copy-start | bytes 3076
  0.0 0.7 copy-start.6
  5.1 11.6 %all-to-all-start = ((f32[8,8,256]{2,1,0:T(8,128)}), f32[8,8,256]{2,1,0:T(8,128)S(1)}, u32[]{:S(2)}, u32[]{:S(2)}) async-start(f32[8,8,256]{2,1,0:T(8,128)} %get-tuple-element.23), calls=%async_computation | async-start | bytes 131072 | tf_op jit(solution)/shard_map/all_to_all | solution.py:380
  16.7 36.0 %copy-start = (bf16[4,1024,1,128]{3,1,2,0:T(8,128)(2,1)S(1)}, bf16[4,1024,1,128]{3,1,2,0:T(8,128)(2,1)}, u32[]{:S(2)}) copy-start(bf16[4,1024,1,128]{3,1,2,0:T(8,128)(2,1)} %param.15) | copy-start | bytes 3145732
  16.7 36.0 %copy-start.1 = (bf16[4,1024,1,128]{3,1,2,0:T(8,128)(2,1)S(1)}, bf16[4,1024,1,128]{3,1,2,0:T(8,128)(2,1)}, u32[]{:S(2)}) copy-start(bf16[4,1024,1,128]{3,1,2,0:T(8,128)(2,1)} %param.16) | copy-start | bytes 3145732
  17.4 26.3 %all-to-all-start.1 = ((f32[8,8,256]{2,1,0:T(8,128)}), f32[8,8,256]{2,1,0:T(8,128)S(1)}, u32[]{:S(2)}, u32[]{:S(2)}) async-start(f32[8,8,256]{2,1,0:T(8,128)} %sum_near.2), calls=%async_computation.1 | async-start | bytes 131072 | tf_op jit(solution)/shard_map/all_to_all | solution.py:380
  31.4 16.2 %collective-permute-start = (f32[264,256]{1,0:T(8,128)S(1)}, f32[264,256]{1,0:T(8,128)S(1)}, u32[]{:S(2)}, u32[]{:S(2)}) collective-permute-start(f32[264,256]{1,0:T(8,128)S(1)} %pad_maximum_fusion), channel_id=1, source_target_pairs={{0,32},{32,0},{1,33},{33,1},{2,34},{34,2},{3,35},{35,3},{4,36},{36... | collective-permute-start | bytes 811016 | tf_op jit(solution)/shard_map/ppermute | solution.py:444
  44.3 8.5 %all-to-all-start.2 = ((f32[8,8,256]{2,1,0:T(8,128)}), f32[8,8,256]{2,1,0:T(8,128)S(1)}, u32[]{:S(2)}, u32[]{:S(2)}) async-start(f32[8,8,256]{2,1,0:T(8,128)} %sum_far.2), calls=%async_computation.2 | async-start | bytes 131072 | tf_op jit(solution)/shard_map/all_to_all | solution.py:380
  47.6 1.0 copy-start.3
  54.7 43.0 %copy-start.2 = (bf16[2304,256]{1,0:T(8,128)(2,1)S(1)}, bf16[2304,256]{1,0:T(8,128)(2,1)}, u32[]{:S(2)}) copy-start(bf16[2304,256]{1,0:T(8,128)(2,1)} %get-tuple-element.33.w_ref) | copy-start | bytes 3538948
  54.7 43.0 %copy-start.5 = (f32[256]{0:T(256)S(1)}, f32[256]{0:T(256)}, u32[]{:S(2)}) copy-start(f32[256]{0:T(256)} %param.10) | copy-start | bytes 3076

commit v8 on v7

--- a/solution.py
+++ b/solution.py
@@ -86,12 +86,10 @@
                 out_ref[s * copies + j, :, k * 128 : k * 128 + 128] = halves[s][k]
 
 
-def norm(hidden, gain):
+def project(hidden, gain, weights, out_ref):
     squares = jnp.sum(hidden * hidden, axis=1, keepdims=True)
-    return (hidden * gain).astype(bf16), squares
-
-
-def pack(y, squares, out_ref):
+    normed = (hidden * gain).astype(bf16)
+    y = lax.dot_general(normed, weights, NT, preferred_element_type=f32)
     first = iota((8, 128), 0) < 4
     few = iota((8, 128), 1) < 16
     spread = jnp.broadcast_to(squares, (8, 128))
@@ -105,9 +103,8 @@
         out_ref[p, :, 128:] = jnp.where(few, tail, spread)
 
 
-def decode_qkv_kernel(codes_hbm, scale_hbm, gain_hbm, hidden_ref, w_hbm, hid_ref, out_ref,
-                      codes_ref, scale_ref, gain_ref, w_ref, code_sems, scale_sem, gain_sem,
-                      w_sems):
+def decode_qkv_kernel(codes_hbm, scale_hbm, gain_hbm, hidden_ref, w_ref, hid_ref, out_ref,
+                      codes_ref, scale_ref, gain_ref, code_sems, scale_sem, gain_sem):
     chunks = code_sems.shape[0]
     chunk_rows = codes_ref.shape[0] // chunks
     copies = []
@@ -122,15 +119,9 @@
     gain_copy.start()
     for copy in copies:
         copy.start()
-    hidden = hidden_ref[...].astype(f32)
-    hidden = jnp.concatenate([hidden, hidden], axis=0)
-    hid_ref[...] = hidden
     scale_copy.wait()
-    gain_copy.wait()
-    normed, squares = norm(hidden, gain_ref[...])
     lane = iota((32, 128), 1)
     word = iota((32, 128), 0)
-    kept, products = [], []
     for tile in range(18):
         if tile * 32 % chunk_rows == 0:
             copies[tile * 32 // chunk_rows].wait()
@@ -144,17 +135,17 @@
             values = byte_sum((window >> (8 - 2 * r)) & 0xFFFF) * column
             at = tile * 128 + r * 32
             w_ref[at : at + 32, :] = values.astype(bf16)
-        if (tile + 1) * 32 % chunk_rows == 0:
-            done = tile * 32 // chunk_rows
-            rows = pl.ds(done * 4 * chunk_rows, 4 * chunk_rows)
-            kept.append(pltpu.make_async_copy(w_ref.at[rows], w_hbm.at[rows], w_sems.at[done]))
-            kept[-1].start()
-            products.append(
-                lax.dot_general(normed, w_ref[rows, :], NT, preferred_element_type=f32)
-            )
-    pack(jnp.concatenate(products, axis=1), squares, out_ref)
-    for copy in kept:
-        copy.wait()
+    hidden = hidden_ref[...].astype(f32)
+    hidden = jnp.concatenate([hidden, hidden], axis=0)
+    hid_ref[...] = hidden
+    gain_copy.wait()
+    project(hidden, gain_ref[...], w_ref[...], out_ref)
+
+
+def keep_kernel(w_ref, kept_ref, sem):
+    copy = pltpu.make_async_copy(w_ref, kept_ref, sem)
+    copy.start()
+    copy.wait()
 
 
 def decode_out_kernel(info_ref, codes_ref, scale_ref, other_ref, w_ref):
@@ -368,8 +359,7 @@
 def next_kernel(in_ref, hid_ref, gain_ref, w_ref, new_ref, out_ref):
     hidden = updated(in_ref, hid_ref).astype(f32)
     new_ref[...] = hidden
-    normed, squares = norm(hidden, gain_ref[...])
-    pack(lax.dot_general(normed, w_ref[...], NT, preferred_element_type=f32), squares, out_ref)
+    project(hidden, gain_ref[...], w_ref[...], out_ref)
 
 
 def last_kernel(in_ref, hid_ref, out_ref):
@@ -414,7 +404,7 @@
 
     w_qkv, hidden, partial = call(
         decode_qkv_kernel,
-        (pltpu.HBM((2304, 256), bf16), shape_of((8, 256)), shape_of((near, 8, 256))),
+        (shape_of((2304, 256), bf16), shape_of((8, 256)), shape_of((near, 8, 256))),
         "decode_qkv",
         (hidden_in,),
         remote=(qkv_codes.T, qkv_scale.reshape(18, 128), gain),
@@ -422,24 +412,25 @@
             pltpu.VMEM((576, 256), jnp.int32),
             pltpu.VMEM((18, 128), f32),
             pltpu.VMEM((1, 256), f32),
-            pltpu.VMEM((2304, 256), bf16),
             pltpu.SemaphoreType.DMA((6,)),
             pltpu.SemaphoreType.DMA,
             pltpu.SemaphoreType.DMA,
-            pltpu.SemaphoreType.DMA((6,)),
         ),
-        out_specs=(
-            pl.BlockSpec(memory_space=pltpu.HBM),
-            pl.BlockSpec(memory_space=pltpu.VMEM),
-            pl.BlockSpec(memory_space=pltpu.VMEM),
-        ),
+    )
+    w_qkv = call(
+        keep_kernel,
+        pltpu.HBM((2304, 256), bf16),
+        "keep",
+        (w_qkv,),
+        scratch=(pltpu.SemaphoreType.DMA,),
+        out_specs=pl.BlockSpec(memory_space=pltpu.HBM),
     )
     fresh = ()
     for step in range(DECODE_STEPS):
         partial = exchange(partial, NEAR)
         if step == 0:
-            partial, wanted, info, cosines, sines = lax.optimization_barrier(
-                (partial, wanted, info, cosines, sines)
+            partial, w_qkv, wanted, info, cosines, sines = lax.optimization_barrier(
+                (partial, w_qkv, wanted, info, cosines, sines)
             )
             other = lax.ppermute(wanted, "z_low", [(0, 1), (1, 0)])
         partial = call(pass_sum_kernel, shape_of((far, 8, 256)), "sum_near", (partial,))

time: 173 us -> 172 us (level)
  other arithmetic: 2.6 us -> 0.33 us
    pallas_call x14 -> x15, Pallas kernels: 15.7 us -> 15.9 us  [call(): pl.pallas_call(kernel, out_shape=outs, in_specs=specs, out_specs=out_spec...]
  transfers between devices with their start and end apart: 4 -> 4, of which waited for: 3 -> 3; matrix products, arithmetic and copies ran while one was open for 2% -> 0% of each run, Pallas kernels for 1% -> 2%
where the time goes in v8:
time: 172 us; the launch traced here: 171 us
  blocking collectives  111 us (65%)
  starting transfers between devices  26 us (15%)
  Pallas kernels  15.9 us (9%)
  waiting for transfers between devices  15.6 us (9%)
  local copies, waits for them, and re-layouts  1.98 us (1%)
    all_to_all x9, blocking collectives, exchange(): return lax.all_to_all(value, axes, split_axis=0, concat_axis=0, tiled=True)  111 us
    all_to_all x3, starting transfers between devices, exchange(): return lax.all_to_all(value, axes, split_axis=0, concat_axis=0, tiled=True)  23.8 us
    pallas_call x15, Pallas kernels, call(): pl.pallas_call(kernel, out_shape=outs, in_specs=specs, out_specs=out_spec...  15.9 us
    all_to_all x3, waiting for transfers between devices, exchange(): return lax.all_to_all(value, axes, split_axis=0, concat_axis=0, tiled=True)  15.6 us
  transfers between devices with their start and end apart: 4, of which 3 were waited for; matrix products, arithmetic and copies ran while one was open for 0% of the time, Pallas kernels for 2%

profile of v8, /device:TPU:1, one launch (start us, length us, event | category | flops | bytes accessed | tf_op | source)
XLA Modules:
  0.0 170.9 jit_solution(4935033159393110736)
XLA Ops:
  0.0 0.7 copy-done.7
  0.7 3.6 %decode_qkv.1 = (bf16[2304,256]{1,0:T(8,128)(2,1)S(1)}, f32[8,256]{1,0:T(8,128)S(1)}, f32[8,8,256]{2,1,0:T(8,128)}) custom-call(s32[576,256]{1,0:T(8,128)} %bitcast.23, f32[18,128]{1,0:T(8,128)} %bitcast.24, f32[1,256]{1,0:T(1,128)} %bitcast.21, bf16[4,256]{1,0:T(4,128)(2,1)S(1)} %copy-done.7), custom_call_target="tpu_custom_call" | custom-call | tf_op jit(solution)/shard_map/decode_qkv/pallas_call | solution.py:38
  4.3 6.4 %all-to-all-start = ((f32[8,8,256]{2,1,0:T(8,128)}), f32[8,8,256]{2,1,0:T(8,128)S(1)}, u32[]{:S(2)}, u32[]{:S(2)}) async-start(f32[8,8,256]{2,1,0:T(8,128)} %get-tuple-element.24), calls=%async_computation | async-start | bytes 131072 | tf_op jit(solution)/shard_map/all_to_all | solution.py:370
  10.7 0.0 copy-start.8
  10.7 0.0 copy-start.3
  10.7 0.0 copy-start.5
  10.7 1.1 keep.1.w_ref
  11.8 0.0 copy-done.8
  11.8 0.2 copy-done.3
  12.1 0.1 multiply_sine_fusion
  12.2 0.1 fusion.4
  12.3 0.1 pad_add_fusion.info_ref
  12.4 0.0 copy-done.5
  12.4 3.5 %all-to-all-done.in_ref = f32[8,8,256]{2,1,0:T(8,128)S(1)} async-done(((f32[8,8,256]{2,1,0:T(8,128)}), f32[8,8,256]{2,1,0:T(8,128)S(1)}, u32[]{:S(2)}, u32[]{:S(2)}) %all-to-all-start) | async-done | bytes 65568 | tf_op jit(solution)/shard_map/all_to_all | solution.py:370
  15.9 0.6 sum_near.2
  16.5 14.0 %all-to-all-start.1 = ((f32[8,8,256]{2,1,0:T(8,128)}), f32[8,8,256]{2,1,0:T(8,128)S(1)}, u32[]{:S(2)}, u32[]{:S(2)}) async-start(f32[8,8,256]{2,1,0:T(8,128)} %sum_near.2), calls=%async_computation.1 | async-start | bytes 131072 | tf_op jit(solution)/shard_map/all_to_all | solution.py:370
  30.6 2.3 %collective-permute-start = (f32[264,256]{1,0:T(8,128)S(1)}, f32[264,256]{1,0:T(8,128)S(1)}, u32[]{:S(2)}, u32[]{:S(2)}) collective-permute-start(f32[264,256]{1,0:T(8,128)S(1)} %pad_maximum_fusion), channel_id=1, source_target_pairs={{0,32},{32,0},{1,33},{33,1},{2,34},{34,2},{3,35},{35,3},{4,36},{36... | collective-permute-start | bytes 811016 | tf_op jit(solution)/shard_map/ppermute | solution.py:435
  32.8 10.0 %all-to-all-done.1.in_ref = f32[8,8,256]{2,1,0:T(8,128)S(1)} async-done(((f32[8,8,256]{2,1,0:T(8,128)}), f32[8,8,256]{2,1,0:T(8,128)S(1)}, u32[]{:S(2)}, u32[]{:S(2)}) %all-to-all-start.1) | async-done | bytes 65568 | tf_op jit(solution)/shard_map/all_to_all | solution.py:370
  42.8 0.6 sum_far.2
  43.4 3.3 %all-to-all-start.2 = ((f32[8,8,256]{2,1,0:T(8,128)}), f32[8,8,256]{2,1,0:T(8,128)S(1)}, u32[]{:S(2)}, u32[]{:S(2)}) async-start(f32[8,8,256]{2,1,0:T(8,128)} %sum_far.2), calls=%async_computation.2 | async-start | bytes 131072 | tf_op jit(solution)/shard_map/all_to_all | solution.py:370
  46.8 0.0 collective-permute-done.other_ref
  46.8 0.0 copy-start.4
  46.8 1.0 copy-done.4
  47.8 1.9 %decode_out.1.w_ref = bf16[512,1024]{1,0:T(8,128)(2,1)S(1)} custom-call(s32[6]{0:T(128)S(1)} %pad_add_fusion.info_ref, s32[256,512]{1,0:T(8,128)S(1)} %copy-done.4, f32[1,256]{1,0:T(1,128)S(1)} %bitcast.20, f32[264,256]{1,0:T(8,128)S(1)} %collective-permute-done.other_ref), custom_call_target="tpu_custom_call" | custom-call | tf_op jit(solution)/shard_map/decode_out/pallas_call | solution.py:38
  49.7 2.2 %all-to-all-done.2.in_ref = f32[8,8,256]{2,1,0:T(8,128)S(1)} async-done(((f32[8,8,256]{2,1,0:T(8,128)}), f32[8,8,256]{2,1,0:T(8,128)S(1)}, u32[]{:S(2)}, u32[]{:S(2)}) %all-to-all-start.2) | async-done | bytes 65568 | tf_op jit(solution)/shard_map/all_to_all | solution.py:370
  51.9 0.0 copy-done.1
  51.9 0.0 copy-done.2
  51.9 1.9 %attend.2 = (f32[8,8,640]{2,1,0:T(8,128)S(1)}, f32[8,128]{1,0:T(8,128)S(1)}, f32[8,128]{1,0:T(8,128)S(1)}) custom-call(s32[6]{0:T(128)S(1)} %pad_add_fusion.info_ref, f32[8,8,256]{2,1,0:T(8,128)S(1)} %all-to-all-done.2.in_ref, f32[4,128]{1,0:T(4,128)S(1)} %get-tuple-element.30.cos_ref, f32[4,128]{1,0:T(4,128)S(1)} %get-tuple-element.31.sin_ref, ...), custom_call_target="tpu_custom_call" | custom-call | tf_op jit(solution)/shard_map/attend/pallas_call | solution.py:38
  53.8 0.0 copy-start
  53.8 0.0 copy-start.6
  53.8 8.4 %all_to_all.60.in_ref = f32[8,8,640]{2,1,0:T(8,128)S(1)} all-to-all(f32[8,8,640]{2,1,0:T(8,128)S(1)} %get-tuple-element.32), channel_id=1, replica_groups=mesh['z_high'=8,'z_low'=2,'y'=4,'head'=8] {'z_low','y'}, dimensions={0} | all-to-all | bytes 327680 | tf_op jit(solution)/shard_map/all_to_all | solution.py:370
  62.3 0.1 merge_near.2
  62.4 16.3 %all_to_all.61.in_ref = f32[8,8,640]{2,1,0:T(8,128)S(1)} all-to-all(f32[8,8,640]{2,1,0:T(8,128)S(1)} %merge_near.2), channel_id=1, replica_groups=mesh['z_high'=8,'z_low'=2,'y'=4,'head'=8] {'z_high'}, dimensions={0} | all-to-all | bytes 327680 | tf_op jit(solution)/shard_map/all_to_all | solution.py:370
  78.7 1.2 finish.2
  79.9 17.2 %all_to_all.62.in_ref = f32[16,8,128]{2,1,0:T(8,128)S(1)} all-to-all(f32[16,8,128]{2,1,0:T(8,128)S(1)} %finish.2), channel_id=1, replica_groups=mesh['z_high'=8,'z_low'=2,'y'=4,'head'=8] {'z_low','head'}, dimensions={0} | all-to-all | bytes 131072 | tf_op jit(solution)/shard_map/all_to_all | solution.py:370
  97.1 0.0 copy-done
  97.1 0.0 copy-done.6
  97.1 0.6 next_step.1
  97.6 7.7 %all_to_all.63.in_ref = f32[8,8,256]{2,1,0:T(8,128)S(1)} all-to-all(f32[8,8,256]{2,1,0:T(8,128)S(1)} %get-tuple-element.36), channel_id=1, replica_groups=mesh['z_high'=8,'z_low'=2,'y'=4,'head'=8] {'z_low','y'}, dimensions={0} | all-to-all | bytes 131072 | tf_op jit(solution)/shard_map/all_to_all | solution.py:370
  105.3 14.6 %all_to_all.64.in_ref = f32[8,8,256]{2,1,0:T(8,128)S(1)} all-to-all(f32[8,8,256]{2,1,0:T(8,128)S(1)} %sum_near.3), channel_id=1, replica_groups=mesh['z_high'=8,'z_low'=2,'y'=4,'head'=8] {'z_high'}, dimensions={0} | all-to-all | bytes 131072 | tf_op jit(solution)/shard_map/all_to_all | solution.py:370
  119.9 7.6 %all_to_all.65.in_ref = f32[8,8,256]{2,1,0:T(8,128)S(1)} all-to-all(f32[8,8,256]{2,1,0:T(8,128)S(1)} %sum_far.3), channel_id=1, replica_groups=mesh['z_high'=8,'z_low'=2,'y'=4,'head'=8] {'z_low','y'}, dimensions={0} | all-to-all | bytes 131072 | tf_op jit(solution)/shard_map/all_to_all | solution.py:370
  127.5 2.3 %attend.3 = (f32[8,8,640]{2,1,0:T(8,128)S(1)}, f32[8,128]{1,0:T(8,128)}, f32[8,128]{1,0:T(8,128)}) custom-call(s32[6]{0:T(128)S(1)} %pad_add_fusion.info_ref, f32[8,8,256]{2,1,0:T(8,128)S(1)} %all_to_all.65.in_ref, f32[4,128]{1,0:T(4,128)S(1)} %get-tuple-element.37.cos_ref, f32[4,128]{1,0:T(4,128)S(1)} %get-tuple-element.38.sin_ref, ...), custom_call_target="tpu_custom_call" | custom-call | tf_op jit(solution)/shard_map/attend/pallas_call | solution.py:38
  129.8 8.0 %all_to_all.66.in_ref = f32[8,8,640]{2,1,0:T(8,128)S(1)} all-to-all(f32[8,8,640]{2,1,0:T(8,128)S(1)} %get-tuple-element.41), channel_id=1, replica_groups=mesh['z_high'=8,'z_low'=2,'y'=4,'head'=8] {'z_low','y'}, dimensions={0} | all-to-all | bytes 327680 | tf_op jit(solution)/shard_map/all_to_all | solution.py:370
  137.8 0.1 merge_near.3
  138.0 16.1 %all_to_all.67.in_ref = f32[8,8,640]{2,1,0:T(8,128)S(1)} all-to-all(f32[8,8,640]{2,1,0:T(8,128)S(1)} %merge_near.3), channel_id=1, replica_groups=mesh['z_high'=8,'z_low'=2,'y'=4,'head'=8] {'z_high'}, dimensions={0} | all-to-all | bytes 327680 | tf_op jit(solution)/shard_map/all_to_all | solution.py:370
  154.1 1.2 finish.3
  155.3 15.0 %all_to_all.68.in_ref = f32[16,8,128]{2,1,0:T(8,128)S(1)} all-to-all(f32[16,8,128]{2,1,0:T(8,128)S(1)} %finish.3), channel_id=1, replica_groups=mesh['z_high'=8,'z_low'=2,'y'=4,'head'=8] {'z_low','head'}, dimensions={0} | all-to-all | bytes 131072 | tf_op jit(solution)/shard_map/all_to_all | solution.py:370
  170.3 0.6 last.1
  (11 shorter events, 0.1 us)
Async XLA Ops:
  0.0 0.7 copy-start.7
  4.3 11.6 %all-to-all-start = ((f32[8,8,256]{2,1,0:T(8,128)}), f32[8,8,256]{2,1,0:T(8,128)S(1)}, u32[]{:S(2)}, u32[]{:S(2)}) async-start(f32[8,8,256]{2,1,0:T(8,128)} %get-tuple-element.24), calls=%async_computation | async-start | bytes 131072 | tf_op jit(solution)/shard_map/all_to_all | solution.py:370
  10.7 1.1 copy-start.8
  10.7 1.4 copy-start.3
  10.7 1.6 copy-start.5
  15.9 36.0 %copy-start.1 = (bf16[4,1024,1,128]{3,1,2,0:T(8,128)(2,1)S(1)}, bf16[4,1024,1,128]{3,1,2,0:T(8,128)(2,1)}, u32[]{:S(2)}) copy-start(bf16[4,1024,1,128]{3,1,2,0:T(8,128)(2,1)} %param.15) | copy-start | bytes 3145732
  15.9 36.0 %copy-start.2 = (bf16[4,1024,1,128]{3,1,2,0:T(8,128)(2,1)S(1)}, bf16[4,1024,1,128]{3,1,2,0:T(8,128)(2,1)}, u32[]{:S(2)}) copy-start(bf16[4,1024,1,128]{3,1,2,0:T(8,128)(2,1)} %param.16) | copy-start | bytes 3145732
  16.5 26.3 %all-to-all-start.1 = ((f32[8,8,256]{2,1,0:T(8,128)}), f32[8,8,256]{2,1,0:T(8,128)S(1)}, u32[]{:S(2)}, u32[]{:S(2)}) async-start(f32[8,8,256]{2,1,0:T(8,128)} %sum_near.2), calls=%async_computation.1 | async-start | bytes 131072 | tf_op jit(solution)/shard_map/all_to_all | solution.py:370
  30.6 16.2 %collective-permute-start = (f32[264,256]{1,0:T(8,128)S(1)}, f32[264,256]{1,0:T(8,128)S(1)}, u32[]{:S(2)}, u32[]{:S(2)}) collective-permute-start(f32[264,256]{1,0:T(8,128)S(1)} %pad_maximum_fusion), channel_id=1, source_target_pairs={{0,32},{32,0},{1,33},{33,1},{2,34},{34,2},{3,35},{35,3},{4,36},{36... | collective-permute-start | bytes 811016 | tf_op jit(solution)/shard_map/ppermute | solution.py:435
  43.4 8.5 %all-to-all-start.2 = ((f32[8,8,256]{2,1,0:T(8,128)}), f32[8,8,256]{2,1,0:T(8,128)S(1)}, u32[]{:S(2)}, u32[]{:S(2)}) async-start(f32[8,8,256]{2,1,0:T(8,128)} %sum_far.2), calls=%async_computation.2 | async-start | bytes 131072 | tf_op jit(solution)/shard_map/all_to_all | solution.py:370
  46.8 1.0 copy-start.4
  53.8 43.3 %copy-start = (bf16[2304,256]{1,0:T(8,128)(2,1)S(1)}, bf16[2304,256]{1,0:T(8,128)(2,1)}, u32[]{:S(2)}) copy-start(bf16[2304,256]{1,0:T(8,128)(2,1)} %keep.1.w_ref) | copy-start | bytes 3538948
  53.8 43.2 %copy-start.6 = (f32[256]{0:T(256)S(1)}, f32[256]{0:T(256)}, u32[]{:S(2)}) copy-start(f32[256]{0:T(256)} %param.10) | copy-start | bytes 3076

commit v9 on v8

--- a/solution.py
+++ b/solution.py
@@ -53,7 +53,7 @@
 def byte_sum(state):
     x = state * 34038481 + 76625530
     pairs = (x & 0x00FF00FF) + ((x >> 8) & 0x00FF00FF)
-    total = (pairs + (pairs >> 16)) & 0x7FF
+    total = (pairs * 0x10001) >> 16
     return (total - 510).astype(f32)
 
 
@@ -115,10 +115,11 @@
         )
     scale_copy = pltpu.make_async_copy(scale_hbm, scale_ref, scale_sem)
     gain_copy = pltpu.make_async_copy(gain_hbm, gain_ref, gain_sem)
+    copies[0].start()
     scale_copy.start()
+    for copy in copies[1:]:
+        copy.start()
     gain_copy.start()
-    for copy in copies:
-        copy.start()
     scale_copy.wait()
     lane = iota((32, 128), 1)
     word = iota((32, 128), 0)
@@ -218,9 +219,9 @@
         out_ref[j, :, 512:] = stats
 
 
-def attend_kernel(features, earlier, info_ref, in_ref, cos_ref, sin_ref, keys_ref, values_ref,
+def attend_kernel(features, earlier, last_step, info_ref, in_ref, cos_ref, sin_ref, keys_ref, values_ref,
                   *refs):
-    out_ref, k_ref, v_ref, q_ref = refs[2 * earlier :]
+    out_ref, *kept_refs, q_ref = refs[2 * earlier :]
     first = iota((8, 128), 0) < 4
     lane = iota((8, 128), 1)
     rms = lax.rsqrt(in_ref[0, :, 144:145] / features + EPSILON)
@@ -241,8 +242,9 @@
     q_ref[...] = turned[:64]
     new_key = turned[64:]
     new_value = x[72:].astype(bf16).astype(f32)
-    k_ref[...] = new_key
-    v_ref[...] = new_value
+    if not last_step:
+        kept_refs[0][...] = new_key
+        kept_refs[1][...] = new_value
     new_keys = [refs[2 * u][...] for u in range(earlier)] + [new_key]
     new_values = [refs[2 * u + 1][...] for u in range(earlier)] + [new_value]
     owner = info_ref[4] == 0
@@ -446,15 +448,17 @@
                 (info,),
             )
             partial, w_out = lax.optimization_barrier((partial, w_out))
-        part, new_key, new_value = call(
-            functools.partial(attend_kernel, features, step),
-            (shape_of((near, 8, 640)), shape_of((8, 128)), shape_of((8, 128))),
+        last_step = step + 1 == DECODE_STEPS
+        kept = () if last_step else (shape_of((8, 128)), shape_of((8, 128)))
+        part, *new = call(
+            functools.partial(attend_kernel, features, step, last_step),
+            (shape_of((near, 8, 640)), *kept),
             "attend",
             (partial, cosines[step], sines[step], keys, values, *fresh),
             (info,),
             scratch=(pltpu.VMEM((64, 128), f32),),
         )
-        fresh += (new_key, new_value)
+        fresh += tuple(new)
         part = exchange(part, NEAR)
         part = call(pass_merge_kernel, shape_of((far, 8, 640)), "merge_near", (part,))
         part = exchange(part, FAR)
@@ -467,7 +471,7 @@
             scratch=(pltpu.VMEM((64, 128), f32),),
         )
         update = exchange(update, ("z_low", "head"))
-        if step + 1 < DECODE_STEPS:
+        if not last_step:
             hidden, partial = call(
                 next_kernel,
                 (shape_of((8, 256)), shape_of((near, 8, 256))),

time: 172 us -> 171 us (level)
  no operation moved by 1% of the time
where the time goes in v9:
time: 171 us; the launch traced here: 170 us
  blocking collectives  111 us (65%)
  starting transfers between devices  26 us (15%)
  waiting for transfers between devices  15.7 us (9%)
  Pallas kernels  15.4 us (9%)
  local copies, waits for them, and re-layouts  1.97 us (1%)
    all_to_all x9, blocking collectives, exchange(): return lax.all_to_all(value, axes, split_axis=0, concat_axis=0, tiled=True)  111 us
    all_to_all x3, starting transfers between devices, exchange(): return lax.all_to_all(value, axes, split_axis=0, concat_axis=0, tiled=True)  23.8 us
    all_to_all x3, waiting for transfers between devices, exchange(): return lax.all_to_all(value, axes, split_axis=0, concat_axis=0, tiled=True)  15.7 us
    pallas_call x15, Pallas kernels, call(): pl.pallas_call(kernel, out_shape=outs, in_specs=specs, out_specs=out_spec...  15.4 us
  transfers between devices with their start and end apart: 4, of which 3 were waited for; matrix products, arithmetic and copies ran while one was open for 0% of the time, Pallas kernels for 2%

profile of v9, /device:TPU:1, one launch (start us, length us, event | category | flops | bytes accessed | tf_op | source)
XLA Modules:
  0.0 170.5 jit_solution(13103854221936998861)
XLA Ops:
  0.0 0.7 copy-done.7
  0.7 3.5 %decode_qkv.1 = (bf16[2304,256]{1,0:T(8,128)(2,1)S(1)}, f32[8,256]{1,0:T(8,128)S(1)}, f32[8,8,256]{2,1,0:T(8,128)}) custom-call(s32[576,256]{1,0:T(8,128)} %bitcast.23, f32[18,128]{1,0:T(8,128)} %bitcast.24, f32[1,256]{1,0:T(1,128)} %bitcast.21, bf16[4,256]{1,0:T(4,128)(2,1)S(1)} %copy-done.7), custom_call_target="tpu_custom_call" | custom-call | tf_op jit(solution)/shard_map/decode_qkv/pallas_call | solution.py:38
  4.2 6.4 %all-to-all-start = ((f32[8,8,256]{2,1,0:T(8,128)}), f32[8,8,256]{2,1,0:T(8,128)S(1)}, u32[]{:S(2)}, u32[]{:S(2)}) async-start(f32[8,8,256]{2,1,0:T(8,128)} %get-tuple-element.23), calls=%async_computation | async-start | bytes 131072 | tf_op jit(solution)/shard_map/all_to_all | solution.py:372
  10.6 0.0 copy-start.8
  10.6 0.0 copy-start.3
  10.6 0.0 copy-start.5
  10.7 1.1 keep.1.w_ref
  11.7 0.0 copy-done.8
  11.8 0.2 copy-done.3
  12.0 0.1 multiply_sine_fusion
  12.1 0.1 fusion.4
  12.2 0.1 pad_add_fusion.info_ref
  12.3 0.0 copy-done.5
  12.3 3.5 %all-to-all-done.in_ref = f32[8,8,256]{2,1,0:T(8,128)S(1)} async-done(((f32[8,8,256]{2,1,0:T(8,128)}), f32[8,8,256]{2,1,0:T(8,128)S(1)}, u32[]{:S(2)}, u32[]{:S(2)}) %all-to-all-start) | async-done | bytes 65568 | tf_op jit(solution)/shard_map/all_to_all | solution.py:372
  15.8 0.6 sum_near.2
  16.4 14.0 %all-to-all-start.1 = ((f32[8,8,256]{2,1,0:T(8,128)}), f32[8,8,256]{2,1,0:T(8,128)S(1)}, u32[]{:S(2)}, u32[]{:S(2)}) async-start(f32[8,8,256]{2,1,0:T(8,128)} %sum_near.2), calls=%async_computation.1 | async-start | bytes 131072 | tf_op jit(solution)/shard_map/all_to_all | solution.py:372
  30.5 2.3 %collective-permute-start = (f32[264,256]{1,0:T(8,128)S(1)}, f32[264,256]{1,0:T(8,128)S(1)}, u32[]{:S(2)}, u32[]{:S(2)}) collective-permute-start(f32[264,256]{1,0:T(8,128)S(1)} %pad_maximum_fusion), channel_id=1, source_target_pairs={{0,32},{32,0},{1,33},{33,1},{2,34},{34,2},{3,35},{35,3},{4,36},{36... | collective-permute-start | bytes 811016 | tf_op jit(solution)/shard_map/ppermute | solution.py:437
  32.8 10.0 %all-to-all-done.1.in_ref = f32[8,8,256]{2,1,0:T(8,128)S(1)} async-done(((f32[8,8,256]{2,1,0:T(8,128)}), f32[8,8,256]{2,1,0:T(8,128)S(1)}, u32[]{:S(2)}, u32[]{:S(2)}) %all-to-all-start.1) | async-done | bytes 65568 | tf_op jit(solution)/shard_map/all_to_all | solution.py:372
  42.7 0.6 sum_far.2
  43.4 3.3 %all-to-all-start.2 = ((f32[8,8,256]{2,1,0:T(8,128)}), f32[8,8,256]{2,1,0:T(8,128)S(1)}, u32[]{:S(2)}, u32[]{:S(2)}) async-start(f32[8,8,256]{2,1,0:T(8,128)} %sum_far.2), calls=%async_computation.2 | async-start | bytes 131072 | tf_op jit(solution)/shard_map/all_to_all | solution.py:372
  46.7 0.0 collective-permute-done.other_ref
  46.7 0.0 copy-start.4
  46.7 1.0 copy-done.4
  47.8 1.8 %decode_out.1.w_ref = bf16[512,1024]{1,0:T(8,128)(2,1)S(1)} custom-call(s32[6]{0:T(128)S(1)} %pad_add_fusion.info_ref, s32[256,512]{1,0:T(8,128)S(1)} %copy-done.4, f32[1,256]{1,0:T(1,128)S(1)} %bitcast.20, f32[264,256]{1,0:T(8,128)S(1)} %collective-permute-done.other_ref), custom_call_target="tpu_custom_call" | custom-call | tf_op jit(solution)/shard_map/decode_out/pallas_call | solution.py:38
  49.6 2.2 %all-to-all-done.2.in_ref = f32[8,8,256]{2,1,0:T(8,128)S(1)} async-done(((f32[8,8,256]{2,1,0:T(8,128)}), f32[8,8,256]{2,1,0:T(8,128)S(1)}, u32[]{:S(2)}, u32[]{:S(2)}) %all-to-all-start.2) | async-done | bytes 65568 | tf_op jit(solution)/shard_map/all_to_all | solution.py:372
  51.9 0.0 copy-done.1
  51.9 0.0 copy-done.2
  51.9 1.9 %attend.2 = (f32[8,8,640]{2,1,0:T(8,128)S(1)}, f32[8,128]{1,0:T(8,128)S(1)}, f32[8,128]{1,0:T(8,128)S(1)}) custom-call(s32[6]{0:T(128)S(1)} %pad_add_fusion.info_ref, f32[8,8,256]{2,1,0:T(8,128)S(1)} %all-to-all-done.2.in_ref, f32[4,128]{1,0:T(4,128)S(1)} %get-tuple-element.29.cos_ref, f32[4,128]{1,0:T(4,128)S(1)} %get-tuple-element.30.sin_ref, ...), custom_call_target="tpu_custom_call" | custom-call | tf_op jit(solution)/shard_map/attend/pallas_call | solution.py:38
  53.8 0.0 copy-start
  53.8 0.0 copy-start.6
  53.8 8.4 %all_to_all.60.in_ref = f32[8,8,640]{2,1,0:T(8,128)S(1)} all-to-all(f32[8,8,640]{2,1,0:T(8,128)S(1)} %get-tuple-element.31), channel_id=1, replica_groups=mesh['z_high'=8,'z_low'=2,'y'=4,'head'=8] {'z_low','y'}, dimensions={0} | all-to-all | bytes 327680 | tf_op jit(solution)/shard_map/all_to_all | solution.py:372
  62.2 0.1 merge_near.2
  62.3 16.3 %all_to_all.61.in_ref = f32[8,8,640]{2,1,0:T(8,128)S(1)} all-to-all(f32[8,8,640]{2,1,0:T(8,128)S(1)} %merge_near.2), channel_id=1, replica_groups=mesh['z_high'=8,'z_low'=2,'y'=4,'head'=8] {'z_high'}, dimensions={0} | all-to-all | bytes 327680 | tf_op jit(solution)/shard_map/all_to_all | solution.py:372
  78.6 1.2 finish.2
  79.8 17.2 %all_to_all.62.in_ref = f32[16,8,128]{2,1,0:T(8,128)S(1)} all-to-all(f32[16,8,128]{2,1,0:T(8,128)S(1)} %finish.2), channel_id=1, replica_groups=mesh['z_high'=8,'z_low'=2,'y'=4,'head'=8] {'z_low','head'}, dimensions={0} | all-to-all | bytes 131072 | tf_op jit(solution)/shard_map/all_to_all | solution.py:372
  97.0 0.0 copy-done
  97.0 0.0 copy-done.6
  97.0 0.6 next_step.1
  97.6 7.7 %all_to_all.63.in_ref = f32[8,8,256]{2,1,0:T(8,128)S(1)} all-to-all(f32[8,8,256]{2,1,0:T(8,128)S(1)} %get-tuple-element.35), channel_id=1, replica_groups=mesh['z_high'=8,'z_low'=2,'y'=4,'head'=8] {'z_low','y'}, dimensions={0} | all-to-all | bytes 131072 | tf_op jit(solution)/shard_map/all_to_all | solution.py:372
  105.3 14.6 %all_to_all.64.in_ref = f32[8,8,256]{2,1,0:T(8,128)S(1)} all-to-all(f32[8,8,256]{2,1,0:T(8,128)S(1)} %sum_near.3), channel_id=1, replica_groups=mesh['z_high'=8,'z_low'=2,'y'=4,'head'=8] {'z_high'}, dimensions={0} | all-to-all | bytes 131072 | tf_op jit(solution)/shard_map/all_to_all | solution.py:372
  119.9 7.6 %all_to_all.65.in_ref = f32[8,8,256]{2,1,0:T(8,128)S(1)} all-to-all(f32[8,8,256]{2,1,0:T(8,128)S(1)} %sum_far.3), channel_id=1, replica_groups=mesh['z_high'=8,'z_low'=2,'y'=4,'head'=8] {'z_low','y'}, dimensions={0} | all-to-all | bytes 131072 | tf_op jit(solution)/shard_map/all_to_all | solution.py:372
  127.4 2.0 %attend.3 = f32[8,8,640]{2,1,0:T(8,128)S(1)} custom-call(s32[6]{0:T(128)S(1)} %pad_add_fusion.info_ref, f32[8,8,256]{2,1,0:T(8,128)S(1)} %all_to_all.65.in_ref, f32[4,128]{1,0:T(4,128)S(1)} %get-tuple-element.36.cos_ref, f32[4,128]{1,0:T(4,128)S(1)} %get-tuple-element.37.sin_ref, bf16[4,1024,128]{2,1,0:T(8,128)(2,1)S(1)} %bitcast.17, ...), custom_call_target="tpu_custom_call" | custom-call | tf_op jit(solution)/shard_map/attend/pallas_call | solution.py:38
  129.4 8.0 %all_to_all.66.in_ref = f32[8,8,640]{2,1,0:T(8,128)S(1)} all-to-all(f32[8,8,640]{2,1,0:T(8,128)S(1)} %attend.3), channel_id=1, replica_groups=mesh['z_high'=8,'z_low'=2,'y'=4,'head'=8] {'z_low','y'}, dimensions={0} | all-to-all | bytes 327680 | tf_op jit(solution)/shard_map/all_to_all | solution.py:372
  137.4 0.1 merge_near.3
  137.5 16.1 %all_to_all.67.in_ref = f32[8,8,640]{2,1,0:T(8,128)S(1)} all-to-all(f32[8,8,640]{2,1,0:T(8,128)S(1)} %merge_near.3), channel_id=1, replica_groups=mesh['z_high'=8,'z_low'=2,'y'=4,'head'=8] {'z_high'}, dimensions={0} | all-to-all | bytes 327680 | tf_op jit(solution)/shard_map/all_to_all | solution.py:372
  153.7 1.2 finish.3
  154.9 15.0 %all_to_all.68.in_ref = f32[16,8,128]{2,1,0:T(8,128)S(1)} all-to-all(f32[16,8,128]{2,1,0:T(8,128)S(1)} %finish.3), channel_id=1, replica_groups=mesh['z_high'=8,'z_low'=2,'y'=4,'head'=8] {'z_low','head'}, dimensions={0} | all-to-all | bytes 131072 | tf_op jit(solution)/shard_map/all_to_all | solution.py:372
  169.9 0.6 last.1
  (11 shorter events, 0.1 us)
Async XLA Ops:
  0.0 0.7 copy-start.7
  4.2 11.6 %all-to-all-start = ((f32[8,8,256]{2,1,0:T(8,128)}), f32[8,8,256]{2,1,0:T(8,128)S(1)}, u32[]{:S(2)}, u32[]{:S(2)}) async-start(f32[8,8,256]{2,1,0:T(8,128)} %get-tuple-element.23), calls=%async_computation | async-start | bytes 131072 | tf_op jit(solution)/shard_map/all_to_all | solution.py:372
  10.6 1.1 copy-start.8
  10.6 1.4 copy-start.3
  10.6 1.6 copy-start.5
  15.8 36.0 %copy-start.1 = (bf16[4,1024,1,128]{3,1,2,0:T(8,128)(2,1)S(1)}, bf16[4,1024,1,128]{3,1,2,0:T(8,128)(2,1)}, u32[]{:S(2)}) copy-start(bf16[4,1024,1,128]{3,1,2,0:T(8,128)(2,1)} %param.15) | copy-start | bytes 3145732
  15.8 36.0 %copy-start.2 = (bf16[4,1024,1,128]{3,1,2,0:T(8,128)(2,1)S(1)}, bf16[4,1024,1,128]{3,1,2,0:T(8,128)(2,1)}, u32[]{:S(2)}) copy-start(bf16[4,1024,1,128]{3,1,2,0:T(8,128)(2,1)} %param.16) | copy-start | bytes 3145732
  16.4 26.3 %all-to-all-start.1 = ((f32[8,8,256]{2,1,0:T(8,128)}), f32[8,8,256]{2,1,0:T(8,128)S(1)}, u32[]{:S(2)}, u32[]{:S(2)}) async-start(f32[8,8,256]{2,1,0:T(8,128)} %sum_near.2), calls=%async_computation.1 | async-start | bytes 131072 | tf_op jit(solution)/shard_map/all_to_all | solution.py:372
  30.5 16.2 %collective-permute-start = (f32[264,256]{1,0:T(8,128)S(1)}, f32[264,256]{1,0:T(8,128)S(1)}, u32[]{:S(2)}, u32[]{:S(2)}) collective-permute-start(f32[264,256]{1,0:T(8,128)S(1)} %pad_maximum_fusion), channel_id=1, source_target_pairs={{0,32},{32,0},{1,33},{33,1},{2,34},{34,2},{3,35},{35,3},{4,36},{36... | collective-permute-start | bytes 811016 | tf_op jit(solution)/shard_map/ppermute | solution.py:437
  43.4 8.5 %all-to-all-start.2 = ((f32[8,8,256]{2,1,0:T(8,128)}), f32[8,8,256]{2,1,0:T(8,128)S(1)}, u32[]{:S(2)}, u32[]{:S(2)}) async-start(f32[8,8,256]{2,1,0:T(8,128)} %sum_far.2), calls=%async_computation.2 | async-start | bytes 131072 | tf_op jit(solution)/shard_map/all_to_all | solution.py:372
  46.7 1.0 copy-start.4
  53.8 43.2 %copy-start = (bf16[2304,256]{1,0:T(8,128)(2,1)S(1)}, bf16[2304,256]{1,0:T(8,128)(2,1)}, u32[]{:S(2)}) copy-start(bf16[2304,256]{1,0:T(8,128)(2,1)} %keep.1.w_ref) | copy-start | bytes 3538948
  53.8 43.2 %copy-start.6 = (f32[256]{0:T(256)S(1)}, f32[256]{0:T(256)}, u32[]{:S(2)}) copy-start(f32[256]{0:T(256)} %param.10) | copy-start | bytes 3076
